TPU v7x, 32 devices: a whole 2x2x4 slice. The times are simulated.
32 devices in a mesh: tab: 8 (over z, y), row: 4 (over x, core).
Axes of the slice: x: 2, y: 2, z: 4, core: 2. Of those that a mesh axis runs over, the one named last changes fastest.
Arguments:
- table_cells: bfloat16 [8, 1024, 12, 512], P('tab', 'row'), may hold values from -6 to 6
- cotangent: bfloat16 [8, 1024, 12, 512], P('tab', 'row'), may hold values from -6 to 6
- row_counts: int32 [8], P('tab'), may hold values from 769 to 1024, as said below
- context_counts: int32 [8], P('tab'), may hold values from 128 to 1024, as said below
- feat_gain: float32 [512], replicated, may hold values from 0.5 to 1.5
- feat_shift: float32 [512], replicated, may hold values from -1.5 to 1.5
- feat_query: bfloat16 [512, 512], replicated, may hold values from -0.25 to 0.25
- feat_key: bfloat16 [512, 512], replicated, may hold values from -0.25 to 0.25
- feat_value: bfloat16 [512, 512], replicated, may hold values from -0.25 to 0.25
- feat_out: bfloat16 [512, 512], replicated, may hold values from -0.375 to 0.375
- feat_bias: float32 [512], replicated, may hold values from -1.5 to 1.5
- row_gain: float32 [512], replicated, may hold values from 0.5 to 1.5
- row_shift: float32 [512], replicated, may hold values from -1.5 to 1.5
- row_query: bfloat16 [512, 512], replicated, may hold values from -0.25 to 0.25
- row_key: bfloat16 [512, 512], replicated, may hold values from -0.25 to 0.25
- row_value: bfloat16 [512, 512], replicated, may hold values from -0.25 to 0.25
- row_out: bfloat16 [512, 512], replicated, may hold values from -4 to 4
- row_bias: float32 [512], replicated, may hold values from -1.5 to 1.5
- mlp_gain: float32 [512], replicated, may hold values from 0.5 to 1.5
- mlp_shift: float32 [512], replicated, may hold values from -1.5 to 1.5
- up_weight: bfloat16 [512, 2048], replicated, may hold values from -0.25 to 0.25
- up_bias: float32 [2048], replicated, may hold values from -1.5 to 1.5
- down_weight: bfloat16 [2048, 512], replicated, may hold values from -0.125 to 0.125
- down_bias: float32 [512], replicated, may hold values from -1.5 to 1.5
Outputs:
- layer_out: bfloat16 [8, 1024, 12, 512], P('tab', 'row')
- cells_grad: bfloat16 [8, 1024, 12, 512], P('tab', 'row')
- feat_gain_grad: float32 [512], P('row')
- feat_shift_grad: float32 [512], P('row')
- feat_query_grad: float32 [512, 512], P('row')
- feat_key_grad: float32 [512, 512], P('row')
- feat_value_grad: float32 [512, 512], P('row')
- feat_out_grad: float32 [512, 512], P('row')
- feat_bias_grad: float32 [512], P('row')
- row_gain_grad: float32 [512], P('row')
- row_shift_grad: float32 [512], P('row')
- row_query_grad: float32 [512, 512], P('row')
- row_key_grad: float32 [512, 512], P('row')
- row_value_grad: float32 [512, 512], P('row')
- row_out_grad: float32 [512, 512], P('row')
- row_bias_grad: float32 [512], P('row')
- mlp_gain_grad: float32 [512], P('row')
- mlp_shift_grad: float32 [512], P('row')
- up_weight_grad: float32 [512, 2048], P('row')
- up_bias_grad: float32 [2048], P('row')
- down_weight_grad: float32 [2048, 512], P('row')
- down_bias_grad: float32 [512], P('row')
Inputs may be any that keep to these rules, and one draw needn't show every extreme that they name: Rows 0 to row_counts[t] - 1 of table t hold data, the rest is padding; some table fills all 1024 rows. Rows 0 to context_counts[t] - 1 of table t are its context; context_counts[t] <= row_counts[t]; some table's context is all 1024 rows.
All inputs are finite; a program needn't handle non-finite values.
Results may differ from a plain program's by a relative error of at most 0.024.
Values may be sent and summed in bfloat16 or wider, within the bound.
No kernel may reach another device: no remote copies, remote signals or barrier semaphores. Data moves between devices by JAX's collectives and lax.ppermute only.
A program may use at most 512 MiB of HBM per device.

v0:
```python
import math

import jax
import jax.numpy as jnp
from jax import lax
from jax.sharding import PartitionSpec as P

HEADS = 4


EPSILON = 1e-05
NEGATIVE = -1e30


def normalize(values, gain_vec, shift_vec):
    row_mean = jnp.mean(values, -1, keepdims=True)
    centred = values - row_mean
    inverse = lax.rsqrt(jnp.mean(centred * centred, -1, keepdims=True) + EPSILON)
    unit_part = centred * inverse
    return (unit_part * gain_vec + shift_vec, unit_part, inverse)


def normalize_back(upstream, unit_part, inverse, gain_vec):
    scaled = upstream * gain_vec
    inner_part = (
        scaled
        - jnp.mean(scaled, -1, keepdims=True)
        - unit_part * jnp.mean(scaled * unit_part, -1, keepdims=True)
    )
    return (
        inverse * inner_part,
        jnp.sum(upstream * unit_part, axis=(0, 1)),
        jnp.sum(upstream, axis=(0, 1)),
    )


def project(left_side, weight):
    return jnp.einsum("rfd,de->rfe", left_side, weight, preferred_element_type=jnp.float32)


def project_back(upstream, weight):
    return jnp.einsum("rfe,de->rfd", upstream, weight, preferred_element_type=jnp.float32)


def outer_sum(left_side, upstream):
    return jnp.einsum("rfd,rfe->de", left_side, upstream, preferred_element_type=jnp.float32)


def split_heads(values):
    return values.reshape(values.shape[0], values.shape[1], HEADS, values.shape[2] // HEADS)


def join_heads(values):
    return values.reshape(values.shape[0], values.shape[1], values.shape[2] * values.shape[3])


def shards(
    table_cells,
    cotangent,
    row_counts,
    context_counts,
    feat_gain,
    feat_shift,
    feat_query,
    feat_key,
    feat_value,
    feat_out,
    feat_bias,
    row_gain,
    row_shift,
    row_query,
    row_key,
    row_value,
    row_out,
    row_bias,
    mlp_gain,
    mlp_shift,
    up_weight,
    up_bias,
    down_weight,
    down_bias,
):
    source = table_cells[0].astype(jnp.float32)
    local_rows, feat_count, model_width = source.shape
    score_scale = 1.0 / math.sqrt(model_width // HEADS)
    total_rows = local_rows * lax.axis_size("row")
    row_ids = lax.axis_index("row") * local_rows + jnp.arange(local_rows, dtype=jnp.int32)
    row_mask = (row_ids < row_counts[0]).astype(jnp.float32)[:, None, None]
    context_mask = jnp.arange(total_rows, dtype=jnp.int32) < context_counts[0]
    normed_a, unit_a, inverse_a = normalize(source, feat_gain, feat_shift)
    normed_a = normed_a.astype(jnp.bfloat16)
    query_a = split_heads(project(normed_a, feat_query).astype(jnp.bfloat16))
    key_a = split_heads(project(normed_a, feat_key).astype(jnp.bfloat16))
    value_a = split_heads(project(normed_a, feat_value).astype(jnp.bfloat16))
    scores_a = (
        jnp.einsum("rfhd,rghd->rhfg", query_a, key_a, preferred_element_type=jnp.float32)
        * score_scale
    )
    probs_a = jax.nn.softmax(scores_a, -1)
    probs_a_low = probs_a.astype(jnp.bfloat16)
    mixed_a = join_heads(
        jnp.einsum(
            "rhfg,rghd->rfhd", probs_a_low, value_a, preferred_element_type=jnp.float32
        ).astype(jnp.bfloat16)
    )
    after_a = source + project(mixed_a, feat_out) + feat_bias
    normed_b, unit_b, inverse_b = normalize(after_a, row_gain, row_shift)
    normed_b = normed_b.astype(jnp.bfloat16)
    query_b = split_heads(project(normed_b, row_query).astype(jnp.bfloat16))
    key_b = project(normed_b, row_key).astype(jnp.bfloat16)
    value_b = project(normed_b, row_value).astype(jnp.bfloat16)
    key_all, value_all = (
        lax.all_gather(key_b, "row", axis=0, tiled=True),
        lax.all_gather(value_b, "row", axis=0, tiled=True),
    )

    def row_scores(key_whole):
        raw_scores = (
            jnp.einsum(
                "ifhd,jfhd->fhij",
                query_b,
                split_heads(key_whole),
                preferred_element_type=jnp.float32,
            )
            * score_scale
        )
        return jnp.where(context_mask, raw_scores, NEGATIVE)

    scores_b = row_scores(key_all)
    highest = jnp.max(scores_b, -1, keepdims=True)
    log_total = highest + jnp.log(jnp.sum(jnp.exp(scores_b - highest), -1, keepdims=True))
    probs_b_low = jnp.exp(scores_b - log_total).astype(jnp.bfloat16)
    mixed_b = join_heads(
        jnp.einsum(
            "fhij,jfhd->ifhd",
            probs_b_low,
            split_heads(value_all),
            preferred_element_type=jnp.float32,
        ).astype(jnp.bfloat16)
    )
    after_b = after_a + project(mixed_b, row_out) + row_bias
    normed_c, unit_c, inverse_c = normalize(after_b, mlp_gain, mlp_shift)
    normed_c = normed_c.astype(jnp.bfloat16)
    hidden = project(normed_c, up_weight) + up_bias
    active, gelu_pull = jax.vjp(jax.nn.gelu, hidden)
    active = active.astype(jnp.bfloat16)
    after_c = after_b + project(active, down_weight) + down_bias
    layer_out = (after_c * row_mask).astype(jnp.bfloat16)
    grad_c = cotangent[0].astype(jnp.float32) * row_mask
    grad_c_low = grad_c.astype(jnp.bfloat16)
    down_bias_grad = jnp.sum(grad_c, axis=(0, 1))
    down_weight_grad = outer_sum(active, grad_c_low)
    active_grad = project_back(grad_c_low, down_weight)
    hidden_grad = gelu_pull(active_grad)[0].astype(jnp.bfloat16)
    up_bias_grad = jnp.sum(hidden_grad.astype(jnp.float32), axis=(0, 1))
    up_weight_grad = outer_sum(normed_c, hidden_grad)
    back_c, mlp_gain_grad, mlp_shift_grad = normalize_back(
        project_back(hidden_grad, up_weight), unit_c, inverse_c, mlp_gain
    )
    grad_b = grad_c + back_c
    grad_b_low = grad_b.astype(jnp.bfloat16)
    row_bias_grad = jnp.sum(grad_b, axis=(0, 1))
    row_out_grad = outer_sum(mixed_b, grad_b_low)
    mixed_b_grad = split_heads(project_back(grad_b_low, row_out).astype(jnp.bfloat16))
    key_back, value_back = (
        lax.all_gather(key_b, "row", axis=0, tiled=True),
        lax.all_gather(value_b, "row", axis=0, tiled=True),
    )
    probs_full = jnp.exp(row_scores(key_back) - log_total)
    probs_grad = jnp.einsum(
        "ifhd,jfhd->fhij", mixed_b_grad, split_heads(value_back), preferred_element_type=jnp.float32
    )
    row_dot = jnp.sum(probs_full * probs_grad, -1, keepdims=True)
    score_b_grad = (probs_full * (probs_grad - row_dot)).astype(jnp.bfloat16)
    query_b_grad = join_heads(
        (
            jnp.einsum(
                "fhij,jfhd->ifhd",
                score_b_grad,
                split_heads(key_back),
                preferred_element_type=jnp.float32,
            )
            * score_scale
        ).astype(jnp.bfloat16)
    )
    flat_rows = feat_count * HEADS
    log_all, dot_all = (
        lax.all_gather(log_total.reshape(flat_rows, local_rows), "row", axis=1, tiled=True),
        lax.all_gather(row_dot.reshape(flat_rows, local_rows), "row", axis=1, tiled=True),
    )
    own_mask = row_ids < context_counts[0]
    key_own = split_heads(key_b)
    value_own = split_heads(value_b)
    query_piece = lax.all_gather(query_b, "row", axis=0, tiled=True)
    grad_piece = lax.all_gather(mixed_b_grad, "row", axis=0, tiled=True)
    count = query_piece.shape[0]
    log_piece = log_all.reshape(feat_count, HEADS, count, 1)
    dot_piece = dot_all.reshape(feat_count, HEADS, count, 1)
    piece_scores = (
        jnp.einsum("ifhd,jfhd->fhij", query_piece, key_own, preferred_element_type=jnp.float32)
        * score_scale
    )
    piece_scores = jnp.where(own_mask, piece_scores, NEGATIVE)
    piece_probs = jnp.exp(piece_scores - log_piece)
    piece_inner = jnp.einsum(
        "ifhd,jfhd->fhij", grad_piece, value_own, preferred_element_type=jnp.float32
    )
    piece_grad = (piece_probs * (piece_inner - dot_piece)).astype(jnp.bfloat16)
    key_total = (
        jnp.einsum("fhij,ifhd->jfhd", piece_grad, query_piece, preferred_element_type=jnp.float32)
        * score_scale
    )
    value_total = jnp.einsum(
        "fhij,ifhd->jfhd",
        piece_probs.astype(jnp.bfloat16),
        grad_piece,
        preferred_element_type=jnp.float32,
    )
    key_total, value_total = (key_total, value_total)
    key_b_grad = join_heads(key_total).astype(jnp.bfloat16)
    value_b_grad = join_heads(value_total).astype(jnp.bfloat16)
    row_query_grad = outer_sum(normed_b, query_b_grad)
    row_key_grad = outer_sum(normed_b, key_b_grad)
    row_value_grad = outer_sum(normed_b, value_b_grad)
    normed_b_grad = (
        project_back(query_b_grad, row_query)
        + project_back(key_b_grad, row_key)
        + project_back(value_b_grad, row_value)
    )
    back_b, row_gain_grad, row_shift_grad = normalize_back(
        normed_b_grad, unit_b, inverse_b, row_gain
    )
    grad_a = grad_b + back_b
    grad_a_low = grad_a.astype(jnp.bfloat16)
    feat_bias_grad = jnp.sum(grad_a, axis=(0, 1))
    feat_out_grad = outer_sum(mixed_a, grad_a_low)
    mixed_a_grad = split_heads(project_back(grad_a_low, feat_out).astype(jnp.bfloat16))
    probs_a_grad = jnp.einsum(
        "rfhd,rghd->rhfg", mixed_a_grad, value_a, preferred_element_type=jnp.float32
    )
    score_a_grad = (
        probs_a * (probs_a_grad - jnp.sum(probs_a * probs_a_grad, -1, keepdims=True))
    ).astype(jnp.bfloat16)
    query_a_grad = join_heads(
        (
            jnp.einsum("rhfg,rghd->rfhd", score_a_grad, key_a, preferred_element_type=jnp.float32)
            * score_scale
        ).astype(jnp.bfloat16)
    )
    key_a_grad = join_heads(
        (
            jnp.einsum("rhfg,rfhd->rghd", score_a_grad, query_a, preferred_element_type=jnp.float32)
            * score_scale
        ).astype(jnp.bfloat16)
    )
    value_a_grad = join_heads(
        jnp.einsum(
            "rhfg,rfhd->rghd", probs_a_low, mixed_a_grad, preferred_element_type=jnp.float32
        ).astype(jnp.bfloat16)
    )
    feat_query_grad = outer_sum(normed_a, query_a_grad)
    feat_key_grad = outer_sum(normed_a, key_a_grad)
    feat_value_grad = outer_sum(normed_a, value_a_grad)
    normed_a_grad = (
        project_back(query_a_grad, feat_query)
        + project_back(key_a_grad, feat_key)
        + project_back(value_a_grad, feat_value)
    )
    back_a, feat_gain_grad, feat_shift_grad = normalize_back(
        normed_a_grad, unit_a, inverse_a, feat_gain
    )
    cells_grad = (grad_a + back_a).astype(jnp.bfloat16)
    row_summed = (
        lax.psum_scatter(
            feat_gain_grad.astype(jnp.bfloat16), "row", scatter_dimension=0, tiled=True
        ).astype(jnp.float32),
        lax.psum_scatter(
            feat_shift_grad.astype(jnp.bfloat16), "row", scatter_dimension=0, tiled=True
        ).astype(jnp.float32),
        lax.psum_scatter(
            feat_query_grad.astype(jnp.bfloat16), "row", scatter_dimension=0, tiled=True
        ).astype(jnp.float32),
        lax.psum_scatter(
            feat_key_grad.astype(jnp.bfloat16), "row", scatter_dimension=0, tiled=True
        ).astype(jnp.float32),
        lax.psum_scatter(
            feat_value_grad.astype(jnp.bfloat16), "row", scatter_dimension=0, tiled=True
        ).astype(jnp.float32),
        lax.psum_scatter(
            feat_out_grad.astype(jnp.bfloat16), "row", scatter_dimension=0, tiled=True
        ).astype(jnp.float32),
        lax.psum_scatter(
            feat_bias_grad.astype(jnp.bfloat16), "row", scatter_dimension=0, tiled=True
        ).astype(jnp.float32),
        lax.psum_scatter(
            row_gain_grad.astype(jnp.bfloat16), "row", scatter_dimension=0, tiled=True
        ).astype(jnp.float32),
        lax.psum_scatter(
            row_shift_grad.astype(jnp.bfloat16), "row", scatter_dimension=0, tiled=True
        ).astype(jnp.float32),
        lax.psum_scatter(
            row_query_grad.astype(jnp.bfloat16), "row", scatter_dimension=0, tiled=True
        ).astype(jnp.float32),
        lax.psum_scatter(
            row_key_grad.astype(jnp.bfloat16), "row", scatter_dimension=0, tiled=True
        ).astype(jnp.float32),
        lax.psum_scatter(
            row_value_grad.astype(jnp.bfloat16), "row", scatter_dimension=0, tiled=True
        ).astype(jnp.float32),
        lax.psum_scatter(
            row_out_grad.astype(jnp.bfloat16), "row", scatter_dimension=0, tiled=True
        ).astype(jnp.float32),
        lax.psum_scatter(
            row_bias_grad.astype(jnp.bfloat16), "row", scatter_dimension=0, tiled=True
        ).astype(jnp.float32),
        lax.psum_scatter(
            mlp_gain_grad.astype(jnp.bfloat16), "row", scatter_dimension=0, tiled=True
        ).astype(jnp.float32),
        lax.psum_scatter(
            mlp_shift_grad.astype(jnp.bfloat16), "row", scatter_dimension=0, tiled=True
        ).astype(jnp.float32),
        lax.psum_scatter(
            up_weight_grad.astype(jnp.bfloat16), "row", scatter_dimension=0, tiled=True
        ).astype(jnp.float32),
        lax.psum_scatter(
            up_bias_grad.astype(jnp.bfloat16), "row", scatter_dimension=0, tiled=True
        ).astype(jnp.float32),
        lax.psum_scatter(
            down_weight_grad.astype(jnp.bfloat16), "row", scatter_dimension=0, tiled=True
        ).astype(jnp.float32),
        lax.psum_scatter(
            down_bias_grad.astype(jnp.bfloat16), "row", scatter_dimension=0, tiled=True
        ).astype(jnp.float32),
    )
    (
        part_fg,
        part_fs,
        part_fq,
        part_fk,
        part_fv,
        part_fo,
        part_fb,
        part_rg,
        part_rs,
        part_rq,
        part_rk,
        part_rv,
        part_ro,
        part_rb,
        part_mg,
        part_ms,
        part_uw,
        part_ub,
        part_dw,
        part_db,
    ) = row_summed
    summed = (
        lax.psum(part_fg.astype(jnp.bfloat16), "tab").astype(jnp.float32),
        lax.psum(part_fs.astype(jnp.bfloat16), "tab").astype(jnp.float32),
        lax.psum(part_fq.astype(jnp.bfloat16), "tab").astype(jnp.float32),
        lax.psum(part_fk.astype(jnp.bfloat16), "tab").astype(jnp.float32),
        lax.psum(part_fv.astype(jnp.bfloat16), "tab").astype(jnp.float32),
        lax.psum(part_fo.astype(jnp.bfloat16), "tab").astype(jnp.float32),
        lax.psum(part_fb.astype(jnp.bfloat16), "tab").astype(jnp.float32),
        lax.psum(part_rg.astype(jnp.bfloat16), "tab").astype(jnp.float32),
        lax.psum(part_rs.astype(jnp.bfloat16), "tab").astype(jnp.float32),
        lax.psum(part_rq.astype(jnp.bfloat16), "tab").astype(jnp.float32),
        lax.psum(part_rk.astype(jnp.bfloat16), "tab").astype(jnp.float32),
        lax.psum(part_rv.astype(jnp.bfloat16), "tab").astype(jnp.float32),
        lax.psum(part_ro.astype(jnp.bfloat16), "tab").astype(jnp.float32),
        lax.psum(part_rb.astype(jnp.bfloat16), "tab").astype(jnp.float32),
        lax.psum(part_mg.astype(jnp.bfloat16), "tab").astype(jnp.float32),
        lax.psum(part_ms.astype(jnp.bfloat16), "tab").astype(jnp.float32),
        lax.psum(part_uw.astype(jnp.bfloat16), "tab").astype(jnp.float32),
        lax.psum(part_ub.astype(jnp.bfloat16), "tab").astype(jnp.float32),
        lax.psum(part_dw.astype(jnp.bfloat16), "tab").astype(jnp.float32),
        lax.psum(part_db.astype(jnp.bfloat16), "tab").astype(jnp.float32),
    )
    return (
        layer_out[None],
        cells_grad[None],
        summed[0],
        summed[1],
        summed[2],
        summed[3],
        summed[4],
        summed[5],
        summed[6],
        summed[7],
        summed[8],
        summed[9],
        summed[10],
        summed[11],
        summed[12],
        summed[13],
        summed[14],
        summed[15],
        summed[16],
        summed[17],
        summed[18],
        summed[19],
    )


def solution(mesh):
    in_specs = (
        P("tab", "row", None, None),
        P("tab", "row", None, None),
        P("tab"),
        P("tab"),
        P(),
        P(),
        P(),
        P(),
        P(),
        P(),
        P(),
        P(),
        P(),
        P(),
        P(),
        P(),
        P(),
        P(),
        P(),
        P(),
        P(),
        P(),
        P(),
        P(),
    )
    out_specs = (
        P("tab", "row", None, None),
        P("tab", "row", None, None),
        P("row"),
        P("row"),
        P("row", None),
        P("row", None),
        P("row", None),
        P("row", None),
        P("row"),
        P("row"),
        P("row"),
        P("row", None),
        P("row", None),
        P("row", None),
        P("row", None),
        P("row"),
        P("row"),
        P("row"),
        P("row", None),
        P("row"),
        P("row", None),
        P("row"),
    )
    return jax.shard_map(shards, mesh=mesh, in_specs=in_specs, out_specs=out_specs, check_vma=False)
```

profile of v0, /device:TPU:0, one launch (start us, length us, event | category | flops | bytes accessed | tf_op | source)
XLA Modules:
  0.0 885.3 jit_solution(11723977111391763241)
XLA Ops:
  16.2 5.6 reshape.202
  21.8 5.7 convolution_convert_fusion.4
  32.9 5.6 convolution_convert_fusion.5
  38.5 5.7 reshape.200
  44.2 10.0 %fusion.67 = f32[256,4,12,12]{2,3,1,0:T(8,128)} fusion(bf16[256,12,4,128]{3,2,0,1:T(4,128)(2,1)} %reshape.202, bf16[256,12,4,128]{3,2,0,1:T(4,128)(2,1)} %reshape.201), kind=kOutput, calls=%fused_computation.101 | convolution fusion | flops 37748736 | bytes 6881280 | tf_op jit(solution)/shard_map/rfhd,rghd->rhfg/dot_general | solution.py:96
  54.2 10.3 %fusion.176 = (f32[256,4,12]{2,1,0:T(4,128)S(1)}, f32[256,4,12,12]{2,3,1,0:T(8,128)S(1)}) fusion(f32[256,4,12,12]{2,3,1,0:T(8,128)} %fusion.67), kind=kOutput, calls=%fused_computation.212 | output fusion | flops 589835 | bytes 1228800 | tf_op jit(solution)/shard_map/sub | solution.py:99
  72.8 7.8 copy.132
  108.9 70.0 %all-gather.7.cloned.1.call-done = bf16[1024,12,512]{2,0,1:T(8,128)(2,1)} async-done(((bf16[256,12,512]{2,0,1:T(8,128)(2,1)}), bf16[1024,12,512]{2,0,1:T(8,128)(2,1)}) %all-gather.7.cloned.1.call-update) | async-done | bytes 12582928 | tf_op jit(solution)/shard_map/all_gather | solution.py:113
  178.9 17.5 %copy.202 = bf16[1024,12,512]{0,2,1:T(8,128)(2,1)} copy(bf16[1024,12,512]{2,0,1:T(8,128)(2,1)} %all-gather.7.cloned.1.call-done) | data formatting | bytes 25165824 | tf_op jit(solution)/shard_map/reshape | solution.py:50
  196.5 23.4 %fusion.1 = (f32[12,4,256]{2,1,0:T(4,128)S(1)}, f32[12,4,256,1024]{3,2,1,0:T(8,128)}) fusion(pred[1024]{0:T(1024)(128)(4,1)S(1)} %iota_compare_fusion, bf16[1024,12,4,128]{0,3,2,1:T(8,128)(2,1)} %bitcast.299, bf16[12,32,4,8,128]{4,3,2,1,0:T(8,128)(2,1)} %copy-done.11), kind=kOutput, calls=%fused_computation.8 | convolution fusion | flops 3258961920 | bytes 66110464 | tf_op jit(solution)/shard_map/ifhd,jfhd->fhij/dot_general | solution.py:119
  219.9 21.4 %exponential_reduce_fusion = f32[12,4,256]{2,1,0:T(4,128)S(1)} fusion(f32[12,4,256,1024]{3,2,1,0:T(8,128)} %get-tuple-element.74, f32[12,4,256]{2,1,0:T(4,128)S(1)} %get-tuple-element.73, pred[1024]{0:T(1024)(128)(4,1)S(1)} %iota_compare_fusion), kind=kLoop, calls=%fused_computation.6 | loop fusion | flops 50319360 | bytes 50430976 | tf_op jit(solution)/shard_map/reduce_sum | solution.py:131
  241.3 21.3 %all-gather.5.cloned.1.call-done = bf16[1024,12,512]{2,0,1:T(8,128)(2,1)} async-done(((bf16[256,12,512]{2,0,1:T(8,128)(2,1)}), bf16[1024,12,512]{2,0,1:T(8,128)(2,1)}) %all-gather.5.cloned.1.call-update) | async-done | bytes 12582928 | tf_op jit(solution)/shard_map/all_gather | solution.py:114
  262.6 27.8 %fusion.95 = bf16[12,4,128,256]{3,2,1,0:T(8,128)(2,1)} fusion(f32[12,4,256,1024]{3,2,1,0:T(8,128)} %get-tuple-element.74, f32[12,4,256]{2,1,0:T(4,128)S(1)} %bitcast.319, pred[1024]{0:T(1024)(128)(4,1)S(1)} %iota_compare_fusion, bf16[1024,12,512]{2,0,1:T(8,128)(2,1)} %all-gather.5.cloned.1.call-done), kind=kOutput, calls=%fused_computation.132 | convolution fusion | flops 3273129984 | bytes 66110464 | tf_op jit(solution)/shard_map/fhij,jfhd->ifhd/dot_general | solution.py:134
  290.4 5.7 fusion.178
  297.3 16.9 %multiply_convert_fusion.2 = (bf16[256,12,2048]{2,0,1:T(8,128)(2,1)}, f32[256,12,2048]{2,0,1:T(8,128)}) fusion(f32[2048]{0:T(1024)S(1)} %copy-done.58, bf16[512,2048]{1,0:T(8,128)(2,1)S(1)} %copy-done, f32[256,12,512]{2,0,1:T(8,128)S(1)} %get-tuple-element.76, f32[512]{0:T(512)S(1)} %copy-done.60, f32[512]{0:T(512)S(1)} %copy-done.55, ...), kind=kOutput, calls=%fused_computation.25 | convolution fusion | flops 6513229824 | bytes 46174208 | tf_op jit(solution)/shard_map/rfd,de->rfe/dot_general | solution.py:38
  314.2 26.5 %fusion.179 = (bf16[2048]{0:T(1024)(128)(2,1)}, bf16[256,12,2048]{2,0,1:T(8,128)(2,1)}) fusion(f32[256,12,2048]{2,0,1:T(8,128)} %get-tuple-element.78, f32[2048]{0:T(1024)S(1)} %copy-done.58, bf16[2048,512]{1,0:T(8,128)(2,1)} %param.46, bf16[1,256,12,512]{3,1,2,0:T(8,128)(2,1)S(1)} %copy-done.14, f32[256]{0:T(256)S(1)} %compare_convert_fusion), kind=kOutput, calls=%fused_computation.215 | convolution fusion | flops 6585579520 | bytes 43004928 | tf_op jit(solution)/shard_map/rfe,de->rfd/dot_general | solution.py:42
  340.7 11.5 %multiply_reduce_fusion.3 = (bf16[512]{0:T(512)(128)(2,1)}, f32[256,12]{0,1:T(8,128)S(1)}, f32[256,12]{0,1:T(8,128)S(1)}, bf16[512]{0:T(512)(128)(2,1)}, f32[256,12,512]{2,0,1:T(8,128)S(1)}) fusion(f32[256,12,512]{2,0,1:T(8,128)S(1)} %get-tuple-element.76, f32[256,12]{0,1:T(8,128)S(1)} %add_rsqrt_fusion, f32[256,12]{0,1:T(8,128)S(1)} %broadcast_multiply_fusion.6, ...), kind=kOutput, calls=%fused_computation.72 | convolution fusion | flops 6456599552 | bytes 27316224 | tf_op jit(solution)/shard_map/rfe,de->rfd/dot_general | solution.py:42
  362.3 6.3 fusion.131
  368.7 42.4 %multiply_reduce_fusion = (f32[12,4,256]{2,1,0:T(4,128)S(1)}, f32[12,4,256,1024]{3,2,1,0:T(8,128)}) fusion(f32[12,4,256,1024]{3,2,1,0:T(8,128)} %get-tuple-element.74, f32[12,4,256]{2,1,0:T(4,128)S(1)} %bitcast.320, pred[1024]{0:T(1024)(128)(4,1)S(1)} %iota_compare_fusion, bf16[12,32,4,8,128]{4,3,2,1,0:T(8,128)(2,1)} %copy-done.10, ...), kind=kOutput, calls=%fused_computation.4 | convolution fusion | flops 3284127744 | bytes 116491264 | tf_op jit(solution)/shard_map/ifhd,jfhd->fhij/dot_general | solution.py:170
  411.1 38.5 %multiply_convert_fusion.9 = bf16[12,4,128,256]{3,2,1,0:T(8,128)(2,1)} fusion(bf16[1024,12,4,128]{0,3,2,1:T(8,128)(2,1)} %bitcast.300, f32[12,4,256,1024]{3,2,1,0:T(8,128)} %get-tuple-element.81, f32[12,4,256,1024]{3,2,1,0:T(8,128)} %get-tuple-element.74, f32[12,4,256]{2,1,0:T(4,128)S(1)} %get-tuple-element.80, f32[12,4,256]{2,1,0:T(4,128)S(1)} %bitcast.321, ...), kind=kOutput, calls=%fused_computation.79 | convolution fusion | flops 3299868672 | bytes 116491264 | tf_op jit(solution)/shard_map/fhij,jfhd->ifhd/dot_general | solution.py:177
  455.6 14.8 %bitcast_convert_fusion.1 = bf16[512,2048]{1,0:T(8,128)(2,1)} fusion(bf16[256,12,2048]{2,0,1:T(8,128)(2,1)} %get-tuple-element.87, f32[256,12,512]{2,0,1:T(8,128)} %copy-done.3, f32[512]{0:T(512)S(1)} %copy-done.61, f32[512]{0:T(512)S(1)} %copy-done.55, f32[256,12]{0,1:T(8,128)S(1)} %add_rsqrt_fusion, f32[256,12]{0,1:T(8,128)S(1)} %broadcast_multiply_fusion.6), kind=kOutput, calls=%fused_computation.109 | convolution fusion | flops 6451363840 | bytes 21000192 | tf_op jit(solution)/shard_map/rfd,rfe->de/dot_general | solution.py:46
  472.4 5.6 all_gather.23
  478.1 5.6 all_gather.25
  483.8 6.4 fusion.141
  490.2 11.8 %bitcast_convert_fusion = bf16[2048,512]{1,0:T(8,128)(2,1)} fusion(bf16[256,12,2048]{2,0,1:T(8,128)(2,1)} %get-tuple-element.77, bf16[1,256,12,512]{3,1,2,0:T(8,128)(2,1)} %param.25, f32[256]{0:T(256)S(1)} %compare_convert_fusion), kind=kOutput, calls=%fused_computation.108 | convolution fusion | flops 6448218112 | bytes 17826816 | tf_op jit(solution)/shard_map/rfd,rfe->de/dot_general | solution.py:46
  502.3 23.5 %fusion.81 = f32[12,4,1024,256]{3,2,1,0:T(8,128)} fusion(bf16[1024,12,4,128]{3,0,2,1:T(8,128)(2,1)} %all-gather.9.cloned.1.call-done, bf16[256,12,512]{2,0,1:T(8,128)(2,1)} %convolution_convert_fusion.1), kind=kOutput, calls=%fused_computation.118 | convolution fusion | flops 3221225472 | bytes 66060288 | tf_op jit(solution)/shard_map/ifhd,jfhd->fhij/dot_general | solution.py:200
  525.8 32.3 %multiply_convert_fusion.8 = bf16[12,4,128,256]{3,2,1,0:T(8,128)(2,1)} fusion(bf16[1024,12,4,128]{3,0,2,1:T(8,128)(2,1)} %all-gather.9.cloned.1.call-done, f32[12,4,1024,256]{3,2,1,0:T(8,128)} %fusion.81, f32[12,4,1024]{2,1,0:T(4,128)S(1)} %sub.145, f32[12,4,1024]{2,1,0:T(4,128)S(1)} %sub.142, pred[256]{0:T(512)(128)(4,1)S(1)} %fusion.156, ...), kind=kOutput, calls=%fused_computation.78 | convolution fusion | flops 6521094144 | bytes 82182400 | tf_op jit(solution)/shard_map/fhij,ifhd->jfhd/dot_general | solution.py:210
  558.1 6.3 fusion.138
  564.4 24.2 %fusion.92 = bf16[12,4,128,256]{3,2,1,0:T(8,128)(2,1)} fusion(bf16[1024,12,4,128]{3,0,2,1:T(8,128)(2,1)} %all-gather.11.cloned.1.call-done, f32[12,4,1024,256]{3,2,1,0:T(8,128)} %fusion.81, f32[12,4,1024]{2,1,0:T(4,128)S(1)} %sub.142, pred[256]{0:T(512)(128)(4,1)S(1)} %fusion.156), kind=kOutput, calls=%fused_computation.131 | convolution fusion | flops 3273129984 | bytes 66257152 | tf_op jit(solution)/shard_map/fhij,ifhd->jfhd/dot_general | solution.py:213
  588.7 12.2 %multiply_reduce_fusion.4 = (bf16[512]{0:T(512)(128)(2,1)S(1)}, f32[256,12]{0,1:T(8,128)S(1)}, f32[256,12]{0,1:T(8,128)S(1)}, bf16[512]{0:T(512)(128)(2,1)S(1)}, f32[256,12,512]{2,0,1:T(8,128)}) fusion(f32[256,12,512]{2,0,1:T(8,128)} %copy-done.2, f32[256,12]{0,1:T(8,128)S(1)} %copy-done.39, f32[256,12]{0,1:T(8,128)S(1)} %copy-done.37, ...), kind=kOutput, calls=%fused_computation.73 | convolution fusion | flops 1627907072 | bytes 28889088 | tf_op jit(solution)/shard_map/rfe,de->rfd/dot_general | solution.py:42
  603.7 7.5 fusion.175
  628.5 13.7 %multiply_reduce_fusion.1 = (f32[256,4,12]{2,1,0:T(4,128)S(1)}, f32[256,4,12,12]{2,3,1,0:T(8,128)}) fusion(f32[256,4,12,12]{2,3,1,0:T(8,128)} %copy-done.9, f32[256,4,12]{2,1,0:T(4,128)S(1)} %copy-done.21, bf16[256,12,4,128]{3,2,0,1:T(4,128)(2,1)} %reshape.200, bf16[256,12,4,128]{3,2,0,1:T(4,128)(2,1)} %reshape.212), kind=kOutput, calls=%fused_computation.44 | convolution fusion | flops 38178816 | bytes 7569408 | tf_op jit(solution)/shard_map/rfhd,rghd->rhfg/dot_general | solution.py:238
  642.3 6.4 fusion.128
  648.9 8.8 convert_bitcast_fusion.1
  657.8 7.6 copy.160
  665.3 6.4 fusion.124
  671.8 7.3 multiply_convert_fusion.7
  685.8 7.5 copy.154
  693.4 6.4 fusion.122
  700.1 7.8 fusion.73
  707.9 7.6 copy.157
  715.5 6.4 fusion.123
  722.0 14.5 %fusion.75 = bf16[1,256,12,512]{3,1,2,0:T(8,128)(2,1)} fusion(f32[256,12,512]{2,0,1:T(8,128)} %copy-done.3, f32[256]{0:T(256)S(1)} %copy-done.49, f32[512]{0:T(512)S(1)} %copy-done.64, bf16[256,12,2048]{2,0,1:T(8,128)(2,1)} %get-tuple-element.77, bf16[2048,512]{1,0:T(8,128)(2,1)} %param.46), kind=kOutput, calls=%fused_computation.114 | convolution fusion | flops 6448742400 | bytes 24120320 | tf_op jit(solution)/shard_map/rfd,de->rfe/dot_general | solution.py:38
  749.3 10.6 %fusion.50 = (bf16[512]{0:T(512)(128)(2,1)S(1)}, f32[256,12]{0,1:T(8,128)S(1)}, f32[256,12]{0,1:T(8,128)S(1)}, bf16[512]{0:T(512)(128)(2,1)S(1)}, f32[256,12,512]{2,0,1:T(8,128)}) fusion(bf16[1,256,12,512]{3,1,2,0:T(8,128)(2,1)} %param.24, f32[256,12]{0,1:T(8,128)S(1)} %copy-done.43, f32[256,12]{0,1:T(8,128)S(1)} %copy-done.41, f32[512]{0:T(512)S(1)} %copy-done.47, ...), kind=kOutput, calls=%fused_computation.65 | convolution fusion | flops 1629479936 | bytes 25743360 | tf_op jit(solution)/shard_map/rfe,de->rfd/dot_general | solution.py:42
  760.0 11.0 %all-reduce.12 = (bf16[512]{0:T(512)(128)(2,1)S(1)}, bf16[512]{0:T(512)(128)(2,1)S(1)}, bf16[512]{0:T(512)(128)(2,1)S(1)}, bf16[512]{0:T(512)(128)(2,1)S(1)}, bf...) all-reduce(bf16[512]{0:T(512)(128)(2,1)S(1)} %get-tuple-element.26,, ...), channel_id=2, replica_groups=mesh['tab'=8,'row'=4] {'row'}, use_global_device_ids=true, to_apply=%region_19.20.clone | all-reduce | flops 6656 | bytes 26624
  771.7 22.4 %all-reduce.10 = (bf16[128]{0:T(256)(128)(2,1)S(1)}, bf16[128]{0:T(256)(128)(2,1)S(1)}, bf16[128]{0:T(256)(128)(2,1)S(1)}, bf16[128]{0:T(256)(128)(2,1)S(1)}, bf...) all-reduce(bf16[128]{0:T(256)(128)(2,1)S(1)} %dynamic-slice.1, ...), channel_id=1, replica_groups=mesh['tab'=8,'row'=4] {'tab'}, use_global_device_ids=true, to_apply=%region_20.21 | all-reduce | flops 1664 | bytes 6656 | tf_op jit(solution)/shard_map/psum | solution.py:358
  799.3 8.7 fusion.76
  808.0 53.0 %all-reduce.15.cloned.1.call-done = (bf16[128,512]{1,0:T(8,128)(2,1)}, bf16[128,512]{1,0:T(8,128)(2,1)}, bf16[128,512]{1,0:T(8,128)(2,1)}, bf16[128,512]{1,0:T(8...) async-done(((bf16[128,512]{1,0:T(8,128)(2,1)}, ...) | async-done | bytes 2097168 | tf_op jit(solution)/shard_map/psum | solution.py:360
  (248 shorter events, 131.1 us)
Async XLA Ops:
  7.2 290.1 %copy-start = (bf16[512,2048]{1,0:T(8,128)(2,1)S(1)}, bf16[512,2048]{1,0:T(8,128)(2,1)}, u32[]{:S(2)}) copy-start(bf16[512,2048]{1,0:T(8,128)(2,1)} %param.44) | copy-start | bytes 6291460
  7.2 171.7 %all-gather.7.cloned.1.call-start = ((), (), s32[]{:S(2)}) async-start(), calls=%async_computation.11 | async-start | bytes 15728640 | tf_op jit(solution)/shard_map/all_gather | solution.py:113
  9.8 23.1 %copy-start.40 = (f32[256,12]{0,1:T(8,128)}, f32[256,12]{0,1:T(8,128)S(1)}, u32[]{:S(2)}) copy-start(f32[256,12]{0,1:T(8,128)S(1)} %broadcast_multiply_fusion.8) | copy-start | bytes 36868
  12.7 20.2 %copy-start.42 = (f32[256,12]{0,1:T(8,128)}, f32[256,12]{0,1:T(8,128)S(1)}, u32[]{:S(2)}) copy-start(f32[256,12]{0,1:T(8,128)S(1)} %add_rsqrt_fusion.2) | copy-start | bytes 36868
  21.8 11.1 %copy-start.34 = (bf16[512,512]{1,0:T(8,128)(2,1)S(1)}, bf16[512,512]{1,0:T(8,128)(2,1)}, u32[]{:S(2)}) copy-start(bf16[512,512]{1,0:T(8,128)(2,1)} %param.32) | copy-start | bytes 1572868
  54.2 13.9 %copy-start.15 = (bf16[256,12,4,128]{3,2,0,1:T(4,128)(2,1)S(1)}, bf16[256,12,4,128]{3,2,0,1:T(4,128)(2,1)}, u32[]{:S(2)}) copy-start(bf16[256,12,4,128]{3,2,0,1:T(4,128)(2,1)} %reshape.200) | copy-start | bytes 9437188
  72.8 7.8 copy-start.28
  72.8 7.8 copy-start.59
  94.0 168.6 %all-gather.5.cloned.1.call-start = ((), (), s32[]{:S(2)}) async-start(), calls=%async_computation.10 | async-start | bytes 15728640 | tf_op jit(solution)/shard_map/all_gather | solution.py:114
  99.6 402.7 %all-gather.9.cloned.1.call-start = ((), (), s32[]{:S(2)}) async-start(), calls=%async_computation.12 | async-start | bytes 15728640 | tf_op jit(solution)/shard_map/all_gather | solution.py:194
  107.5 418.3 %all-gather.11.cloned.1.call-start = ((), (), s32[]{:S(2)}) async-start(), calls=%async_computation.13 | async-start | bytes 15728640 | tf_op jit(solution)/shard_map/all_gather | solution.py:195
  108.9 381.3 %copy-start.48 = (f32[256]{0:T(256)}, f32[256]{0:T(256)S(1)}, u32[]{:S(2)}) copy-start(f32[256]{0:T(256)S(1)} %compare_convert_fusion) | copy-start | bytes 3076
  262.6 27.8 %copy-start.19 = (bf16[512,512]{1,0:T(8,128)(2,1)S(1)}, bf16[512,512]{1,0:T(8,128)(2,1)}, u32[]{:S(2)}) copy-start(bf16[512,512]{1,0:T(8,128)(2,1)} %param.40) | copy-start | bytes 1572868
  262.6 27.8 %copy-start.54 = (f32[512]{0:T(512)S(1)}, f32[512]{0:T(512)}, u32[]{:S(2)}) copy-start(f32[512]{0:T(512)} %param.41) | copy-start | bytes 6148
  296.1 56.1 %copy-start.3 = (f32[256,12,512]{2,0,1:T(8,128)}, f32[256,12,512]{2,0,1:T(8,128)S(1)}, u32[]{:S(2)}) copy-start(f32[256,12,512]{2,0,1:T(8,128)S(1)} %get-tuple-element.76) | copy-start | bytes 18874372
  297.3 16.9 %copy-start.14 = (bf16[1,256,12,512]{3,1,2,0:T(8,128)(2,1)S(1)}, bf16[1,256,12,512]{3,1,2,0:T(8,128)(2,1)}, u32[]{:S(2)}) copy-start(bf16[1,256,12,512]{3,1,2,0:T(8,128)(2,1)} %param.25) | copy-start | bytes 9437188
  362.2 383.4 %reduce-scatter.25.cloned.1.call-start = ((), (), s32[]{:S(2)}) async-start(), calls=%async_computation.21 | async-start | bytes 655360 | tf_op jit(solution)/shard_map/reduce_scatter | solution.py:310
  368.6 377.0 %reduce-scatter.19.cloned.1.call-start = ((), (), s32[]{:S(2)}) async-start(), calls=%async_computation.18 | async-start | bytes 655360 | tf_op jit(solution)/shard_map/reduce_scatter | solution.py:301
  455.2 15.3 %copy-start.65 = (u32[32]{0:T(128)S(1)}, u32[32]{0:T(128)}, u32[]{:S(2)}) copy-start(u32[32]{0:T(128)} %constant.54) | copy-start | bytes 388
  455.2 28.6 %copy-start.25 = (bf16[512,512]{1,0:T(8,128)(2,1)S(1)}, bf16[512,512]{1,0:T(8,128)(2,1)}, u32[]{:S(2)}) copy-start(bf16[512,512]{1,0:T(8,128)(2,1)} %param.37) | copy-start | bytes 1572868
  455.2 290.5 %reduce-scatter.27.cloned.1.call-start = ((), (), s32[]{:S(2)}) async-start(), calls=%async_computation.22 | async-start | bytes 2621440 | tf_op jit(solution)/shard_map/reduce_scatter | solution.py:322
  470.4 275.2 %reduce-scatter.29.cloned.1.call-start = ((), (), s32[]{:S(2)}) async-start(), calls=%async_computation.23 | async-start | bytes 2621440 | tf_op jit(solution)/shard_map/reduce_scatter | solution.py:328
  502.0 243.7 %reduce-scatter.23.cloned.1.call-start = ((), (), s32[]{:S(2)}) async-start(), calls=%async_computation.20 | async-start | bytes 655360 | tf_op jit(solution)/shard_map/reduce_scatter | solution.py:307
  525.8 32.3 %copy-start.27 = (bf16[512,512]{1,0:T(8,128)(2,1)S(1)}, bf16[512,512]{1,0:T(8,128)(2,1)}, u32[]{:S(2)}) copy-start(bf16[512,512]{1,0:T(8,128)(2,1)} %param.38) | copy-start | bytes 1572868
  564.4 24.2 %copy-start.23 = (bf16[512,512]{1,0:T(8,128)(2,1)S(1)}, bf16[512,512]{1,0:T(8,128)(2,1)}, u32[]{:S(2)}) copy-start(bf16[512,512]{1,0:T(8,128)(2,1)} %param.39) | copy-start | bytes 1572868
  564.4 24.2 %copy-start.37 = (f32[256,12]{0,1:T(8,128)S(1)}, f32[256,12]{0,1:T(8,128)}, u32[]{:S(2)}) copy-start(f32[256,12]{0,1:T(8,128)} %copy-done.36) | copy-start | bytes 36868
  564.4 24.2 %copy-start.39 = (f32[256,12]{0,1:T(8,128)S(1)}, f32[256,12]{0,1:T(8,128)}, u32[]{:S(2)}) copy-start(f32[256,12]{0,1:T(8,128)} %copy-done.38) | copy-start | bytes 36868
  564.4 24.2 %copy-start.45 = (f32[512]{0:T(512)S(1)}, f32[512]{0:T(512)}, u32[]{:S(2)}) copy-start(f32[512]{0:T(512)} %param.35) | copy-start | bytes 6148
  588.6 12.2 %copy-start.17 = (bf16[256,12,512]{2,0,1:T(8,128)(2,1)S(1)}, bf16[256,12,512]{2,0,1:T(8,128)(2,1)}, u32[]{:S(2)}) copy-start(bf16[256,12,512]{2,0,1:T(8,128)(2,1)} %copy-done.16) | copy-start | bytes 9437188
  588.6 12.2 %copy-start.18 = (bf16[12,4,128,256]{3,2,1,0:T(8,128)(2,1)S(1)}, bf16[12,4,128,256]{3,2,1,0:T(8,128)(2,1)}, u32[]{:S(2)}) copy-start(bf16[12,4,128,256]{3,2,1,0:T(8,128)(2,1)} %fusion.92) | copy-start | bytes 9437188
  603.6 142.1 %reduce-scatter.21.cloned.1.call-start = ((), (), s32[]{:S(2)}) async-start(), calls=%async_computation.19 | async-start | bytes 655360 | tf_op jit(solution)/shard_map/reduce_scatter | solution.py:304
  603.7 10.2 %copy-start.29 = (bf16[512,512]{1,0:T(8,128)(2,1)S(1)}, bf16[512,512]{1,0:T(8,128)(2,1)}, u32[]{:S(2)}) copy-start(bf16[512,512]{1,0:T(8,128)(2,1)} %param.33) | copy-start | bytes 1572868
  628.5 117.2 %reduce-scatter.17.cloned.1.call-start = ((), (), s32[]{:S(2)}) async-start(), calls=%async_computation.17 | async-start | bytes 655360 | tf_op jit(solution)/shard_map/reduce_scatter | solution.py:289
  648.7 97.0 %reduce-scatter.15.cloned.1.call-start = ((), (), s32[]{:S(2)}) async-start(), calls=%async_computation.16 | async-start | bytes 655360 | tf_op jit(solution)/shard_map/reduce_scatter | solution.py:286
  657.7 7.6 copy-start.63
  671.8 74.0 %reduce-scatter.11.cloned.1.call-start = ((), (), s32[]{:S(2)}) async-start(), calls=%async_computation.14 | async-start | bytes 655360 | tf_op jit(solution)/shard_map/reduce_scatter | solution.py:280
  671.8 9.3 %copy-start.7 = (bf16[256,12,4,128]{3,2,0,1:T(4,128)(2,1)S(1)}, bf16[256,12,4,128]{3,2,0,1:T(4,128)(2,1)}, u32[]{:S(2)}) copy-start(bf16[256,12,4,128]{3,2,0,1:T(4,128)(2,1)} %reshape.202) | copy-start | bytes 9437188
  699.8 49.4 %reduce-scatter.13.cloned.1.call-start = ((), (), s32[]{:S(2)}) async-start(), calls=%async_computation.15 | async-start | bytes 655360 | tf_op jit(solution)/shard_map/reduce_scatter | solution.py:283
  722.0 14.6 %copy-start.31 = (bf16[512,512]{1,0:T(8,128)(2,1)S(1)}, bf16[512,512]{1,0:T(8,128)(2,1)}, u32[]{:S(2)}) copy-start(bf16[512,512]{1,0:T(8,128)(2,1)} %param.31) | copy-start | bytes 1572868
  722.0 139.1 %all-reduce.15.cloned.1.call-start = ((), (), s32[]{:S(2)}) async-start(), calls=%async_computation.24 | async-start | bytes 4194304 | tf_op jit(solution)/shard_map/psum | solution.py:360
  722.0 14.5 %copy-start.13 = (bf16[256,12,4,128]{0,3,2,1:T(8,128)(2,1)S(1)}, bf16[256,12,4,128]{0,3,2,1:T(8,128)(2,1)}, u32[]{:S(2)}) copy-start(bf16[256,12,4,128]{0,3,2,1:T(8,128)(2,1)} %copy.157) | copy-start | bytes 9437188
  741.1 8.2 copy-start.35
  749.3 10.7 %copy-start.50 = (bf16[512]{0:T(512)(128)(2,1)S(1)}, bf16[512]{0:T(512)(128)(2,1)}, u32[]{:S(2)}) copy-start(bf16[512]{0:T(512)(128)(2,1)} %get-tuple-element.64) | copy-start | bytes 3076
  749.3 10.7 %copy-start.51 = (bf16[512]{0:T(512)(128)(2,1)S(1)}, bf16[512]{0:T(512)(128)(2,1)}, u32[]{:S(2)}) copy-start(bf16[512]{0:T(512)(128)(2,1)} %get-tuple-element.68) | copy-start | bytes 3076
  749.3 10.7 %copy-start.52 = (bf16[2048]{0:T(1024)(128)(2,1)S(1)}, bf16[2048]{0:T(1024)(128)(2,1)}, u32[]{:S(2)}) copy-start(bf16[2048]{0:T(1024)(128)(2,1)} %get-tuple-element.86) | copy-start | bytes 12292
  749.3 10.7 %copy-start.56 = (bf16[512]{0:T(512)(128)(2,1)S(1)}, bf16[512]{0:T(512)(128)(2,1)}, u32[]{:S(2)}) copy-start(bf16[512]{0:T(512)(128)(2,1)} %get-tuple-element.22) | copy-start | bytes 3076
  749.3 10.7 %copy-start.57 = (bf16[512]{0:T(512)(128)(2,1)S(1)}, bf16[512]{0:T(512)(128)(2,1)}, u32[]{:S(2)}) copy-start(bf16[512]{0:T(512)(128)(2,1)} %get-tuple-element.31) | copy-start | bytes 3076
  799.3 79.0 %copy-start.1 = (bf16[512,2048]{1,0:T(8,128)(2,1)S(1)}, bf16[512,2048]{1,0:T(8,128)(2,1)}, u32[]{:S(2)}) copy-start(bf16[512,2048]{1,0:T(8,128)(2,1)} %param.44) | copy-start | bytes 6291460
  (33 other events, 133.1 us)
Sparse Core Ops, SparseCore 0:
  94.1 84.7 all-gather.6
  180.5 82.0 all-gather.4
  264.2 82.0 all-gather.8
  362.3 82.6 all-gather.10
  447.4 21.6 reduce-scatter.24
  471.6 21.6 reduce-scatter.18
  495.8 31.4 reduce-scatter.26
  529.9 31.4 reduce-scatter.28
  603.7 22.6 reduce-scatter.22
  628.9 22.3 reduce-scatter.20
  653.8 21.6 reduce-scatter.16
  678.0 21.6 reduce-scatter.14
  702.8 21.6 reduce-scatter.10
  727.5 21.6 reduce-scatter.12
  754.0 106.9 all-reduce.14
where the time goes:
time: 893 us; the launch traced here: 885 us
  matrix products  492 us (55%)
  waiting for transfers between devices  148 us (17%)
  local copies, waits for them, and re-layouts  90.7 us (10%)
  other arithmetic  90.5 us (10%)
  blocking collectives  44.6 us (5%)
  between operations  17.9 us (2%)
    dot_general x10, matrix products, project_back(): jnp.einsum('rfe,de->rfd', upstream, weight, preferred_element_type=jnp.fl...  88 us
    dot_general x10, matrix products, outer_sum(): jnp.einsum('rfd,rfe->de', left_side, upstream, preferred_element_type=jnp...  72.4 us
    all_gather x1, waiting for transfers between devices, shards(): lax.all_gather(key_b, 'row', axis=0, tiled=True)  70 us
    dot_general x10, matrix products, project(): jnp.einsum('rfd,de->rfe', left_side, weight, preferred_element_type=jnp.f...  69.7 us
    psum x1, waiting for transfers between devices, shards(): lax.psum(part_fq.astype(jnp.bfloat16), 'tab').astype(jnp.float32)  53 us
    reshape x7, local copies, waits for them, and re-layouts, split_heads(): values.reshape(values.shape[0], values.shape[1], HEADS, values.shape[2] /...  44.8 us
    dot_general x1, matrix products, shards(): jnp.einsum('ifhd,jfhd->fhij', mixed_b_grad, split_heads(value_back), pref...  42.4 us
    dot_general x1, matrix products, shards(): jnp.einsum('fhij,jfhd->ifhd', score_b_grad, split_heads(key_back), prefer...  38.5 us
  transfers between devices with their start and end apart: 15, of which 4 were waited for; matrix products, arithmetic and copies ran while one was open for 63% of the time, Pallas kernels for 0%

commit v1 on v0

--- a/solution.py
+++ b/solution.py
@@ -1,8 +1,11 @@
+import functools
 import math
 
 import jax
 import jax.numpy as jnp
 from jax import lax
+from jax.experimental import pallas as pl
+from jax.experimental.pallas import tpu as pltpu
 from jax.sharding import PartitionSpec as P
 
 HEADS = 4
@@ -402,6 +405,647 @@
     )
 
 
+HEAD = 128
+GROUP = 16
+LOG2E = 1.4426950408889634
+F32 = jnp.float32
+BF16 = jnp.bfloat16
+
+
+def dot_nn(a, b):
+    return jnp.dot(a, b, preferred_element_type=F32)
+
+
+def dot_nt(a, b):
+    return lax.dot_general(a, b, (((1,), (1,)), ((), ())), preferred_element_type=F32)
+
+
+def dot_tn(a, b):
+    return lax.dot_general(a, b, (((0,), (0,)), ((), ())), preferred_element_type=F32)
+
+
+def unit_of(values):
+    centred = values - jnp.mean(values, -1, keepdims=True)
+    inverse = lax.rsqrt(jnp.mean(centred * centred, -1, keepdims=True) + EPSILON)
+    return centred * inverse, inverse
+
+
+def norm_back(upstream, unit, inverse, gain):
+    scaled = upstream * gain
+    return inverse * (
+        scaled
+        - jnp.mean(scaled, -1, keepdims=True)
+        - unit * jnp.mean(scaled * unit, -1, keepdims=True)
+    )
+
+
+def column_sum(values):
+    return jnp.sum(values, 0, keepdims=True)
+
+
+def vmem_spec():
+    return pl.BlockSpec(memory_space=pltpu.VMEM)
+
+
+def smem_spec():
+    return pl.BlockSpec(memory_space=pltpu.SMEM)
+
+
+def params_of(mib=56):
+    return pltpu.CompilerParams(vmem_limit_bytes=mib * 1024 * 1024)
+
+
+def piece_feature(me, index, group):
+    return (me ^ (index // group)) * group + index % group
+
+
+def fill_order(order_ref, me, feats, group):
+    rows = lax.broadcasted_iota(jnp.int32, (GROUP, GROUP * GROUP), 0)
+    cols = lax.broadcasted_iota(jnp.int32, (GROUP, GROUP * GROUP), 1)
+    for index in range(feats):
+        hit = cols == rows * GROUP + piece_feature(me, index, group)
+        order_ref[index * GROUP : (index + 1) * GROUP, :] = jnp.where(hit, 1.0, 0.0).astype(BF16)
+
+
+def same_row(size):
+    rows = lax.broadcasted_iota(jnp.int32, (size, size), 0)
+    cols = lax.broadcasted_iota(jnp.int32, (size, size), 1)
+    return (rows % GROUP) == (cols % GROUP)
+
+
+def to_pieces_kernel(group, me_ref, cells_ref, *rest):
+    feats = cells_ref.shape[2]
+    outs, (padded, order) = rest[:feats], rest[feats:]
+    rows = cells_ref.shape[1]
+
+    @pl.when(pl.program_id(0) == 0)
+    def _():
+        fill_order(order, me_ref[0], feats, group)
+        padded[...] = jnp.zeros_like(padded)
+
+    padded[:, :feats, :] = cells_ref[0]
+    width = cells_ref.shape[3]
+    flat = padded[...].reshape(rows * GROUP, width)
+    for part in range(rows // GROUP):
+        moved = dot_nn(order[...], flat[part * GROUP * GROUP : (part + 1) * GROUP * GROUP]).astype(BF16)
+        for index in range(feats):
+            outs[index][part * GROUP : (part + 1) * GROUP, :] = moved[index * GROUP : (index + 1) * GROUP]
+
+
+def to_pieces(me, cells, group, block=64):
+    _, rows, feats, width = cells.shape
+    return pl.pallas_call(
+        functools.partial(to_pieces_kernel, group),
+        grid=(rows // block,),
+        in_specs=[smem_spec(), pl.BlockSpec((1, block, feats, width), lambda i: (0, i, 0, 0))],
+        out_specs=[pl.BlockSpec((block, width), lambda i: (i, 0))] * feats,
+        out_shape=[jax.ShapeDtypeStruct((rows, width), BF16)] * feats,
+        scratch_shapes=[
+            pltpu.VMEM((block, GROUP, width), BF16),
+            pltpu.VMEM((feats * GROUP, GROUP * GROUP), BF16),
+        ],
+        compiler_params=params_of(),
+        name="to_pieces",
+    )(me, cells)
+
+
+def from_pieces_kernel(group, me_ref, *rest):
+    feats = len(rest) - 2
+    ins, out_ref, order = rest[:feats], rest[feats], rest[feats + 1]
+    rows, width = ins[0].shape
+
+    @pl.when(pl.program_id(0) == 0)
+    def _():
+        fill_order(order, me_ref[0], feats, group)
+
+    for part in range(rows // GROUP):
+        tall = jnp.concatenate([ref[part * GROUP : (part + 1) * GROUP, :] for ref in ins], 0)
+        moved = dot_tn(order[...], tall).astype(BF16).reshape(GROUP, GROUP, width)
+        out_ref[0, part * GROUP : (part + 1) * GROUP] = moved[:, :feats, :]
+
+
+def from_pieces(me, pieces, group, block=64):
+    rows, width = pieces[0].shape
+    feats = len(pieces)
+    return pl.pallas_call(
+        functools.partial(from_pieces_kernel, group),
+        grid=(rows // block,),
+        in_specs=[smem_spec()] + [pl.BlockSpec((block, width), lambda i: (i, 0))] * feats,
+        out_specs=pl.BlockSpec((1, block, feats, width), lambda i: (0, i, 0, 0)),
+        out_shape=jax.ShapeDtypeStruct((1, rows, feats, width), BF16),
+        scratch_shapes=[pltpu.VMEM((feats * GROUP, GROUP * GROUP), BF16)],
+        compiler_params=params_of(),
+        name="from_pieces",
+    )(me, *pieces)
+
+
+def feat_forward_kernel(
+    group, me_ref, cells_ref, gain, shift, w_query, w_key, w_value, w_out, bias, *rest
+):
+    feats, rows, width = cells_ref.shape[2], cells_ref.shape[1], cells_ref.shape[3]
+    outs = rest[:feats]
+    x_ref, q_ref, k_ref, v_ref, mixed_ref, padded, order = rest[feats:]
+    size = feats * GROUP
+    scale = 1.0 / math.sqrt(HEAD)
+
+    @pl.when(pl.program_id(0) == 0)
+    def _():
+        fill_order(order, me_ref[0], feats, group)
+        padded[...] = jnp.zeros_like(padded)
+
+    padded[:, :feats, :] = cells_ref[0]
+    flat = padded[...].reshape(rows * GROUP, width)
+    parts = rows // GROUP
+    for part in range(parts):
+        moved = dot_nn(order[...], flat[part * GROUP * GROUP : (part + 1) * GROUP * GROUP])
+        x_ref[part * size : (part + 1) * size, :] = moved.astype(BF16)
+    unit, _ = unit_of(x_ref[...].astype(F32))
+    normed = (unit * gain[...] + shift[...]).astype(BF16)
+    q_ref[...] = dot_nn(normed, w_query[...]).astype(BF16)
+    k_ref[...] = dot_nn(normed, w_key[...]).astype(BF16)
+    v_ref[...] = dot_nn(normed, w_value[...]).astype(BF16)
+    own = same_row(size)
+    for part in range(parts):
+        span = slice(part * size, (part + 1) * size)
+        for head in range(HEADS):
+            lanes = slice(head * HEAD, (head + 1) * HEAD)
+            scores = jnp.where(own, dot_nt(q_ref[span, lanes], k_ref[span, lanes]) * scale, NEGATIVE)
+            grown = jnp.exp(scores - jnp.max(scores, -1, keepdims=True))
+            probs = (grown / jnp.sum(grown, -1, keepdims=True)).astype(BF16)
+            mixed_ref[span, lanes] = dot_nn(probs, v_ref[span, lanes]).astype(BF16)
+    after = x_ref[...].astype(F32) + dot_nn(mixed_ref[...], w_out[...]) + bias[...]
+    after = after.astype(BF16)
+    for part in range(parts):
+        for index in range(feats):
+            start = part * size + index * GROUP
+            outs[index][part * GROUP : (part + 1) * GROUP, :] = after[start : start + GROUP]
+
+
+def feat_forward(me, cells, weights, group, block=64):
+    _, rows, feats, width = cells.shape
+    tokens = block * feats
+    kept = jax.ShapeDtypeStruct((rows * feats, width), BF16)
+    whole = pl.BlockSpec((width, width), lambda i: (0, 0))
+    vector = pl.BlockSpec((1, width), lambda i: (0, 0))
+    return pl.pallas_call(
+        functools.partial(feat_forward_kernel, group),
+        grid=(rows // block,),
+        in_specs=[smem_spec(), pl.BlockSpec((1, block, feats, width), lambda i: (0, i, 0, 0))]
+        + [vector, vector, whole, whole, whole, whole, vector],
+        out_specs=[pl.BlockSpec((block, width), lambda i: (i, 0))] * feats
+        + [pl.BlockSpec((tokens, width), lambda i: (i, 0))] * 5,
+        out_shape=[jax.ShapeDtypeStruct((rows, width), BF16)] * feats + [kept] * 5,
+        scratch_shapes=[
+            pltpu.VMEM((block, GROUP, width), BF16),
+            pltpu.VMEM((feats * GROUP, GROUP * GROUP), BF16),
+        ],
+        compiler_params=params_of(),
+        name="feat_forward",
+    )(me, cells, *weights)
+
+
+def pick(lane, *values):
+    out = jnp.zeros(lane.shape, F32)
+    for index, value in enumerate(values):
+        out = jnp.where(lane == index, value, out)
+    return out
+
+
+def thirds(values):
+    high = values.astype(BF16).astype(F32)
+    rest = values - high
+    middle = rest.astype(BF16).astype(F32)
+    return high, middle, rest - middle
+
+
+def lane_of(rows):
+    return lax.broadcasted_iota(jnp.int32, (rows, HEAD), 1)
+
+
+def key_extra(info_ref, piece, rows):
+    first = (info_ref[0] ^ piece) * rows
+    row = lax.broadcasted_iota(jnp.int32, (rows, HEAD), 0) + first
+    lane = lane_of(rows)
+    bias = jnp.where(row < info_ref[2], 0.0, NEGATIVE)
+    return jnp.where(lane == 0, bias, jnp.where(lane < 4, 1.0, 0.0)).astype(BF16)
+
+
+def row_forward_kernel(pieces, info_ref, *rest):
+    ins, rest = rest[:pieces], rest[pieces:]
+    gain, shift, w_query, w_key, w_value, q_ref, k_ref, v_ref, mixed_ref, extra_ref, keys = rest
+    rows = ins[0].shape[0]
+    tile = 256
+    scale = LOG2E / math.sqrt(HEAD)
+    for piece in range(pieces):
+        span = slice(piece * rows, (piece + 1) * rows)
+        unit, _ = unit_of(ins[piece][...].astype(F32))
+        normed = (unit * gain[...] + shift[...]).astype(BF16)
+        q_ref[span, :] = dot_nn(normed, w_query[...]).astype(BF16)
+        k_ref[span, :] = dot_nn(normed, w_key[...]).astype(BF16)
+        v_ref[span, :] = dot_nn(normed, w_value[...]).astype(BF16)
+        keys[span, :] = key_extra(info_ref, piece, rows)
+    lane = lane_of(tile)
+    ones = jnp.where(lane == 0, 1.0, 0.0).astype(BF16)
+
+    def one_tile(index, carry):
+        span = pl.ds(pl.multiple_of(index * tile, tile), tile)
+        for head in range(HEADS):
+            lanes = slice(head * HEAD, (head + 1) * HEAD)
+            scores = dot_nt(
+                jnp.concatenate([q_ref[span, lanes], ones], 1),
+                jnp.concatenate([k_ref[:, lanes], keys[...]], 1),
+            )
+            highest = jnp.max(scores, -1, keepdims=True)
+            grown = jnp.exp2((scores - highest) * scale)
+            total = jnp.sum(grown, -1, keepdims=True)
+            mixed = dot_nn(grown.astype(BF16), v_ref[:, lanes]) / total
+            mixed_ref[span, lanes] = mixed.astype(BF16)
+            high, middle, low = thirds(-(highest + jnp.log2(total) * (1.0 / scale)))
+            extra_ref[span, lanes] = pick(lane, 1.0, high, middle, low).astype(BF16)
+        return carry
+
+    lax.fori_loop(0, q_ref.shape[0] // tile, one_tile, 0)
+
+
+def row_forward(info, ins, weights):
+    rows, width = ins[0].shape
+    whole = jax.ShapeDtypeStruct((rows * len(ins), width), BF16)
+    return pl.pallas_call(
+        functools.partial(row_forward_kernel, len(ins)),
+        in_specs=[smem_spec()] + [vmem_spec()] * (len(ins) + 5),
+        out_specs=[vmem_spec()] * 5,
+        out_shape=[whole] * 4 + [jax.ShapeDtypeStruct((rows * len(ins), HEADS * HEAD), BF16)],
+        scratch_shapes=[pltpu.VMEM((rows * len(ins), HEAD), BF16)],
+        compiler_params=params_of(),
+        name="row_forward",
+    )(info, *ins, *weights)
+
+
+def mlp_kernel(pieces, first, info_ref, *rest):
+    afters, cots, rest = rest[:pieces], rest[pieces : 2 * pieces], rest[2 * pieces :]
+    mixed_ref, w_row, row_bias, gain, shift, w_up, up_bias, w_down, down_bias = rest[:9]
+    rest = rest[9:]
+    if not first:
+        old, rest = rest[:4], rest[4:]
+    outs, rest = rest[:pieces], rest[pieces:]
+    mixed_grad_ref, grad_ref, up_ref, down_ref, row_ref, vec_ref = rest
+    rows, width = afters[0].shape
+    wide = w_up.shape[1]
+    chunk = 512
+    if first:
+        for ref in (up_ref, down_ref, row_ref, vec_ref):
+            ref[...] = jnp.zeros_like(ref)
+    else:
+        for ref, was in zip((up_ref, down_ref, row_ref, vec_ref), old):
+            ref[...] = was[...]
+    c_one, c_three = math.sqrt(2.0 / math.pi), math.sqrt(2.0 / math.pi) * 0.044715
+    for piece in range(pieces):
+        span = slice(piece * rows, (piece + 1) * rows)
+        row = lax.broadcasted_iota(jnp.int32, (rows, 1), 0) + (info_ref[0] ^ piece) * rows
+        keep = row < info_ref[1]
+        mixed = mixed_ref[span, :]
+        after_b = afters[piece][...].astype(F32) + dot_nn(mixed, w_row[...]) + row_bias[...]
+        unit, inverse = unit_of(after_b)
+        normed = (unit * gain[...] + shift[...]).astype(BF16)
+        grad_c_low = jnp.where(keep, cots[piece][...], jnp.zeros((), BF16))
+        grad_c = grad_c_low.astype(F32)
+        normed_t = normed.T
+        grad_t = grad_c_low.T
+        total = after_b + down_bias[...]
+        upstream = jnp.zeros((rows, width), F32)
+        for part in range(wide // chunk):
+            lanes = slice(part * chunk, (part + 1) * chunk)
+            hidden = dot_nn(normed, w_up[:, lanes]) + up_bias[:, lanes]
+            square = hidden * hidden
+            bent = jnp.tanh(hidden * (c_one + c_three * square))
+            half = 0.5 * (1.0 + bent)
+            active = (hidden * half).astype(BF16)
+            slope = half + (0.5 * hidden) * (1.0 - bent * bent) * (c_one + 3.0 * c_three * square)
+            hidden_grad = (dot_nt(grad_c_low, w_down[lanes, :]) * slope).astype(BF16)
+            total += dot_nn(active, w_down[lanes, :])
+            down_ref[:, lanes] += dot_nn(grad_t, active)
+            up_ref[:, lanes] += dot_nn(normed_t, hidden_grad)
+            upstream += dot_nt(hidden_grad, w_up[:, lanes])
+            vec_ref[part : part + 1, :] += column_sum(hidden_grad.astype(F32))
+        outs[piece][...] = jnp.where(keep, total, 0.0).astype(BF16)
+        grad_b = grad_c + norm_back(upstream, unit, inverse, gain[...])
+        grad_low = grad_b.astype(BF16)
+        grad_ref[span, :] = grad_b
+        row_ref[...] += dot_tn(mixed, grad_low)
+        mixed_grad_ref[span, :] = dot_nt(grad_low, w_row[...]).astype(BF16)
+        vec_ref[4:5, :] += column_sum(grad_c)
+        vec_ref[5:6, :] += column_sum(upstream * unit)
+        vec_ref[6:7, :] += column_sum(upstream)
+        vec_ref[7:8, :] += column_sum(grad_b)
+
+
+def mlp(info, afters, cots, mixed, weights, old):
+    rows, width = afters[0].shape
+    count = len(afters)
+    wide = weights[4].shape[1]
+    first = old is None
+    sums = [
+        jax.ShapeDtypeStruct((width, wide), F32),
+        jax.ShapeDtypeStruct((width, wide), F32),
+        jax.ShapeDtypeStruct((width, width), F32),
+        jax.ShapeDtypeStruct((8, width), F32),
+    ]
+    args = [*afters, *cots, mixed, *weights] + ([] if first else list(old))
+    return pl.pallas_call(
+        functools.partial(mlp_kernel, count, first),
+        in_specs=[smem_spec()] + [vmem_spec()] * len(args),
+        out_specs=[vmem_spec()] * (count + 6),
+        out_shape=[jax.ShapeDtypeStruct((rows, width), BF16)] * count
+        + [jax.ShapeDtypeStruct((rows * count, width), BF16), jax.ShapeDtypeStruct((rows * count, width), F32)]
+        + sums,
+        compiler_params=params_of(60),
+        name="mlp",
+    )(info, *args)
+
+
+def row_backward_kernel(pieces, first, info_ref, *rest):
+    afters, rest = rest[:pieces], rest[pieces:]
+    q_ref, k_ref, v_ref, extra_ref, mixed_ref, mixed_grad_ref, grad_ref = rest[:7]
+    gain, shift, w_query, w_key, w_value = rest[7:12]
+    rest = rest[12:]
+    if not first:
+        old, rest = rest[:4], rest[4:]
+    outs, rest = rest[:pieces], rest[pieces:]
+    sum_query, sum_key, sum_value, vec_ref, keys, key_sum, value_sum, query_grad = rest
+    rows, width = afters[0].shape
+    tile = 256
+    scale = LOG2E / math.sqrt(HEAD)
+    score_scale = 1.0 / math.sqrt(HEAD)
+    for piece in range(pieces):
+        keys[piece * rows : (piece + 1) * rows, :] = key_extra(info_ref, piece, rows)
+    key_sum[...] = jnp.zeros_like(key_sum)
+    value_sum[...] = jnp.zeros_like(value_sum)
+    lane = lane_of(tile)
+
+    def one_tile(index, carry):
+        span = pl.ds(pl.multiple_of(index * tile, tile), tile)
+        for head in range(HEADS):
+            lanes = slice(head * HEAD, (head + 1) * HEAD)
+            query, upstream = q_ref[span, lanes], mixed_grad_ref[span, lanes]
+            scores = dot_nt(
+                jnp.concatenate([k_ref[:, lanes], keys[...]], 1),
+                jnp.concatenate([query, extra_ref[span, lanes]], 1),
+            )
+            probs = jnp.exp2(scores * scale)
+            row_dot = jnp.sum(
+                upstream.astype(F32) * mixed_ref[span, lanes].astype(F32), -1, keepdims=True
+            )
+            high, middle, low = thirds(-row_dot)
+            inner = dot_nt(
+                jnp.concatenate([v_ref[:, lanes], keys[...]], 1),
+                jnp.concatenate([upstream, pick(lane, 0.0, high, middle, low).astype(BF16)], 1),
+            )
+            value_sum[:, lanes] += dot_nn(probs.astype(BF16), upstream)
+            score_grad = (probs * inner).astype(BF16)
+            key_sum[:, lanes] += dot_nn(score_grad, query)
+            query_grad[span, lanes] = (dot_tn(score_grad, k_ref[:, lanes]) * score_scale).astype(BF16)
+        return carry
+
+    lax.fori_loop(0, q_ref.shape[0] // tile, one_tile, 0)
+    if first:
+        for ref in (sum_query, sum_key, sum_value, vec_ref):
+            ref[...] = jnp.zeros_like(ref)
+    else:
+        for ref, was in zip((sum_query, sum_key, sum_value, vec_ref), old):
+            ref[...] = was[...]
+    for piece in range(pieces):
+        span = slice(piece * rows, (piece + 1) * rows)
+        unit, inverse = unit_of(afters[piece][...].astype(F32))
+        normed_t = (unit * gain[...] + shift[...]).astype(BF16).T
+        d_query = query_grad[span, :]
+        d_key = (key_sum[span, :] * score_scale).astype(BF16)
+        d_value = value_sum[span, :].astype(BF16)
+        sum_query[...] += dot_nn(normed_t, d_query)
+        sum_key[...] += dot_nn(normed_t, d_key)
+        sum_value[...] += dot_nn(normed_t, d_value)
+        upstream = dot_nt(d_query, w_query[...]) + dot_nt(d_key, w_key[...]) + dot_nt(d_value, w_value[...])
+        grad_a = grad_ref[span, :] + norm_back(upstream, unit, inverse, gain[...])
+        outs[piece][...] = grad_a.astype(BF16)
+        vec_ref[0:1, :] += column_sum(upstream * unit)
+        vec_ref[1:2, :] += column_sum(upstream)
+        vec_ref[2:3, :] += column_sum(grad_a)
+
+
+def row_backward(info, afters, kept, mixed_grad, grad_b, weights, old):
+    rows, width = afters[0].shape
+    count = len(afters)
+    query, key, value, mixed, extra = kept
+    first = old is None
+    args = [*afters, query, key, value, extra, mixed, mixed_grad, grad_b, *weights]
+    args += [] if first else list(old)
+    return pl.pallas_call(
+        functools.partial(row_backward_kernel, count, first),
+        in_specs=[smem_spec()] + [vmem_spec()] * len(args),
+        out_specs=[vmem_spec()] * (count + 4),
+        out_shape=[jax.ShapeDtypeStruct((rows, width), BF16)] * count
+        + [jax.ShapeDtypeStruct((width, width), F32)] * 3
+        + [jax.ShapeDtypeStruct((8, width), F32)],
+        scratch_shapes=[
+            pltpu.VMEM((rows * count, HEAD), BF16),
+            pltpu.VMEM((rows * count, width), F32),
+            pltpu.VMEM((rows * count, width), F32),
+            pltpu.VMEM((rows * count, width), BF16),
+        ],
+        compiler_params=params_of(),
+        name="row_backward",
+    )(info, *args)
+
+
+def feat_backward_kernel(
+    group, feats, me_ref, x_ref, q_ref, k_ref, v_ref, mixed_ref, gain, shift, w_query, w_key, w_value, w_out, *rest
+):
+    grads, rest = rest[:feats], rest[feats:]
+    out_ref, sum_query, sum_key, sum_value, sum_out, vec_ref, order, d_query, d_key, d_value = rest
+    rows, width = grads[0].shape
+    parts, size = rows // GROUP, feats * GROUP
+    scale = 1.0 / math.sqrt(HEAD)
+
+    @pl.when(pl.program_id(0) == 0)
+    def _():
+        fill_order(order, me_ref[0], feats, group)
+        for ref in (sum_query, sum_key, sum_value, sum_out, vec_ref):
+            ref[...] = jnp.zeros_like(ref)
+
+    grad_low = jnp.concatenate(
+        [ref[part * GROUP : (part + 1) * GROUP, :] for part in range(parts) for ref in grads], 0
+    )
+    grad_a = grad_low.astype(F32)
+    sum_out[...] += dot_tn(mixed_ref[...], grad_low)
+    mixed_grad = dot_nt(grad_low, w_out[...]).astype(BF16)
+    own = same_row(size)
+    for part in range(parts):
+        span = slice(part * size, (part + 1) * size)
+        for head in range(HEADS):
+            lanes = slice(head * HEAD, (head + 1) * HEAD)
+            query, key, value = q_ref[span, lanes], k_ref[span, lanes], v_ref[span, lanes]
+            upstream = mixed_grad[span, lanes]
+            scores = jnp.where(own, dot_nt(query, key) * scale, NEGATIVE)
+            grown = jnp.exp(scores - jnp.max(scores, -1, keepdims=True))
+            probs = grown / jnp.sum(grown, -1, keepdims=True)
+            inner = dot_nt(upstream, value)
+            score_grad = (probs * (inner - jnp.sum(probs * inner, -1, keepdims=True))).astype(BF16)
+            d_query[span, lanes] = (dot_nn(score_grad, key) * scale).astype(BF16)
+            d_key[span, lanes] = (dot_tn(score_grad, query) * scale).astype(BF16)
+            d_value[span, lanes] = dot_tn(probs.astype(BF16), upstream).astype(BF16)
+    unit, inverse = unit_of(x_ref[...].astype(F32))
+    normed_t = (unit * gain[...] + shift[...]).astype(BF16).T
+    sum_query[...] += dot_nn(normed_t, d_query[...])
+    sum_key[...] += dot_nn(normed_t, d_key[...])
+    sum_value[...] += dot_nn(normed_t, d_value[...])
+    upstream = (
+        dot_nt(d_query[...], w_query[...])
+        + dot_nt(d_key[...], w_key[...])
+        + dot_nt(d_value[...], w_value[...])
+    )
+    cells = (grad_a + norm_back(upstream, unit, inverse, gain[...])).astype(BF16)
+    vec_ref[0:1, :] += column_sum(upstream * unit)
+    vec_ref[1:2, :] += column_sum(upstream)
+    for part in range(parts):
+        moved = dot_tn(order[...], cells[part * size : (part + 1) * size])
+        moved = moved.astype(BF16).reshape(GROUP, GROUP, width)
+        out_ref[0, part * GROUP : (part + 1) * GROUP] = moved[:, :feats, :]
+
+
+def feat_backward(me, kept, grads, weights, group, block=64):
+    rows, width = grads[0].shape
+    feats = len(grads)
+    tokens = block * feats
+    whole = pl.BlockSpec((width, width), lambda i: (0, 0))
+    vector = pl.BlockSpec((1, width), lambda i: (0, 0))
+    return pl.pallas_call(
+        functools.partial(feat_backward_kernel, group, feats),
+        grid=(rows // block,),
+        in_specs=[smem_spec()]
+        + [pl.BlockSpec((tokens, width), lambda i: (i, 0))] * 5
+        + [vector, vector, whole, whole, whole, whole]
+        + [pl.BlockSpec((block, width), lambda i: (i, 0))] * feats,
+        out_specs=[pl.BlockSpec((1, block, feats, width), lambda i: (0, i, 0, 0))]
+        + [whole] * 4
+        + [pl.BlockSpec((8, width), lambda i: (0, 0))],
+        out_shape=[jax.ShapeDtypeStruct((1, rows, feats, width), BF16)]
+        + [jax.ShapeDtypeStruct((width, width), F32)] * 4
+        + [jax.ShapeDtypeStruct((8, width), F32)],
+        scratch_shapes=[pltpu.VMEM((feats * GROUP, GROUP * GROUP), BF16)]
+        + [pltpu.VMEM((tokens, width), BF16)] * 3,
+        compiler_params=params_of(),
+        name="feat_backward",
+    )(me, *kept, *weights, *grads)
+
+
+def swap(values, step):
+    count = lax.axis_size("row")
+    if step == 0:
+        return values
+    return lax.ppermute(values, "row", [(index, index ^ step) for index in range(count)])
+
+
+def total_over(values):
+    part = lax.psum_scatter(values.astype(BF16), "row", scatter_dimension=0, tiled=True)
+    return lax.psum(part, "tab").astype(F32)
+
+
+def by_feature(
+    table_cells,
+    cotangent,
+    row_counts,
+    context_counts,
+    feat_gain,
+    feat_shift,
+    feat_query,
+    feat_key,
+    feat_value,
+    feat_out,
+    feat_bias,
+    row_gain,
+    row_shift,
+    row_query,
+    row_key,
+    row_value,
+    row_out,
+    row_bias,
+    mlp_gain,
+    mlp_shift,
+    up_weight,
+    up_bias,
+    down_weight,
+    down_bias,
+):
+    count = lax.axis_size("row")
+    feats = table_cells.shape[2]
+    group = feats // count
+    me = lax.axis_index("row").astype(jnp.int32)
+    place = me.reshape(1)
+    info = jnp.stack([me, row_counts[0], context_counts[0]])
+
+    def flat(vector):
+        return vector.reshape(1, -1)
+
+    cot_out = to_pieces(place, cotangent, group)
+    feat_weights = (flat(feat_gain), flat(feat_shift), feat_query, feat_key, feat_value, feat_out)
+    forward = feat_forward(place, table_cells, (*feat_weights, flat(feat_bias)), group)
+    after_out, kept_a = forward[:feats], forward[feats:]
+
+    row_weights = (flat(row_gain), flat(row_shift), row_query, row_key, row_value)
+    mlp_weights = (
+        row_out,
+        flat(row_bias),
+        flat(mlp_gain),
+        flat(mlp_shift),
+        up_weight,
+        flat(up_bias),
+        down_weight,
+        flat(down_bias),
+    )
+    afters = [[swap(after_out[k * group + j], k) for k in range(count)] for j in range(group)]
+    cots = [[swap(cot_out[k * group + j], k) for k in range(count)] for j in range(group)]
+    mlp_sums, row_sums = None, None
+    layer_back = [None] * feats
+    grad_back = [None] * feats
+    for j in range(group):
+        kept = row_forward(info, afters[j], row_weights)
+        found = mlp(info, afters[j], cots[j], kept[3], mlp_weights, mlp_sums)
+        layer, mixed_grad, grad_b, mlp_sums = found[:count], found[count], found[count + 1], found[count + 2 :]
+        back = row_backward(info, afters[j], kept, mixed_grad, grad_b, row_weights, row_sums)
+        grad, row_sums = back[:count], back[count:]
+        for k in range(count):
+            layer_back[k * group + j] = swap(layer[k], k)
+            grad_back[k * group + j] = swap(grad[k], k)
+    layer_out = from_pieces(place, layer_back, group)
+    cells_grad, *feat_sums = feat_backward(place, kept_a, grad_back, feat_weights, group)
+    up_sum, down_sum, row_out_sum, mlp_vec = mlp_sums
+    sum_rq, sum_rk, sum_rv, row_vec = row_sums
+    sum_fq, sum_fk, sum_fv, sum_fo, feat_vec = feat_sums
+    return (
+        layer_out,
+        cells_grad,
+        total_over(feat_vec[0]),
+        total_over(feat_vec[1]),
+        total_over(sum_fq),
+        total_over(sum_fk),
+        total_over(sum_fv),
+        total_over(sum_fo),
+        total_over(row_vec[2]),
+        total_over(row_vec[0]),
+        total_over(row_vec[1]),
+        total_over(sum_rq),
+        total_over(sum_rk),
+        total_over(sum_rv),
+        total_over(row_out_sum),
+        total_over(mlp_vec[7]),
+        total_over(mlp_vec[5]),
+        total_over(mlp_vec[6]),
+        total_over(up_sum),
+        total_over(mlp_vec[:4].reshape(-1)),
+        total_over(down_sum.T),
+        total_over(mlp_vec[4]),
+    )
+
+
 def solution(mesh):
     in_specs = (
         P("tab", "row", None, None),
@@ -453,4 +1097,6 @@
         P("row", None),
         P("row"),
     )
-    return jax.shard_map(shards, mesh=mesh, in_specs=in_specs, out_specs=out_specs, check_vma=False)
+    count = mesh.shape["row"]
+    body = by_feature if count in (1, 2, 4) else shards
+    return jax.shard_map(body, mesh=mesh, in_specs=in_specs, out_specs=out_specs, check_vma=False)

time: 893 us -> 706 us (0.79)
  matrix products: 492 us -> 0 us
  Pallas kernels: 0 us -> 290 us
  waiting for transfers between devices: 148 us -> 246 us
  local copies, waits for them, and re-layouts: 90.7 us -> 28.2 us
  other arithmetic: 90.5 us -> 33.9 us
  starting transfers between devices: 1.59 us -> 32.9 us
    dot_general x43 -> x0, matrix products: 492 us -> none  [the longest x10 88 us: project_back(): jnp.einsum('rfe,de->rfd', upstream, weight, preferred_element_type=jnp.fl...]
    pallas_call x0 -> x13, Pallas kernels: none -> 290 us  [the longest x3 87.7 us: mlp(): pl.pallas_call(functools.partial(mlp_kernel, count, first), in_specs=[sme...]
    reduce_scatter x10, waiting for transfers between devices: 3.54 us -> 153 us  [total_over(): lax.psum_scatter(values.astype(BF16), 'row', scatter_dimension=0, tiled=T...]
    all_gather x4 -> x0, waiting for transfers between devices: 91.3 us -> none  [the longest x1 70 us: shards(): lax.all_gather(key_b, 'row', axis=0, tiled=True)]
    ppermute x0 -> x36, waiting for transfers between devices: none -> 69.8 us  [swap(): lax.ppermute(values, 'row', [(index, index ^ step) for index in range(cou...]
    reshape x7 -> x0, local copies, waits for them, and re-layouts: 44.8 us -> none  [split_heads(): values.reshape(values.shape[0], values.shape[1], HEADS, values.shape[2] /...]
    reduce_sum x7 -> x0, other arithmetic: 40.5 us -> none  [the longest x1 21.4 us: shards(): jnp.sum(jnp.exp(scores_b - highest), -1, keepdims=True)]
    ppermute x0 -> x36, starting transfers between devices: none -> 32.2 us  [swap(): lax.ppermute(values, 'row', [(index, index ^ step) for index in range(cou...]
  transfers between devices with their start and end apart: 15 -> 47, of which waited for: 4 -> 23; matrix products, arithmetic and copies ran while one was open for 63% -> 6% of each run, Pallas kernels for 0% -> 28%
where the time goes in v1:
time: 706 us; the launch traced here: 696 us
  Pallas kernels  290 us (41%)
  waiting for transfers between devices  246 us (35%)
  blocking collectives  47.6 us (7%)
  other arithmetic  33.9 us (5%)
  starting transfers between devices  32.9 us (5%)
  local copies, waits for them, and re-layouts  28.2 us (4%)
  between operations  17.7 us (3%)
    reduce_scatter x10, waiting for transfers between devices, total_over(): lax.psum_scatter(values.astype(BF16), 'row', scatter_dimension=0, tiled=T...  153 us
    pallas_call x3, Pallas kernels, mlp(): pl.pallas_call(functools.partial(mlp_kernel, count, first), in_specs=[sme...  87.7 us
    ppermute x36, waiting for transfers between devices, swap(): lax.ppermute(values, 'row', [(index, index ^ step) for index in range(cou...  69.8 us
    pallas_call x3, Pallas kernels, row_backward(): pl.pallas_call(functools.partial(row_backward_kernel, count, first), in_s...  69.1 us
    pallas_call x1, Pallas kernels, feat_backward(): pl.pallas_call(functools.partial(feat_backward_kernel, group, feats), gri...  57.6 us
    pallas_call x3, Pallas kernels, row_forward(): pl.pallas_call(functools.partial(row_forward_kernel, len(ins)), in_specs=...  43.3 us
    ppermute x36, starting transfers between devices, swap(): lax.ppermute(values, 'row', [(index, index ^ step) for index in range(cou...  32.2 us
    unnamed x162, local copies, waits for them, and re-layouts  28.1 us
  transfers between devices with their start and end apart: 47, of which 23 were waited for; matrix products, arithmetic and copies ran while one was open for 6% of the time, Pallas kernels for 28%

profile of v1, /device:TPU:0, one launch (start us, length us, event | category | flops | bytes accessed | tf_op | source)
XLA Modules:
  0.0 695.7 jit_solution(5909094301627131556)
XLA Ops:
  7.2 5.8 copy.51.cells_ref
  13.0 21.1 %feat_forward.1 = (bf16[256,512]{1,0:T(8,128)(2,1)}, bf16[256,512]{1,0:T(8,128)(2,1)}, bf16[256,512]{1,0:T(8,128)(2,1)}, bf16[256,512]{1,0:T(8,128)(2,1)}, bf16[...) custom-call(s32[1]{0:T(128)} %bitcast.me_ref, ...), custom_call_target="tpu_custom_call" | custom-call | tf_op jit(solution)/shard_map/feat_forward/pallas_call | solution.py:590
  34.7 2.6 collective-permute-start.1
  37.3 3.9 copy.52.cells_ref
  41.2 5.2 to_pieces.1
  51.4 4.6 collective-permute-done.4.rest_6_
  57.9 3.2 collective-permute-done.5.rest_7_
  63.5 3.7 collective-permute-done.7.rest_2_
  67.7 4.6 collective-permute-done.8.rest_3_
  74.2 4.2 collective-permute-done.10.rest_6_
  79.0 5.1 collective-permute-done.13.rest_2_
  86.0 3.1 collective-permute-done.14.rest_3_
  93.3 14.7 %row_forward.3 = (bf16[1024,512]{1,0:T(8,128)(2,1)}, bf16[1024,512]{1,0:T(8,128)(2,1)}, bf16[1024,512]{1,0:T(8,128)(2,1)}, bf16[1024,512]{1,0:T(8,128)(2,1)}, bf16[1024,512]{1,0:T(8,128)(2,1)}) custom-call(s32[3]{0:T(128)} %pad_add_fusion.info_ref, bf16[256,512]{1,0:T(8,128)(2,1)} %get-tuple-element.126.rest_0_, bf16[256,512]{1,0:T(8,128)(2,1)} %copy-done.7, ...), custom_call_target="tpu_custom_call" | custom-call | tf_op jit(solution)/shard_map/row_forward/pallas_call | solution.py:673
  108.0 14.3 %row_forward.4 = (bf16[1024,512]{1,0:T(8,128)(2,1)}, bf16[1024,512]{1,0:T(8,128)(2,1)}, bf16[1024,512]{1,0:T(8,128)(2,1)}, bf16[1024,512]{1,0:T(8,128)(2,1)}, bf16[1024,512]{1,0:T(8,128)(2,1)}) custom-call(s32[3]{0:T(128)} %pad_add_fusion.info_ref, bf16[256,512]{1,0:T(8,128)(2,1)} %get-tuple-element.136.rest_0_, bf16[256,512]{1,0:T(8,128)(2,1)} %copy-done.1, ...), custom_call_target="tpu_custom_call" | custom-call | tf_op jit(solution)/shard_map/row_forward/pallas_call | solution.py:673
  122.3 14.4 %row_forward.5 = (bf16[1024,512]{1,0:T(8,128)(2,1)}, bf16[1024,512]{1,0:T(8,128)(2,1)}, bf16[1024,512]{1,0:T(8,128)(2,1)}, bf16[1024,512]{1,0:T(8,128)(2,1)}, bf16[1024,512]{1,0:T(8,128)(2,1)}) custom-call(s32[3]{0:T(128)} %pad_add_fusion.info_ref, bf16[256,512]{1,0:T(8,128)(2,1)} %get-tuple-element.150.rest_0_, bf16[256,512]{1,0:T(8,128)(2,1)} %copy-done.3, ...), custom_call_target="tpu_custom_call" | custom-call | tf_op jit(solution)/shard_map/row_forward/pallas_call | solution.py:673
  136.6 27.3 %mlp.3 = (bf16[256,512]{1,0:T(8,128)(2,1)}, bf16[256,512]{1,0:T(8,128)(2,1)}, bf16[256,512]{1,0:T(8,128)(2,1)}, bf16[256,512]{1,0:T(8,128)(2,1)}, bf16[1024,512]...) custom-call(s32[3]{0:T(128)} %pad_add_fusion.info_ref, ...), custom_call_target="tpu_custom_call" | custom-call | tf_op jit(solution)/shard_map/mlp/pallas_call | solution.py:754
  163.9 22.6 %row_backward.3 = (bf16[256,512]{1,0:T(8,128)(2,1)}, bf16[256,512]{1,0:T(8,128)(2,1)}, bf16[256,512]{1,0:T(8,128)(2,1)}, bf16[256,512]{1,0:T(8,128)(2,1)}, f32[5...) custom-call(s32[3]{0:T(128)} %pad_add_fusion.info_ref, ...), custom_call_target="tpu_custom_call" | custom-call | tf_op jit(solution)/shard_map/row_backward/pallas_call | solution.py:841
  187.3 30.0 %mlp.4 = (bf16[256,512]{1,0:T(8,128)(2,1)}, bf16[256,512]{1,0:T(8,128)(2,1)}, bf16[256,512]{1,0:T(8,128)(2,1)}, bf16[256,512]{1,0:T(8,128)(2,1)}, bf16[1024,512]...) custom-call(s32[3]{0:T(128)} %pad_add_fusion.info_ref, ...), custom_call_target="tpu_custom_call" | custom-call | tf_op jit(solution)/shard_map/mlp/pallas_call | solution.py:754
  218.3 30.4 %mlp.5 = (bf16[256,512]{1,0:T(8,128)(2,1)}, bf16[256,512]{1,0:T(8,128)(2,1)}, bf16[256,512]{1,0:T(8,128)(2,1)}, bf16[256,512]{1,0:T(8,128)(2,1)}, bf16[1024,512]...) custom-call(s32[3]{0:T(128)} %pad_add_fusion.info_ref, ...), custom_call_target="tpu_custom_call" | custom-call | tf_op jit(solution)/shard_map/mlp/pallas_call | solution.py:754
  248.7 23.1 %row_backward.4 = (bf16[256,512]{1,0:T(8,128)(2,1)}, bf16[256,512]{1,0:T(8,128)(2,1)}, bf16[256,512]{1,0:T(8,128)(2,1)}, bf16[256,512]{1,0:T(8,128)(2,1)}, f32[5...) custom-call(s32[3]{0:T(128)} %pad_add_fusion.info_ref, ...), custom_call_target="tpu_custom_call" | custom-call | tf_op jit(solution)/shard_map/row_backward/pallas_call | solution.py:841
  271.9 23.3 %row_backward.5 = (bf16[256,512]{1,0:T(8,128)(2,1)}, bf16[256,512]{1,0:T(8,128)(2,1)}, bf16[256,512]{1,0:T(8,128)(2,1)}, bf16[256,512]{1,0:T(8,128)(2,1)}, f32[5...) custom-call(s32[3]{0:T(128)} %pad_add_fusion.info_ref, ...), custom_call_target="tpu_custom_call" | custom-call | tf_op jit(solution)/shard_map/row_backward/pallas_call | solution.py:841
  295.2 2.2 convert_element_type.151
  305.6 5.6 collective-permute-done.32.rest_8_
  311.2 4.7 collective-permute-done.35.rest_11_
  319.3 6.0 collective-permute-done.31.rest_7_
  325.3 4.7 collective-permute-done.34.rest_10_
  330.0 6.5 collective-permute-done.30.rest_6_
  336.5 4.7 collective-permute-done.33.rest_9_
  341.9 57.6 %feat_backward.1 = (bf16[1,256,12,512]{3,2,1,0:T(8,128)(2,1)}, f32[512,512]{1,0:T(8,128)}, f32[512,512]{1,0:T(8,128)}, f32[512,512]{1,0:T(8,128)}, f32[512,512]{1,0:T(8,128)}, /*index=5*/f32[8,512]{1,0:T(8,128)}) custom-call(s32[1]{0:T(128)} %bitcast.me_ref, bf16[3072,512]{1,0:T(8,128)(2,1)} %get-tuple-element.173.x_ref, ...), custom_call_target="tpu_custom_call" | custom-call | tf_op jit(solution)/shard_map/feat_backward/pallas_call | solution.py:920
  399.5 2.3 convert_element_type.137
  405.9 3.9 convert_element_type.165
  409.9 3.9 convert_bitcast_fusion
  414.3 9.6 %reduce-scatter.11.cloned.1.call-done = bf16[128,512]{1,0:T(8,128)(2,1)} async-done(((bf16[512,512]{1,0:T(8,128)(2,1)}), bf16[128,512]{1,0:T(8,128)(2,1)}) %reduce-scatter.11.cloned.1.call-update) | async-done | bytes 131088 | tf_op jit(solution)/shard_map/reduce_scatter | solution.py:948
  423.9 24.8 %reduce-scatter.13.cloned.1.call-done = bf16[128,512]{1,0:T(8,128)(2,1)} async-done(((bf16[512,512]{1,0:T(8,128)(2,1)}), bf16[128,512]{1,0:T(8,128)(2,1)}) %reduce-scatter.13.cloned.1.call-update) | async-done | bytes 131088 | tf_op jit(solution)/shard_map/reduce_scatter | solution.py:948
  448.7 24.8 %reduce-scatter.15.cloned.1.call-done = bf16[128,512]{1,0:T(8,128)(2,1)} async-done(((bf16[512,512]{1,0:T(8,128)(2,1)}), bf16[128,512]{1,0:T(8,128)(2,1)}) %reduce-scatter.15.cloned.1.call-update) | async-done | bytes 131088 | tf_op jit(solution)/shard_map/reduce_scatter | solution.py:948
  473.5 24.3 %reduce-scatter.17.cloned.1.call-done = bf16[128,512]{1,0:T(8,128)(2,1)} async-done(((bf16[512,512]{1,0:T(8,128)(2,1)}), bf16[128,512]{1,0:T(8,128)(2,1)}) %reduce-scatter.17.cloned.1.call-update) | async-done | bytes 131088 | tf_op jit(solution)/shard_map/reduce_scatter | solution.py:948
  497.8 34.6 %reduce-scatter.27.cloned.1.call-done = bf16[128,2048]{1,0:T(8,128)(2,1)} async-done(((bf16[512,2048]{1,0:T(8,128)(2,1)}), bf16[128,2048]{1,0:T(8,128)(2,1)}) %reduce-scatter.27.cloned.1.call-update) | async-done | bytes 524304 | tf_op jit(solution)/shard_map/reduce_scatter | solution.py:948
  532.4 34.6 %reduce-scatter.29.cloned.1.call-done = bf16[512,512]{0,1:T(8,128)(2,1)} async-done(((bf16[2048,512]{0,1:T(8,128)(2,1)}), bf16[512,512]{0,1:T(8,128)(2,1)}) %reduce-scatter.29.cloned.1.call-update) | async-done | bytes 524304 | tf_op jit(solution)/shard_map/reduce_scatter | solution.py:948
  572.8 3.4 collective-permute-done.23.rest_8_
  576.3 4.7 collective-permute-done.26.rest_11_
  583.6 26.1 %all-reduce.12 = (bf16[512]{0:T(512)(128)(2,1)S(1)}, bf16[512]{0:T(512)(128)(2,1)S(1)}, bf16[512]{0:T(512)(128)(2,1)S(1)}, bf16[512]{0:T(512)(128)(2,1)S(1)}, bf...) all-reduce(bf16[512]{0:T(512)(128)(2,1)S(1)} %get-tuple-element.282, ...), channel_id=2, replica_groups=mesh['tab'=8,'row'=4] {'row'}, use_global_device_ids=true, to_apply=%region_0.0.clone | all-reduce | flops 6656 | bytes 26624
  610.5 21.5 %all-reduce.10 = (bf16[128]{0:T(256)(128)(2,1)S(1)}, bf16[128]{0:T(256)(128)(2,1)S(1)}, bf16[128]{0:T(256)(128)(2,1)S(1)}, bf16[128]{0:T(256)(128)(2,1)S(1)}, bf...) all-reduce(bf16[128]{0:T(256)(128)(2,1)S(1)} %dynamic-slice.1, ...), channel_id=1, replica_groups=mesh['tab'=8,'row'=4] {'tab'}, use_global_device_ids=true, to_apply=%region_1.0 | all-reduce | flops 1664 | bytes 6656 | tf_op jit(solution)/shard_map/psum | solution.py:949
  637.1 5.6 copy.54
  643.8 5.6 from_pieces.1
  649.4 5.8 copy.53
  655.2 23.2 %all-reduce.15.cloned.1.call-done = (bf16[512,512]{0,1:T(8,128)(2,1)}, bf16[128,512]{1,0:T(8,128)(2,1)}, bf16[128,512]{1,0:T(8,128)(2,1)}, bf16[128,512]{1,0:T(8...) async-done(((bf16[512,512]{0,1:T(8,128)(2,1)}, ...) | async-done | bytes 2097168 | tf_op jit(solution)/shard_map/psum | solution.py:949
  678.5 2.2 convert_element_type.166
  680.7 2.2 copy.55
  (269 shorter events, 55.7 us)
Async XLA Ops:
  7.2 407.0 %reduce-scatter.19.cloned.1.call-start = ((), (), s32[]{:S(2)}) async-start(), calls=%async_computation.14 | async-start | bytes 655360 | tf_op jit(solution)/shard_map/reduce_scatter | solution.py:948
  34.2 14.4 %collective-permute-start = (bf16[256,512]{1,0:T(8,128)(2,1)}, bf16[256,512]{1,0:T(8,128)(2,1)S(1)}, u32[]{:S(2)}, u32[]{:S(2)}) collective-permute-start(bf16[256,512]{1,0:T(8,128)(2,1)} %get-tuple-element.127), channel_id=1, source_target_pairs={{0,1},{1,0},{2,3},{3,2},{4,5},{5,4},{6,7},{7,6},{8,9},{9,8},{10,11... | collective-permute-start | bytes 786440 | tf_op jit(solution)/shard_map/ppermute | solution.py:944
  34.7 13.9 %collective-permute-start.1 = (bf16[256,512]{1,0:T(8,128)(2,1)}, bf16[256,512]{1,0:T(8,128)(2,1)S(1)}, u32[]{:S(2)}, u32[]{:S(2)}) collective-permute-start(bf16[256,512]{1,0:T(8,128)(2,1)} %get-tuple-element.128), channel_id=1, source_target_pairs={{0,2},{1,3},{2,0},{3,1},{4,6},{5,7},{6,4},{7,5},{8,10},{9,11},{10,... | collective-permute-start | bytes 786440 | tf_op jit(solution)/shard_map/ppermute | solution.py:944
  37.2 12.5 %collective-permute-start.2 = (bf16[256,512]{1,0:T(8,128)(2,1)}, bf16[256,512]{1,0:T(8,128)(2,1)S(1)}, u32[]{:S(2)}, u32[]{:S(2)}) collective-permute-start(bf16[256,512]{1,0:T(8,128)(2,1)} %get-tuple-element.129), channel_id=1, source_target_pairs={{0,3},{1,2},{2,1},{3,0},{4,7},{5,6},{6,5},{7,4},{8,11},{9,10},{10,... | collective-permute-start | bytes 786440 | tf_op jit(solution)/shard_map/ppermute | solution.py:944
  46.4 4.8 collective-permute-start.3
  46.6 9.3 %collective-permute-start.4 = (bf16[256,512]{1,0:T(8,128)(2,1)}, bf16[256,512]{1,0:T(8,128)(2,1)S(1)}, u32[]{:S(2)}, u32[]{:S(2)}) collective-permute-start(bf16[256,512]{1,0:T(8,128)(2,1)} %get-tuple-element.132), channel_id=1, source_target_pairs={{0,2},{1,3},{2,0},{3,1},{4,6},{5,7},{6,4},{7,5},{8,10},{9,11},{10,... | collective-permute-start | bytes 786440 | tf_op jit(solution)/shard_map/ppermute | solution.py:944
  48.6 12.6 %collective-permute-start.5 = (bf16[256,512]{1,0:T(8,128)(2,1)}, bf16[256,512]{1,0:T(8,128)(2,1)S(1)}, u32[]{:S(2)}, u32[]{:S(2)}) collective-permute-start(bf16[256,512]{1,0:T(8,128)(2,1)} %get-tuple-element.133), channel_id=1, source_target_pairs={{0,3},{1,2},{2,1},{3,0},{4,7},{5,6},{6,5},{7,4},{8,11},{9,10},{10,... | collective-permute-start | bytes 786440 | tf_op jit(solution)/shard_map/ppermute | solution.py:944
  48.6 12.9 %collective-permute-start.6 = (bf16[256,512]{1,0:T(8,128)(2,1)S(1)}, bf16[256,512]{1,0:T(8,128)(2,1)S(1)}, u32[]{:S(2)}, u32[]{:S(2)}) collective-permute-start(bf16[256,512]{1,0:T(8,128)(2,1)S(1)} %copy-done.70), channel_id=1, source_target_pairs={{0,1},{1,0},{2,3},{3,2},{4,5},{5,4},{6,7},{7,6},{8,9},{9,8},{10,11... | collective-permute-start | bytes 786440 | tf_op jit(solution)/shard_map/ppermute | solution.py:944
  49.7 17.5 %collective-permute-start.7 = (bf16[256,512]{1,0:T(8,128)(2,1)S(1)}, bf16[256,512]{1,0:T(8,128)(2,1)S(1)}, u32[]{:S(2)}, u32[]{:S(2)}) collective-permute-start(bf16[256,512]{1,0:T(8,128)(2,1)S(1)} %copy-done.69), channel_id=1, source_target_pairs={{0,2},{1,3},{2,0},{3,1},{4,6},{5,7},{6,4},{7,5},{8,10},{9,11},{10,... | collective-permute-start | bytes 786440 | tf_op jit(solution)/shard_map/ppermute | solution.py:944
  51.3 21.0 %collective-permute-start.8 = (bf16[256,512]{1,0:T(8,128)(2,1)S(1)}, bf16[256,512]{1,0:T(8,128)(2,1)S(1)}, u32[]{:S(2)}, u32[]{:S(2)}) collective-permute-start(bf16[256,512]{1,0:T(8,128)(2,1)S(1)} %copy-done.68), channel_id=1, source_target_pairs={{0,3},{1,2},{2,1},{3,0},{4,7},{5,6},{6,5},{7,4},{8,11},{9,10},{10,... | collective-permute-start | bytes 786440 | tf_op jit(solution)/shard_map/ppermute | solution.py:944
  56.0 22.5 %collective-permute-start.10 = (bf16[256,512]{1,0:T(8,128)(2,1)}, bf16[256,512]{1,0:T(8,128)(2,1)S(1)}, u32[]{:S(2)}, u32[]{:S(2)}) collective-permute-start(bf16[256,512]{1,0:T(8,128)(2,1)} %get-tuple-element.142), channel_id=1, source_target_pairs={{0,2},{1,3},{2,0},{3,1},{4,6},{5,7},{6,4},{7,5},{8,10},{9,11},{10,... | collective-permute-start | bytes 786440 | tf_op jit(solution)/shard_map/ppermute | solution.py:944
  61.2 17.3 %collective-permute-start.12 = (bf16[256,512]{1,0:T(8,128)(2,1)S(1)}, bf16[256,512]{1,0:T(8,128)(2,1)S(1)}, u32[]{:S(2)}, u32[]{:S(2)}) collective-permute-start(bf16[256,512]{1,0:T(8,128)(2,1)S(1)} %copy-done.67), channel_id=1, source_target_pairs={{0,1},{1,0},{2,3},{3,2},{4,5},{5,4},{6,7},{7,6},{8,9},{9,8},{10,11... | collective-permute-start | bytes 786440 | tf_op jit(solution)/shard_map/ppermute | solution.py:944
  61.5 22.6 %collective-permute-start.13 = (bf16[256,512]{1,0:T(8,128)(2,1)S(1)}, bf16[256,512]{1,0:T(8,128)(2,1)S(1)}, u32[]{:S(2)}, u32[]{:S(2)}) collective-permute-start(bf16[256,512]{1,0:T(8,128)(2,1)S(1)} %copy-done.66), channel_id=1, source_target_pairs={{0,2},{1,3},{2,0},{3,1},{4,6},{5,7},{6,4},{7,5},{8,10},{9,11},{10,... | collective-permute-start | bytes 786440 | tf_op jit(solution)/shard_map/ppermute | solution.py:944
  67.2 21.9 %collective-permute-start.14 = (bf16[256,512]{1,0:T(8,128)(2,1)S(1)}, bf16[256,512]{1,0:T(8,128)(2,1)S(1)}, u32[]{:S(2)}, u32[]{:S(2)}) collective-permute-start(bf16[256,512]{1,0:T(8,128)(2,1)S(1)} %copy-done.65), channel_id=1, source_target_pairs={{0,3},{1,2},{2,1},{3,0},{4,7},{5,6},{6,5},{7,4},{8,11},{9,10},{10,... | collective-permute-start | bytes 786440 | tf_op jit(solution)/shard_map/ppermute | solution.py:944
  72.3 114.2 %collective-permute-start.11 = (bf16[256,512]{1,0:T(8,128)(2,1)}, bf16[256,512]{1,0:T(8,128)(2,1)S(1)}, u32[]{:S(2)}, u32[]{:S(2)}) collective-permute-start(bf16[256,512]{1,0:T(8,128)(2,1)} %get-tuple-element.143), channel_id=1, source_target_pairs={{0,3},{1,2},{2,1},{3,0},{4,7},{5,6},{6,5},{7,4},{8,11},{9,10},{10,... | collective-permute-start | bytes 786440 | tf_op jit(solution)/shard_map/ppermute | solution.py:944
  78.5 108.1 %collective-permute-start.9 = (bf16[256,512]{1,0:T(8,128)(2,1)}, bf16[256,512]{1,0:T(8,128)(2,1)S(1)}, u32[]{:S(2)}, u32[]{:S(2)}) collective-permute-start(bf16[256,512]{1,0:T(8,128)(2,1)} %get-tuple-element.141), channel_id=1, source_target_pairs={{0,1},{1,0},{2,3},{3,2},{4,5},{5,4},{6,7},{7,6},{8,9},{9,8},{10,11... | collective-permute-start | bytes 786440 | tf_op jit(solution)/shard_map/ppermute | solution.py:944
  78.5 138.9 %collective-permute-start.15 = (bf16[256,512]{1,0:T(8,128)(2,1)}, bf16[256,512]{1,0:T(8,128)(2,1)S(1)}, u32[]{:S(2)}, u32[]{:S(2)}) collective-permute-start(bf16[256,512]{1,0:T(8,128)(2,1)} %get-tuple-element.155), channel_id=1, source_target_pairs={{0,1},{1,0},{2,3},{3,2},{4,5},{5,4},{6,7},{7,6},{8,9},{9,8},{10,11... | collective-permute-start | bytes 786440 | tf_op jit(solution)/shard_map/ppermute | solution.py:944
  84.1 133.3 %collective-permute-start.16 = (bf16[256,512]{1,0:T(8,128)(2,1)}, bf16[256,512]{1,0:T(8,128)(2,1)S(1)}, u32[]{:S(2)}, u32[]{:S(2)}) collective-permute-start(bf16[256,512]{1,0:T(8,128)(2,1)} %get-tuple-element.156), channel_id=1, source_target_pairs={{0,2},{1,3},{2,0},{3,1},{4,6},{5,7},{6,4},{7,5},{8,10},{9,11},{10,... | collective-permute-start | bytes 786440 | tf_op jit(solution)/shard_map/ppermute | solution.py:944
  89.2 128.3 %collective-permute-start.17 = (bf16[256,512]{1,0:T(8,128)(2,1)}, bf16[256,512]{1,0:T(8,128)(2,1)S(1)}, u32[]{:S(2)}, u32[]{:S(2)}) collective-permute-start(bf16[256,512]{1,0:T(8,128)(2,1)} %get-tuple-element.157), channel_id=1, source_target_pairs={{0,3},{1,2},{2,1},{3,0},{4,7},{5,6},{6,5},{7,4},{8,11},{9,10},{10,... | collective-permute-start | bytes 786440 | tf_op jit(solution)/shard_map/ppermute | solution.py:944
  297.5 116.7 %reduce-scatter.21.cloned.1.call-start = ((), (), s32[]{:S(2)}) async-start(), calls=%async_computation.15 | async-start | bytes 655360 | tf_op jit(solution)/shard_map/reduce_scatter | solution.py:948
  299.8 114.5 %reduce-scatter.23.cloned.1.call-start = ((), (), s32[]{:S(2)}) async-start(), calls=%async_computation.16 | async-start | bytes 655360 | tf_op jit(solution)/shard_map/reduce_scatter | solution.py:948
  300.7 113.5 %reduce-scatter.25.cloned.1.call-start = ((), (), s32[]{:S(2)}) async-start(), calls=%async_computation.17 | async-start | bytes 655360 | tf_op jit(solution)/shard_map/reduce_scatter | solution.py:948
  301.7 122.2 %reduce-scatter.11.cloned.1.call-start = ((), (), s32[]{:S(2)}) async-start(), calls=%async_computation.10 | async-start | bytes 655360 | tf_op jit(solution)/shard_map/reduce_scatter | solution.py:948
  301.7 2.6 collective-permute-start.29
  301.8 9.4 %collective-permute-start.32 = (bf16[256,512]{1,0:T(8,128)(2,1)}, bf16[256,512]{1,0:T(8,128)(2,1)S(1)}, u32[]{:S(2)}, u32[]{:S(2)}) collective-permute-start(bf16[256,512]{1,0:T(8,128)(2,1)} %get-tuple-element.212), channel_id=1, source_target_pairs={{0,2},{1,3},{2,0},{3,1},{4,6},{5,7},{6,4},{7,5},{8,10},{9,11},{10,... | collective-permute-start | bytes 786440 | tf_op jit(solution)/shard_map/ppermute | solution.py:944
  302.2 13.7 %collective-permute-start.35 = (bf16[256,512]{1,0:T(8,128)(2,1)}, bf16[256,512]{1,0:T(8,128)(2,1)S(1)}, u32[]{:S(2)}, u32[]{:S(2)}) collective-permute-start(bf16[256,512]{1,0:T(8,128)(2,1)} %get-tuple-element.215), channel_id=1, source_target_pairs={{0,3},{1,2},{2,1},{3,0},{4,7},{5,6},{6,5},{7,4},{8,11},{9,10},{10,... | collective-permute-start | bytes 786440 | tf_op jit(solution)/shard_map/ppermute | solution.py:944
  303.7 13.6 %collective-permute-start.28 = (bf16[256,512]{1,0:T(8,128)(2,1)}, bf16[256,512]{1,0:T(8,128)(2,1)S(1)}, u32[]{:S(2)}, u32[]{:S(2)}) collective-permute-start(bf16[256,512]{1,0:T(8,128)(2,1)} %get-tuple-element.208), channel_id=1, source_target_pairs={{0,1},{1,0},{2,3},{3,2},{4,5},{5,4},{6,7},{7,6},{8,9},{9,8},{10,11... | collective-permute-start | bytes 786440 | tf_op jit(solution)/shard_map/ppermute | solution.py:944
  304.0 21.2 %collective-permute-start.31 = (bf16[256,512]{1,0:T(8,128)(2,1)S(1)}, bf16[256,512]{1,0:T(8,128)(2,1)S(1)}, u32[]{:S(2)}, u32[]{:S(2)}) collective-permute-start(bf16[256,512]{1,0:T(8,128)(2,1)S(1)} %copy-done.64), channel_id=1, source_target_pairs={{0,2},{1,3},{2,0},{3,1},{4,6},{5,7},{6,4},{7,5},{8,10},{9,11},{10,... | collective-permute-start | bytes 786440 | tf_op jit(solution)/shard_map/ppermute | solution.py:944
  304.4 25.6 %collective-permute-start.34 = (bf16[256,512]{1,0:T(8,128)(2,1)S(1)}, bf16[256,512]{1,0:T(8,128)(2,1)S(1)}, u32[]{:S(2)}, u32[]{:S(2)}) collective-permute-start(bf16[256,512]{1,0:T(8,128)(2,1)S(1)} %copy-done.63), channel_id=1, source_target_pairs={{0,3},{1,2},{2,1},{3,0},{4,7},{5,6},{6,5},{7,4},{8,11},{9,10},{10,... | collective-permute-start | bytes 786440 | tf_op jit(solution)/shard_map/ppermute | solution.py:944
  311.2 18.8 %collective-permute-start.27 = (bf16[256,512]{1,0:T(8,128)(2,1)S(1)}, bf16[256,512]{1,0:T(8,128)(2,1)S(1)}, u32[]{:S(2)}, u32[]{:S(2)}) collective-permute-start(bf16[256,512]{1,0:T(8,128)(2,1)S(1)} %copy-done.62), channel_id=1, source_target_pairs={{0,1},{1,0},{2,3},{3,2},{4,5},{5,4},{6,7},{7,6},{8,9},{9,8},{10,11... | collective-permute-start | bytes 786440 | tf_op jit(solution)/shard_map/ppermute | solution.py:944
  315.9 20.6 %collective-permute-start.30 = (bf16[256,512]{1,0:T(8,128)(2,1)S(1)}, bf16[256,512]{1,0:T(8,128)(2,1)S(1)}, u32[]{:S(2)}, u32[]{:S(2)}) collective-permute-start(bf16[256,512]{1,0:T(8,128)(2,1)S(1)} %copy-done.61), channel_id=1, source_target_pairs={{0,2},{1,3},{2,0},{3,1},{4,6},{5,7},{6,4},{7,5},{8,10},{9,11},{10,... | collective-permute-start | bytes 786440 | tf_op jit(solution)/shard_map/ppermute | solution.py:944
  317.3 23.9 %collective-permute-start.33 = (bf16[256,512]{1,0:T(8,128)(2,1)S(1)}, bf16[256,512]{1,0:T(8,128)(2,1)S(1)}, u32[]{:S(2)}, u32[]{:S(2)}) collective-permute-start(bf16[256,512]{1,0:T(8,128)(2,1)S(1)} %copy-done.60), channel_id=1, source_target_pairs={{0,3},{1,2},{2,1},{3,0},{4,7},{5,6},{6,5},{7,4},{8,11},{9,10},{10,... | collective-permute-start | bytes 786440 | tf_op jit(solution)/shard_map/ppermute | solution.py:944
  401.8 46.9 %reduce-scatter.13.cloned.1.call-start = ((), (), s32[]{:S(2)}) async-start(), calls=%async_computation.11 | async-start | bytes 655360 | tf_op jit(solution)/shard_map/reduce_scatter | solution.py:948
  403.9 69.5 %reduce-scatter.15.cloned.1.call-start = ((), (), s32[]{:S(2)}) async-start(), calls=%async_computation.12 | async-start | bytes 655360 | tf_op jit(solution)/shard_map/reduce_scatter | solution.py:948
  404.9 92.9 %reduce-scatter.17.cloned.1.call-start = ((), (), s32[]{:S(2)}) async-start(), calls=%async_computation.13 | async-start | bytes 655360 | tf_op jit(solution)/shard_map/reduce_scatter | solution.py:948
  405.8 126.5 %reduce-scatter.27.cloned.1.call-start = ((), (), s32[]{:S(2)}) async-start(), calls=%async_computation.18 | async-start | bytes 2621440 | tf_op jit(solution)/shard_map/reduce_scatter | solution.py:948
  409.8 157.1 %reduce-scatter.29.cloned.1.call-start = ((), (), s32[]{:S(2)}) async-start(), calls=%async_computation.19 | async-start | bytes 2621440 | tf_op jit(solution)/shard_map/reduce_scatter | solution.py:948
  413.8 169.8 %copy-start.51 = (f32[8,512]{1,0:T(8,128)S(1)}, f32[8,512]{1,0:T(8,128)}, u32[]{:S(2)}) copy-start(f32[8,512]{1,0:T(8,128)} %get-tuple-element.217) | copy-start | bytes 49156
  413.9 264.6 %all-reduce.15.cloned.1.call-start = ((), (), s32[]{:S(2)}) async-start(), calls=%async_computation.20 | async-start | bytes 4194304 | tf_op jit(solution)/shard_map/psum | solution.py:949
  567.0 4.6 collective-permute-start.20
  567.1 9.2 %collective-permute-start.23 = (bf16[256,512]{1,0:T(8,128)(2,1)S(1)}, bf16[256,512]{1,0:T(8,128)(2,1)S(1)}, u32[]{:S(2)}, u32[]{:S(2)}) collective-permute-start(bf16[256,512]{1,0:T(8,128)(2,1)S(1)} %copy-done.58), channel_id=1, source_target_pairs={{0,2},{1,3},{2,0},{3,1},{4,6},{5,7},{6,4},{7,5},{8,10},{9,11},{10,... | collective-permute-start | bytes 786440 | tf_op jit(solution)/shard_map/ppermute | solution.py:944
  567.4 13.5 %collective-permute-start.26 = (bf16[256,512]{1,0:T(8,128)(2,1)S(1)}, bf16[256,512]{1,0:T(8,128)(2,1)S(1)}, u32[]{:S(2)}, u32[]{:S(2)}) collective-permute-start(bf16[256,512]{1,0:T(8,128)(2,1)S(1)} %copy-done.57), channel_id=1, source_target_pairs={{0,3},{1,2},{2,1},{3,0},{4,7},{5,6},{6,5},{7,4},{8,11},{9,10},{10,... | collective-permute-start | bytes 786440 | tf_op jit(solution)/shard_map/ppermute | solution.py:944
  568.9 12.5 %collective-permute-start.19 = (bf16[256,512]{1,0:T(8,128)(2,1)S(1)}, bf16[256,512]{1,0:T(8,128)(2,1)S(1)}, u32[]{:S(2)}, u32[]{:S(2)}) collective-permute-start(bf16[256,512]{1,0:T(8,128)(2,1)S(1)} %copy-done.56), channel_id=1, source_target_pairs={{0,1},{1,0},{2,3},{3,2},{4,5},{5,4},{6,7},{7,6},{8,9},{9,8},{10,11... | collective-permute-start | bytes 786440 | tf_op jit(solution)/shard_map/ppermute | solution.py:944
  571.2 71.6 %collective-permute-start.22 = (bf16[256,512]{1,0:T(8,128)(2,1)}, bf16[256,512]{1,0:T(8,128)(2,1)S(1)}, u32[]{:S(2)}, u32[]{:S(2)}) collective-permute-start(bf16[256,512]{1,0:T(8,128)(2,1)} %get-tuple-element.168), channel_id=1, source_target_pairs={{0,2},{1,3},{2,0},{3,1},{4,6},{5,7},{6,4},{7,5},{8,10},{9,11},{10,... | collective-permute-start | bytes 786440 | tf_op jit(solution)/shard_map/ppermute | solution.py:944
  571.6 71.2 %collective-permute-start.25 = (bf16[256,512]{1,0:T(8,128)(2,1)S(1)}, bf16[256,512]{1,0:T(8,128)(2,1)S(1)}, u32[]{:S(2)}, u32[]{:S(2)}) collective-permute-start(bf16[256,512]{1,0:T(8,128)(2,1)S(1)} %copy-done.55), channel_id=1, source_target_pairs={{0,3},{1,2},{2,1},{3,0},{4,7},{5,6},{6,5},{7,4},{8,11},{9,10},{10,... | collective-permute-start | bytes 786440 | tf_op jit(solution)/shard_map/ppermute | solution.py:944
  576.2 66.6 %collective-permute-start.18 = (bf16[256,512]{1,0:T(8,128)(2,1)S(1)}, bf16[256,512]{1,0:T(8,128)(2,1)S(1)}, u32[]{:S(2)}, u32[]{:S(2)}) collective-permute-start(bf16[256,512]{1,0:T(8,128)(2,1)S(1)} %copy-done.54), channel_id=1, source_target_pairs={{0,1},{1,0},{2,3},{3,2},{4,5},{5,4},{6,7},{7,6},{8,9},{9,8},{10,11... | collective-permute-start | bytes 786440 | tf_op jit(solution)/shard_map/ppermute | solution.py:944
  580.9 61.9 %collective-permute-start.21 = (bf16[256,512]{1,0:T(8,128)(2,1)S(1)}, bf16[256,512]{1,0:T(8,128)(2,1)S(1)}, u32[]{:S(2)}, u32[]{:S(2)}) collective-permute-start(bf16[256,512]{1,0:T(8,128)(2,1)S(1)} %copy-done.53), channel_id=1, source_target_pairs={{0,2},{1,3},{2,0},{3,1},{4,6},{5,7},{6,4},{7,5},{8,10},{9,11},{10,... | collective-permute-start | bytes 786440 | tf_op jit(solution)/shard_map/ppermute | solution.py:944
  581.4 61.5 %collective-permute-start.24 = (bf16[256,512]{1,0:T(8,128)(2,1)S(1)}, bf16[256,512]{1,0:T(8,128)(2,1)S(1)}, u32[]{:S(2)}, u32[]{:S(2)}) collective-permute-start(bf16[256,512]{1,0:T(8,128)(2,1)S(1)} %copy-done.52), channel_id=1, source_target_pairs={{0,3},{1,2},{2,1},{3,0},{4,7},{5,6},{6,5},{7,4},{8,11},{9,10},{10,... | collective-permute-start | bytes 786440 | tf_op jit(solution)/shard_map/ppermute | solution.py:944
  (71 other events, 2890.5 us)
Sparse Core Ops, SparseCore 0:
  297.6 24.9 reduce-scatter.18
  325.2 21.6 reduce-scatter.20
  349.4 21.6 reduce-scatter.22
  373.5 21.6 reduce-scatter.24
  401.9 21.9 reduce-scatter.10
  427.0 21.6 reduce-scatter.12
  451.7 21.6 reduce-scatter.14
  476.1 21.6 reduce-scatter.16
  500.9 31.4 reduce-scatter.26
  535.5 31.4 reduce-scatter.28
  571.8 106.5 all-reduce.14

commit v2 on v0

--- a/solution.py
+++ b/solution.py
@@ -1,8 +1,11 @@
+import functools
 import math
 
 import jax
 import jax.numpy as jnp
 from jax import lax
+from jax.experimental import pallas as pl
+from jax.experimental.pallas import tpu as pltpu
 from jax.sharding import PartitionSpec as P
 
 HEADS = 4
@@ -402,6 +405,1093 @@
     )
 
 
+HEAD = 128
+GROUP = 16
+LOG2E = 1.4426950408889634
+F32 = jnp.float32
+BF16 = jnp.bfloat16
+SCORE = 1.0 / math.sqrt(HEAD)
+SCALE = LOG2E * SCORE
+
+
+def dot_nn(a, b):
+    return jnp.dot(a, b, preferred_element_type=F32)
+
+
+def dot_nt(a, b):
+    return lax.dot_general(a, b, (((1,), (1,)), ((), ())), preferred_element_type=F32)
+
+
+def dot_tn(a, b):
+    return lax.dot_general(a, b, (((0,), (0,)), ((), ())), preferred_element_type=F32)
+
+
+def unit_of(values):
+    centred = values - jnp.mean(values, -1, keepdims=True)
+    inverse = lax.rsqrt(jnp.mean(centred * centred, -1, keepdims=True) + EPSILON)
+    return centred * inverse, inverse
+
+
+def norm_back(upstream, unit, inverse, gain):
+    scaled = upstream * gain
+    return inverse * (
+        scaled
+        - jnp.mean(scaled, -1, keepdims=True)
+        - unit * jnp.mean(scaled * unit, -1, keepdims=True)
+    )
+
+
+def column_sum(values):
+    return jnp.sum(values, 0, keepdims=True)
+
+
+def vmem_spec():
+    return pl.BlockSpec(memory_space=pltpu.VMEM)
+
+
+def smem_spec():
+    return pl.BlockSpec(memory_space=pltpu.SMEM)
+
+
+def any_spec():
+    return pl.BlockSpec(memory_space=pl.ANY)
+
+
+def fixed(shape):
+    return pl.BlockSpec(shape, lambda *_: (0,) * len(shape))
+
+
+def shape_of(shape, dtype=BF16):
+    return jax.ShapeDtypeStruct(shape, dtype)
+
+
+def params_of(mib=63):
+    return pltpu.CompilerParams(vmem_limit_bytes=mib * 1024 * 1024)
+
+
+def call(kernel, args, waits, in_specs, **rest):
+    count = len(args)
+
+    def body(*refs):
+        kernel(*refs[:count], *refs[count + len(waits) :])
+
+    specs = [*in_specs, *[any_spec() for _ in waits]]
+    return pl.pallas_call(body, in_specs=specs, compiler_params=params_of(), **rest)(*args, *waits)
+
+
+def cost_of(microseconds):
+    return pl.CostEstimate(flops=int(microseconds * 900e6), bytes_accessed=1024, transcendentals=0)
+
+
+def head_lanes(head):
+    return slice(head * HEAD, (head + 1) * HEAD)
+
+
+def lane_of(rows):
+    return lax.broadcasted_iota(jnp.int32, (rows, HEAD), 1)
+
+
+def put_thirds(lane, first, values, base):
+    high = values.astype(BF16).astype(F32)
+    rest = values - high
+    middle = rest.astype(BF16).astype(F32)
+    turn = (lane - first) % 3
+    parts = jnp.where(turn == 0, high, jnp.where(turn == 1, middle, rest - middle))
+    return jnp.where((lane >= first) & (lane < first + 3 * HEADS), parts, base).astype(BF16)
+
+
+def own_lanes(lane, first, head):
+    return (lane >= first + 3 * head) & (lane < first + 3 * head + 3)
+
+
+def head_picker(first, width):
+    head = lax.broadcasted_iota(jnp.int32, (width, HEAD), 0) // HEAD
+    lane = lax.broadcasted_iota(jnp.int32, (width, HEAD), 1)
+    hit = (lane >= first) & (lane < first + 3 * HEADS) & ((lane - first) // 3 == head)
+    return jnp.where(hit, 1.0, 0.0).astype(BF16)
+
+
+def head_dots(left, right, picker):
+    product = left.astype(F32) * right.astype(F32)
+    high = product.astype(BF16)
+    low = (product - high.astype(F32)).astype(BF16)
+    return dot_nn(high, picker) + dot_nn(low, picker)
+
+
+def beside(left, right):
+    return jnp.concatenate([left, right], 1)
+
+
+def split_kernel(group, me_ref, whole_ref, *rest):
+    outs, sems = rest[:-1], rest[-1]
+    copies = []
+    for index, (piece, first, size) in enumerate(split_plan(group)):
+        source = whole_ref.at[pl.ds((me_ref[0] ^ piece) * group + first, size)]
+        copies.append(pltpu.make_async_copy(source, outs[index], sems.at[index]))
+        copies[-1].start()
+    for copy in copies:
+        copy.wait()
+
+
+def split_plan(group):
+    return [(0, 0, group), (1, 0, group)] + [(piece, j, 1) for j in range(group) for piece in (2, 3)]
+
+
+def split(me, whole, group, waits=()):
+    plan = split_plan(group)
+    _, rows, width = whole.shape
+    return call(
+        functools.partial(split_kernel, group),
+        (me, whole,),
+        waits,
+        in_specs=[smem_spec(), any_spec()],
+        out_specs=[vmem_spec()] * len(plan),
+        out_shape=[shape_of((size, rows, width)) for _, _, size in plan],
+        scratch_shapes=[pltpu.SemaphoreType.DMA((len(plan),))],
+        cost_estimate=cost_of(2),
+        name="split",
+    )
+
+
+def query_mask(size):
+    row = lax.broadcasted_iota(jnp.int32, (size, HEAD), 0) % GROUP
+    lane = lane_of(size)
+    return jnp.where((lane < GROUP) & (lane != row), NEGATIVE, 0.0)
+
+
+def key_mask(size, head):
+    row = lax.broadcasted_iota(jnp.int32, (size, HEAD), 0) % GROUP
+    lane = lane_of(size)
+    return jnp.where((lane == row) | own_lanes(lane, GROUP, head), 1.0, 0.0).astype(BF16)
+
+
+def gather_cells(group, me_ref, cells_ref):
+    feats, rows, _ = cells_ref.shape
+    return jnp.concatenate(
+        [
+            cells_ref[(me_ref[0] ^ (index // group)) * group + index % group, part : part + GROUP, :]
+            for part in range(0, rows, GROUP)
+            for index in range(feats)
+        ],
+        0,
+    )
+
+
+def feat_forward_kernel(
+    group, me_ref, cells_ref, gain, shift, w_query, w_key, w_value, w_out, bias, *rest
+):
+    feats, rows, width = cells_ref.shape
+    outs = rest[:feats]
+    q_ref, k_ref, v_ref, mixed_ref, extra_ref = rest[feats:]
+    size, parts = feats * GROUP, rows // GROUP
+    cells = gather_cells(group, me_ref, cells_ref)
+    unit, _ = unit_of(cells.astype(F32))
+    normed = (unit * gain[...] + shift[...]).astype(BF16)
+    q_ref[...] = dot_nn(normed, w_query[...]).astype(BF16)
+    k_ref[...] = dot_nn(normed, w_key[...]).astype(BF16)
+    v_ref[...] = dot_nn(normed, w_value[...]).astype(BF16)
+    mask = query_mask(size)
+    mask_low = mask.astype(BF16)
+    keys = [key_mask(size, head) for head in range(HEADS)]
+    lane = lane_of(size)
+    ones = jnp.ones((size, HEAD), BF16)
+    pairs = [
+        (slice(part * size, (part + 1) * size), head_lanes(head), head)
+        for part in range(parts)
+        for head in range(HEADS)
+    ]
+    scores = [
+        dot_nt(beside(q_ref[span, lanes], mask_low), beside(k_ref[span, lanes], keys[head]))
+        for span, lanes, head in pairs
+    ]
+    tops = [jnp.max(score, -1, keepdims=True) for score in scores]
+    grown = [jnp.exp2((score - top) * SCALE).astype(BF16) for score, top in zip(scores, tops)]
+    both = [dot_nn(grow, beside(v_ref[span, lanes], ones)) for (span, lanes, _), grow in zip(pairs, grown)]
+    for (span, lanes, _), found in zip(pairs, both):
+        mixed_ref[span, lanes] = (found[:, :HEAD] / found[:, HEAD:]).astype(BF16)
+    for part in range(parts):
+        top, total = jnp.zeros((size, HEAD), F32), jnp.ones((size, HEAD), F32)
+        for head in range(HEADS):
+            own = own_lanes(lane, GROUP, head)
+            top = jnp.where(own, tops[part * HEADS + head], top)
+            total = jnp.where(own, both[part * HEADS + head][:, HEAD:], total)
+        minus = -(top + jnp.log2(total) * (1.0 / SCALE))
+        extra_ref[part * size : (part + 1) * size, :] = put_thirds(lane, GROUP, minus, mask)
+    after = cells.astype(F32) + dot_nn(mixed_ref[...], w_out[...]) + bias[...]
+    after = after.astype(BF16)
+    for part in range(parts):
+        for index in range(feats):
+            start = part * size + index * GROUP
+            outs[index][part * GROUP : (part + 1) * GROUP, :] = after[start : start + GROUP]
+
+
+def feat_forward(me, cells, weights, group, block=64, waits=()):
+    feats, rows, width = cells.shape
+    tokens = block * feats
+    vector, whole = fixed((1, width)), fixed((width, width))
+    return call(
+        functools.partial(feat_forward_kernel, group),
+        (me, cells, *weights,),
+        waits,
+        grid=(rows // block,),
+        in_specs=[smem_spec(), pl.BlockSpec((feats, block, width), lambda i: (0, i, 0))]
+        + [vector, vector, whole, whole, whole, whole, vector],
+        out_specs=[pl.BlockSpec((block, width), lambda i: (i, 0))] * feats
+        + [pl.BlockSpec((tokens, width), lambda i: (i, 0))] * 4
+        + [pl.BlockSpec((tokens, HEAD), lambda i: (i, 0))],
+        out_shape=[shape_of((rows, width))] * feats
+        + [shape_of((rows * feats, width))] * 4
+        + [shape_of((rows * feats, HEAD))],
+        cost_estimate=cost_of(15),
+        name="feat_forward",
+    )
+
+
+def feat_backward_kernel(
+    group,
+    place_ref,
+    cells_ref,
+    q_ref,
+    k_ref,
+    v_ref,
+    mixed_ref,
+    extra_ref,
+    gain,
+    shift,
+    w_query,
+    w_key,
+    w_value,
+    w_out,
+    *rest,
+):
+    feats, rows, width = cells_ref.shape
+    grads, rest = rest[:feats], rest[feats:]
+    keep_ref, send_ref, d_query, d_key, d_value, sum_query, sum_key, sum_value, sum_out, vec_ref = rest
+    parts, size = rows // GROUP, feats * GROUP
+
+    @pl.when(pl.program_id(0) == 0)
+    def _():
+        for ref in (sum_query, sum_key, sum_value, sum_out, vec_ref):
+            ref[...] = jnp.zeros_like(ref)
+
+    grad_low = jnp.concatenate(
+        [ref[part * GROUP : (part + 1) * GROUP, :] for part in range(parts) for ref in grads], 0
+    )
+    sum_out[...] += dot_tn(mixed_ref[...], grad_low)
+    mixed_grad = dot_nt(grad_low, w_out[...]).astype(BF16)
+    dots = head_dots(mixed_grad, mixed_ref[...], head_picker(GROUP, width))
+    dots = put_thirds(lane_of(dots.shape[0]), GROUP, -dots, jnp.zeros((), F32))
+    keys = [key_mask(size, head) for head in range(HEADS)]
+    pairs = [
+        (slice(part * size, (part + 1) * size), head_lanes(head), head)
+        for part in range(parts)
+        for head in range(HEADS)
+    ]
+    scores = [dot_nt(beside(k_ref[s, l], keys[h]), beside(q_ref[s, l], extra_ref[s, :])) for s, l, h in pairs]
+    inners = [dot_nt(beside(v_ref[s, l], keys[h]), beside(mixed_grad[s, l], dots[s])) for s, l, h in pairs]
+    probs = [jnp.exp2(score * SCALE) for score in scores]
+    score_grads = [(prob * inner).astype(BF16) for prob, inner in zip(probs, inners)]
+    for (s, l, _), prob in zip(pairs, probs):
+        d_value[s, l] = dot_nn(prob.astype(BF16), mixed_grad[s, l]).astype(BF16)
+    for (s, l, _), score_grad in zip(pairs, score_grads):
+        d_key[s, l] = (dot_nn(score_grad, q_ref[s, l]) * SCORE).astype(BF16)
+    for (s, l, _), score_grad in zip(pairs, score_grads):
+        d_query[s, l] = (dot_tn(score_grad, k_ref[s, l]) * SCORE).astype(BF16)
+    unit, _ = unit_of(gather_cells(group, place_ref, cells_ref).astype(F32))
+    normed_t = (unit * gain[...] + shift[...]).astype(BF16).T
+    sum_query[...] += dot_nn(normed_t, d_query[...])
+    sum_key[...] += dot_nn(normed_t, d_key[...])
+    sum_value[...] += dot_nn(normed_t, d_value[...])
+    vec_ref[2:3, :] += column_sum(d_query[...].astype(F32))
+    vec_ref[3:4, :] += column_sum(d_key[...].astype(F32))
+    vec_ref[4:5, :] += column_sum(d_value[...].astype(F32))
+
+    @pl.when(pl.program_id(0) == pl.num_programs(0) - 1)
+    def _():
+        ones = jnp.ones((8, width), BF16)
+        crossed, plain = jnp.zeros((8, width), F32), jnp.zeros((8, width), F32)
+        for index, (weight, total) in enumerate(
+            ((w_query, sum_query), (w_key, sum_key), (w_value, sum_value))
+        ):
+            product = weight[...].astype(F32) * total[...]
+            column = jnp.broadcast_to(vec_ref[2 + index : 3 + index, :], (8, width))
+            for _ in range(3):
+                crossed = crossed + dot_nt(ones, product.astype(BF16))
+                product = product - product.astype(BF16).astype(F32)
+                plain = plain + dot_nt(column.astype(BF16), weight[...])
+                column = column - column.astype(BF16).astype(F32)
+        vec_ref[0:1, :] = (crossed[:1] - shift[...] * plain[:1]) / gain[...]
+        vec_ref[1:2, :] = plain[:1]
+
+        def fill(out, place, quarter, piece):
+            start = pl.multiple_of(quarter * HEAD + piece * GROUP, GROUP)
+            for index, ref in enumerate((sum_query, sum_key, sum_value, sum_out)):
+                out[place, index * GROUP : (index + 1) * GROUP, :] = ref[pl.ds(start, GROUP), :].astype(BF16)
+            out[place, 4 * GROUP : 5 * GROUP, :] = padded_vec(vec_ref)
+
+        fill_batch(place_ref, keep_ref, send_ref, fill, x_first)
+
+
+def feat_backward(place, cells, kept, grads, weights, group, block=64, waits=()):
+    feats, rows, width = cells.shape
+    tokens = block * feats
+    vector, whole = fixed((1, width)), fixed((width, width))
+    batch = (BATCH, 5 * GROUP, width)
+    row_block = pl.BlockSpec((tokens, width), lambda i: (i, 0))
+    return call(
+        functools.partial(feat_backward_kernel, group),
+        (place, cells, *kept, *weights, *grads,),
+        waits,
+        grid=(rows // block,),
+        in_specs=[smem_spec(), pl.BlockSpec((feats, block, width), lambda i: (0, i, 0))]
+        + [row_block] * 4
+        + [pl.BlockSpec((tokens, HEAD), lambda i: (i, 0))]
+        + [vector, vector, whole, whole, whole, whole]
+        + [pl.BlockSpec((block, width), lambda i: (i, 0))] * feats,
+        out_specs=[fixed(batch)] * 2 + [row_block] * 3,
+        out_shape=[shape_of(batch)] * 2 + [shape_of((rows * feats, width))] * 3,
+        scratch_shapes=[pltpu.VMEM((width, width), F32)] * 4 + [pltpu.VMEM((8, width), F32)],
+        cost_estimate=cost_of(20),
+        name="feat_backward",
+    )
+
+
+def cells_backward_kernel(group, me_ref, cells_ref, d_query, d_key, d_value, gain, w_query, w_key, w_value, *rest):
+    grads, (out_ref, mark_ref) = rest[:-2], rest[-2:]
+    feats, rows, _ = cells_ref.shape
+    mark_ref[...] = jnp.zeros_like(mark_ref)
+    parts, size = rows // GROUP, feats * GROUP
+    unit, inverse = unit_of(gather_cells(group, me_ref, cells_ref).astype(F32))
+    upstream = (
+        dot_nt(d_query[...], w_query[...])
+        + dot_nt(d_key[...], w_key[...])
+        + dot_nt(d_value[...], w_value[...])
+    )
+    back = norm_back(upstream, unit, inverse, gain[...])
+    for index in range(feats):
+        true = (me_ref[0] ^ (index // group)) * group + index % group
+        for part in range(parts):
+            start = part * size + index * GROUP
+            span = slice(part * GROUP, (part + 1) * GROUP)
+            cells = grads[index][span, :].astype(F32) + back[start : start + GROUP]
+            out_ref[true, span, :] = cells.astype(BF16)
+
+
+def cells_backward(me, cells, d_all, weights, grads, group, block=64, waits=()):
+    feats, rows, width = cells.shape
+    tokens = block * feats
+    vector, whole = fixed((1, width)), fixed((width, width))
+    row_block = pl.BlockSpec((tokens, width), lambda i: (i, 0))
+    by_rows = pl.BlockSpec((feats, block, width), lambda i: (0, i, 0))
+    return call(
+        functools.partial(cells_backward_kernel, group),
+        (me, cells, *d_all, *weights, *grads,),
+        waits,
+        grid=(rows // block,),
+        in_specs=[smem_spec(), by_rows]
+        + [row_block] * 3
+        + [vector, whole, whole, whole]
+        + [pl.BlockSpec((block, width), lambda i: (i, 0))] * feats,
+        out_specs=[by_rows, fixed((8, HEAD))],
+        out_shape=[shape_of((feats, rows, width)), shape_of((8, HEAD), F32)],
+        cost_estimate=cost_of(12),
+        name="cells_backward",
+    )
+
+
+def key_extra(info_ref, piece, rows, head):
+    first = (info_ref[0] ^ piece) * rows
+    row = lax.broadcasted_iota(jnp.int32, (rows, HEAD), 0) + first
+    lane = lane_of(rows)
+    bias = jnp.where(row < info_ref[2], 0.0, NEGATIVE)
+    return jnp.where(lane == 0, bias, jnp.where(own_lanes(lane, 1, head), 1.0, 0.0)).astype(BF16)
+
+
+def row_backward_kernel(pieces, info_ref, *rest):
+    q_ref, k_ref, v_ref, extra_ref, mixed_grad_ref, dots_ref, rest = *rest[:6], rest[6:]
+    afters, rest = rest[:pieces], rest[pieces:]
+    grad_hbm, gain, w_query_hbm, w_key_hbm, w_value_hbm = rest[:5]
+    outs, rest = rest[5 : 5 + pieces], rest[5 + pieces :]
+    d_query, d_key, d_value, vec_ref = rest[:4]
+    after, grad, w_query, w_key, w_value, query_all, key_all, value_all, query_sum, sems = rest[4:]
+    rows, width = outs[0].shape
+    full = rows * pieces
+    head = pl.program_id(0)
+    copies = [
+        pltpu.make_async_copy(afters[piece], after.at[pl.ds(piece * rows, rows), :], sems.at[piece])
+        for piece in range(pieces)
+    ]
+    copies.append(pltpu.make_async_copy(grad_hbm, grad, sems.at[pieces]))
+    for index, (source, target) in enumerate(
+        ((w_query_hbm, w_query), (w_key_hbm, w_key), (w_value_hbm, w_value))
+    ):
+        copies.append(pltpu.make_async_copy(source, target, sems.at[pieces + 1 + index]))
+
+    @pl.when(head == 0)
+    def _():
+        for copy in copies:
+            copy.start()
+
+    query = beside(q_ref[...], extra_ref[...])
+    upstream = beside(mixed_grad_ref[...], dots_ref[...])
+    spans = [slice(index * rows, (index + 1) * rows) for index in range(pieces)]
+    keys = [key_extra(info_ref, index, rows, head) for index in range(pieces)]
+    scores = [dot_nt(beside(k_ref[span, :], extra), query) for span, extra in zip(spans, keys)]
+    inners = [dot_nt(beside(v_ref[span, :], extra), upstream) for span, extra in zip(spans, keys)]
+    probs = [jnp.exp2(score * SCALE) for score in scores]
+    score_grads = [(prob * inner).astype(BF16) for prob, inner in zip(probs, inners)]
+    for span, prob in zip(spans, probs):
+        value_all[head, span, :] = dot_nn(prob.astype(BF16), mixed_grad_ref[...]).astype(BF16)
+    for span, score_grad in zip(spans, score_grads):
+        key_all[head, span, :] = (dot_nn(score_grad, q_ref[...]) * SCORE).astype(BF16)
+    query_sum[...] = dot_tn(jnp.concatenate(score_grads, 0), k_ref[...])
+    query_all[head] = (query_sum[...] * SCORE).astype(BF16)
+
+    @pl.when(head == HEADS - 1)
+    def _():
+        for copy in copies:
+            copy.wait()
+        vec_ref[...] = jnp.zeros_like(vec_ref)
+        for piece in range(pieces):
+            span = slice(piece * rows, (piece + 1) * rows)
+            unit, inverse = unit_of(after[span, :].astype(F32))
+            upstream = None
+            for ref, weight, out in (
+                (query_all, w_query, d_query),
+                (key_all, w_key, d_key),
+                (value_all, w_value, d_value),
+            ):
+                flat = jnp.concatenate([ref[index, span, :] for index in range(HEADS)], 1)
+                out[span, :] = flat
+                part = dot_nt(flat, weight[...])
+                upstream = part if upstream is None else upstream + part
+            grad_a = grad[span, :] + norm_back(upstream, unit, inverse, gain[...])
+            outs[piece][...] = grad_a.astype(BF16)
+            vec_ref[0:1, :] += column_sum(upstream * unit)
+            vec_ref[1:2, :] += column_sum(upstream)
+            vec_ref[2:3, :] += column_sum(grad_a)
+
+
+def row_backward(info, kept, back, afters, weights, waits=()):
+    rows, width = afters[0].shape
+    count = len(afters)
+    full = rows * count
+    query, key, value, extra = kept
+    mixed_grad, grad_b, dots = back
+    by_head = pl.BlockSpec((full, HEAD), lambda h: (0, h))
+    return call(
+        functools.partial(row_backward_kernel, count),
+        (info, query, key, value, extra, mixed_grad, dots, *afters, grad_b, *weights,),
+        waits,
+        grid=(HEADS,),
+        in_specs=[smem_spec()]
+        + [by_head] * 3
+        + [fixed((full, HEAD)), by_head, fixed((full, HEAD))]
+        + [any_spec()] * (count + 1)
+        + [fixed((1, width))]
+        + [any_spec()] * 3,
+        out_specs=[fixed((rows, width))] * count + [fixed((full, width))] * 3 + [fixed((8, width))],
+        out_shape=[shape_of((rows, width))] * count + [shape_of((full, width))] * 3 + [shape_of((8, width), F32)],
+        scratch_shapes=[
+            pltpu.VMEM((full, width), BF16),
+            pltpu.VMEM((full, width), F32),
+            pltpu.VMEM((width, width), BF16),
+            pltpu.VMEM((width, width), BF16),
+            pltpu.VMEM((width, width), BF16),
+            pltpu.VMEM((HEADS, full, HEAD), BF16),
+            pltpu.VMEM((HEADS, full, HEAD), BF16),
+            pltpu.VMEM((HEADS, full, HEAD), BF16),
+            pltpu.VMEM((full, HEAD), F32),
+            pltpu.SemaphoreType.DMA((count + 4,)),
+        ],
+        cost_estimate=cost_of(15),
+        name="row_backward",
+    )
+
+
+def row_weights_kernel(group, place_ref, *rest):
+    normeds, rest = rest[:group], rest[group:]
+    grads, rest = rest[: 3 * group], rest[3 * group :]
+    vecs, rest = rest[:group], rest[group:]
+    keep_ref, send_ref, normed, grad, totals, sems = rest
+    copies = []
+    for j in range(group):
+        mine = [pltpu.make_async_copy(normeds[j], normed.at[j], sems.at[4 * j])]
+        for index in range(3):
+            mine.append(pltpu.make_async_copy(grads[3 * j + index], grad.at[j, index], sems.at[4 * j + 1 + index]))
+        for copy in mine:
+            copy.start()
+        copies.append(mine)
+    for j in range(group):
+        for copy in copies[j]:
+            copy.wait()
+        turned = normed[j].T
+        for index in range(3):
+            part = dot_nn(turned, grad[j, index])
+            if j == 0:
+                totals[index] = part
+            else:
+                totals[index] += part
+    vec = sum((ref[...] for ref in vecs[1:]), vecs[0][...])
+
+    def fill(out, place, quarter, piece):
+        start = pl.multiple_of(quarter * HEAD + piece * GROUP, GROUP)
+        for index in range(3):
+            out[place, index * GROUP : (index + 1) * GROUP, :] = totals[index, pl.ds(start, GROUP), :].astype(BF16)
+        out[place, 3 * GROUP : 4 * GROUP, :] = padded_vec(vec)
+
+    fill_batch(place_ref, keep_ref, send_ref, fill, x_first)
+
+
+def row_weights(place, normeds, grads, vecs, waits=()):
+    group = len(normeds)
+    full, width = normeds[0].shape
+    batch = (BATCH, 4 * GROUP, width)
+    return call(
+        functools.partial(row_weights_kernel, group),
+        (place, *normeds, *grads, *vecs,),
+        waits,
+        in_specs=[smem_spec()] + [any_spec()] * (4 * group) + [vmem_spec()] * group,
+        out_specs=[vmem_spec()] * 2,
+        out_shape=[shape_of(batch)] * 2,
+        scratch_shapes=[
+            pltpu.VMEM((group, full, width), BF16),
+            pltpu.VMEM((group, 3, full, width), BF16),
+            pltpu.VMEM((3, width, width), F32),
+            pltpu.SemaphoreType.DMA((4 * group,)),
+        ],
+        cost_estimate=cost_of(8),
+        name="row_weights",
+    )
+
+
+CHUNK = 512
+UP_ROWS, DOWN_ROWS = GROUP * 4, 4 * GROUP
+
+
+def units_of(parts):
+    centred = [part - jnp.mean(part, -1, keepdims=True) for part in parts]
+    inverses = [lax.rsqrt(jnp.mean(part * part, -1, keepdims=True) + EPSILON) for part in centred]
+    return [part * inverse for part, inverse in zip(centred, inverses)], inverses
+
+
+def norms_back(upstreams, units, inverses, gain):
+    scaled = [upstream * gain for upstream in upstreams]
+    means = [jnp.mean(part, -1, keepdims=True) for part in scaled]
+    along = [jnp.mean(part * unit, -1, keepdims=True) for part, unit in zip(scaled, units)]
+    return [
+        inverse * (part - mean - unit * cross)
+        for part, mean, cross, unit, inverse in zip(scaled, means, along, units, inverses)
+    ]
+
+
+def row_and_mlp_kernel(pieces, first, last, with_old, cot_at, info_ref, place_ref, *rest):
+    afters, cots, rest = rest[:pieces], rest[pieces : 2 * pieces], rest[2 * pieces :]
+    row_gain, row_shift, w_query_hbm, w_key_hbm, w_value_hbm = rest[:5]
+    rest = rest[5:]
+    w_row_hbm, row_bias, gain, shift, w_up_hbm, up_bias, w_down_hbm, down_bias = rest[:8]
+    rest = rest[8:]
+    if not first:
+        (old_up, old_down, old_row, old_vec), rest = rest[:4], rest[4:]
+    if with_old:
+        old_layers, rest = rest[: pieces - 1], rest[pieces - 1 :]
+    kept, rest = rest[:5], rest[5:]
+    outs, (mixed_grad_ref, grad_ref, dots_ref), rest = rest[:pieces], rest[pieces : pieces + 3], rest[pieces + 3 :]
+    if last:
+        (keep_ref, send_ref), rest = rest[:2], rest[2:]
+    else:
+        (new_up, new_down, new_row, vec_ref), rest = rest[:4], rest[4:]
+    q_ref, k_ref, v_ref, extra_ref, normed_ref, w_query, w_key, w_value = rest[:8]
+    rest = rest[8:]
+    after, cot, mixed, w_row, w_up, w_down, active_all, hidden_grad_all, up_sum, down_sum, row_sum, sems = rest[:12]
+    if last:
+        vec_ref = rest[12]
+    _, rows, width = outs[0].shape
+    full = rows * pieces
+    wide = w_up.shape[1]
+    spans = [slice(piece * rows, (piece + 1) * rows) for piece in range(pieces)]
+    count = iter(range(32))
+
+    def start(source, target):
+        copy = pltpu.make_async_copy(source, target, sems.at[next(count)])
+        copy.start()
+        return copy
+
+    get_after = [start(ref, after.at[pl.ds(piece * rows, rows), :]) for piece, ref in enumerate(afters)]
+    get_row = [start(w_query_hbm, w_query), start(w_key_hbm, w_key), start(w_value_hbm, w_value)]
+    get_out = [start(w_row_hbm, w_row)]
+    get_up = [start(w_up_hbm, w_up)]
+    get_down = [
+        start(ref.at[cot_at[piece]], cot.at[pl.ds(piece * rows, rows), :]) for piece, ref in enumerate(cots)
+    ]
+    get_down.append(start(w_down_hbm, w_down))
+    get_old = [] if first else [start(old_down, down_sum), start(old_up, up_sum), start(old_row, row_sum)]
+
+    for copy in get_after:
+        copy.wait()
+    units, _ = units_of([after[span, :].astype(F32) for span in spans])
+    normed = [(unit * row_gain[...] + row_shift[...]).astype(BF16) for unit in units]
+    for copy in get_row:
+        copy.wait()
+    for weight, ref in ((w_query, q_ref), (w_key, k_ref), (w_value, v_ref)):
+        for span, part in zip(spans, normed):
+            ref[span, :] = dot_nn(part, weight[...]).astype(BF16)
+    for span, part in zip(spans, normed):
+        normed_ref[span, :] = part
+    puts = [start(source, target) for source, target in zip((q_ref, k_ref, v_ref, normed_ref), kept)]
+    lane = lane_of(rows)
+    one_lane = jnp.where(lane == 0, 1.0, 0.0)
+    query_low = one_lane.astype(BF16)
+    biases = jnp.concatenate([key_extra(info_ref, piece, rows, 0) for piece in range(pieces)], 0)
+    ones = jnp.ones((full, HEAD), BF16)
+    tops = [jnp.zeros((rows, HEAD), F32) for _ in spans]
+    totals = [jnp.ones((rows, HEAD), F32) for _ in spans]
+    for head in range(HEADS):
+        lanes = head_lanes(head)
+        own = own_lanes(lane, 1, head)
+        key, value = beside(k_ref[:, lanes], biases), beside(v_ref[:, lanes], ones)
+        scores = [dot_nt(beside(q_ref[span, lanes], query_low), key) for span in spans]
+        highest = [jnp.max(score, -1, keepdims=True) for score in scores]
+        grown = [jnp.exp2((score - top) * SCALE).astype(BF16) for score, top in zip(scores, highest)]
+        both = [dot_nn(grow, value) for grow in grown]
+        for span, found in zip(spans, both):
+            mixed[span, lanes] = (found[:, :HEAD] / found[:, HEAD:]).astype(BF16)
+        tops = [jnp.where(own, top, old) for top, old in zip(highest, tops)]
+        totals = [jnp.where(own, found[:, HEAD:], old) for found, old in zip(both, totals)]
+    for span, top, total in zip(spans, tops, totals):
+        extra_ref[span, :] = put_thirds(lane, 1, -(top + jnp.log2(total) * (1.0 / SCALE)), one_lane)
+    puts.append(start(extra_ref, kept[4]))
+    for copy in get_out:
+        copy.wait()
+    after_b = [
+        after[span, :].astype(F32) + dot_nn(mixed[span, :], w_row[...]) + row_bias[...] for span in spans
+    ]
+    units, inverses = units_of(after_b)
+    normed = [(unit * gain[...] + shift[...]).astype(BF16) for unit in units]
+    normed_t = jnp.concatenate([part.T for part in normed], 1)
+    for copy in get_up + get_down:
+        copy.wait()
+    keeps = [
+        lax.broadcasted_iota(jnp.int32, (rows, 1), 0) + (info_ref[0] ^ piece) * rows < info_ref[1]
+        for piece in range(pieces)
+    ]
+    grad_c = [jnp.where(keep, cot[span, :], jnp.zeros((), BF16)) for keep, span in zip(keeps, spans)]
+    grad_t = jnp.concatenate([part.T for part in grad_c], 1)
+    ones = jnp.ones((8, full), BF16)
+    parts = [slice(at, at + CHUNK) for at in range(0, wide, CHUNK)]
+
+    def widen(lanes):
+        hiddens = [dot_nn(part, w_up[:, lanes]) + up_bias[:, lanes] for part in normed]
+        return hiddens, [dot_nt(part, w_down[lanes, :]) for part in grad_c]
+
+    c_one, c_three = math.sqrt(2.0 / math.pi), math.sqrt(2.0 / math.pi) * 0.044715
+    ahead = widen(parts[0])
+    bias_sums = []
+    for index, lanes in enumerate(parts):
+        hiddens, active_grads = ahead
+        if index + 1 < len(parts):
+            ahead = widen(parts[index + 1])
+        for span, hidden, active_grad in zip(spans, hiddens, active_grads):
+            square = hidden * hidden
+            half = 0.5 + 0.5 * jnp.tanh(hidden * (c_one + c_three * square))
+            active = hidden * half
+            slope = half + active * (1.0 - half) * (2.0 * c_one + 6.0 * c_three * square)
+            active_all[span, lanes] = active.astype(BF16)
+            hidden_grad_all[span, lanes] = (active_grad * slope).astype(BF16)
+        if index == 0:
+            for copy in get_old:
+                copy.wait()
+        to_down = dot_nn(grad_t, active_all[:, lanes])
+        to_up = dot_nn(normed_t, hidden_grad_all[:, lanes])
+        down_sum[:, lanes] = to_down if first else down_sum[:, lanes] + to_down
+        up_sum[:, lanes] = to_up if first else up_sum[:, lanes] + to_up
+        bias_sums.append(dot_nn(ones, hidden_grad_all[:, lanes])[:1])
+    if not last:
+        puts += [start(down_sum, new_down), start(up_sum, new_up)]
+    upstreams = [dot_nt(hidden_grad_all[span, :], w_up[...]) for span in spans]
+    totals = [dot_nn(active_all[span, :], w_down[...]) for span in spans]
+    backs = norms_back(upstreams, units, inverses, gain[...])
+    grad_b = [part.astype(F32) + back for part, back in zip(grad_c, backs)]
+    grad_low = [part.astype(BF16) for part in grad_b]
+    if with_old:
+        for out, ref in zip(outs[1:], old_layers):
+            out[0] = ref[0]
+    for out, total, base, keep in zip(outs, totals, after_b, keeps):
+        out[out.shape[0] - 1] = jnp.where(keep, total + base + down_bias[...], 0.0).astype(BF16)
+    mixed_grads = [dot_nt(part, w_row[...]).astype(BF16) for part in grad_low]
+    to_row = dot_tn(mixed[...], jnp.concatenate(grad_low, 0))
+    row_sum[...] = to_row if first else row_sum[...] + to_row
+    if not last:
+        puts.append(start(row_sum, new_row))
+    picker = head_picker(1, width)
+    for span, part, mixed_grad in zip(spans, grad_b, mixed_grads):
+        grad_ref[span, :] = part
+        mixed_grad_ref[span, :] = mixed_grad
+    dots = [head_dots(part, mixed[span, :], picker) for part, span in zip(mixed_grads, spans)]
+    for span, dot in zip(spans, dots):
+        dots_ref[span, :] = put_thirds(lane, 1, -dot, jnp.zeros((), F32))
+    sums = bias_sums + [
+        dot_nn(ones, jnp.concatenate(grad_c, 0))[:1],
+        sum(column_sum(upstream * unit) for upstream, unit in zip(upstreams, units)),
+        sum(column_sum(upstream) for upstream in upstreams),
+        sum(column_sum(part) for part in grad_b),
+    ]
+    sums = jnp.concatenate(sums, 0)
+    vec_ref[...] = sums if first else old_vec[...] + sums
+    if last:
+
+        def fill(out, place, quarter, tab):
+            start_row = pl.multiple_of(quarter * HEAD + tab * GROUP, GROUP)
+            for index, lanes in enumerate(parts):
+                out[place, index * GROUP : (index + 1) * GROUP, :] = up_sum[
+                    pl.ds(start_row, GROUP), lanes
+                ].astype(BF16)
+            rows_of = pl.ds(pl.multiple_of(tab * DOWN_ROWS, GROUP), DOWN_ROWS)
+            lanes = pl.ds(pl.multiple_of(quarter * CHUNK, CHUNK), CHUNK)
+            out[place, UP_ROWS : UP_ROWS + DOWN_ROWS, :] = down_sum[rows_of, lanes].astype(BF16)
+            at = UP_ROWS + DOWN_ROWS
+            out[place, at : at + GROUP, :] = row_sum[pl.ds(start_row, GROUP), :].astype(BF16)
+            out[place, at + GROUP : at + 2 * GROUP, :] = padded_vec(vec_ref)
+
+        fill_batch(place_ref, keep_ref, send_ref, fill, y_first)
+    for copy in puts:
+        copy.wait()
+
+
+def row_and_mlp(info, place, afters, cots, cot_at, row_weights, weights, last, old, old_layers, waits=()):
+    rows, width = afters[0].shape
+    pieces = len(afters)
+    full = rows * pieces
+    wide = weights[4].shape[1]
+    first = old is None
+    batch = (BATCH, UP_ROWS + DOWN_ROWS + 2 * GROUP, width)
+    sums = [shape_of((width, wide), F32)] * 2 + [shape_of((width, width), F32), shape_of((8, width), F32)]
+    weights = (*row_weights, *weights)
+    weight_specs = [any_spec() if weight.shape[0] > 1 else vmem_spec() for weight in weights]
+    return call(
+        functools.partial(row_and_mlp_kernel, pieces, first, last, bool(old_layers), cot_at),
+        (info, place, *afters, *cots, *weights, *([] if first else old), *old_layers,),
+        waits,
+        in_specs=[smem_spec()] * 2
+        + [any_spec()] * (2 * pieces)
+        + weight_specs
+        + ([] if first else [any_spec()] * 3 + [vmem_spec()])
+        + [vmem_spec()] * len(old_layers),
+        out_specs=[any_spec()] * 5
+        + [vmem_spec()] * (pieces + 3)
+        + ([vmem_spec()] * 2 if last else [any_spec()] * 3 + [vmem_spec()]),
+        out_shape=[shape_of((full, width))] * 4
+        + [shape_of((full, HEAD))]
+        + [shape_of((1 + (k > 0 and bool(old_layers)), rows, width)) for k in range(pieces)]
+        + [shape_of((full, width)), shape_of((full, width), F32), shape_of((full, HEAD))]
+        + ([shape_of(batch)] * 2 if last else sums),
+        scratch_shapes=[pltpu.VMEM((full, width), BF16)] * 3
+        + [pltpu.VMEM((full, HEAD), BF16), pltpu.VMEM((full, width), BF16)]
+        + [pltpu.VMEM((width, width), BF16)] * 3
+        + [
+            pltpu.VMEM((full, width), BF16),
+            pltpu.VMEM((full, width), BF16),
+            pltpu.VMEM((full, width), BF16),
+            pltpu.VMEM((width, width), BF16),
+            pltpu.VMEM((width, wide), BF16),
+            pltpu.VMEM((wide, width), BF16),
+            pltpu.VMEM((full, wide), BF16),
+            pltpu.VMEM((full, wide), BF16),
+            pltpu.VMEM((width, wide), F32),
+            pltpu.VMEM((width, wide), F32),
+            pltpu.VMEM((width, width), F32),
+            pltpu.SemaphoreType.DMA((32,)),
+        ]
+        + ([pltpu.VMEM((8, width), F32)] if last else []),
+        cost_estimate=cost_of(28),
+        name="row_and_mlp",
+    )
+
+
+BATCH = 16
+
+
+def padded_vec(vec_ref):
+    values = vec_ref[...]
+    return jnp.concatenate([values, jnp.zeros_like(values)], 0).astype(BF16)
+
+
+def y_first(x, y, z):
+    return (y * 4 + z) * 2 + x
+
+
+def x_first(x, y, z):
+    return (x * 2 + y) * 4 + z
+
+
+def fill_batch(place_ref, keep_ref, send_ref, fill, order):
+    for core, out in ((0, keep_ref), (1, send_ref)):
+        for y in range(2):
+            for z in range(4):
+                for x in range(2):
+                    fill(out, order(x, y, z), place_ref[0] ^ (core + 2 * x), place_ref[1] ^ (y + 2 * z))
+
+
+def row_swap(values, step):
+    if step == 0:
+        return values
+    return lax.ppermute(values, "row", [(index, index ^ step) for index in range(4)])
+
+
+def tab_swap(values, step):
+    return lax.ppermute(values, "tab", [(index, index ^ step) for index in range(8)])
+
+
+def add(*parts):
+    total = parts[0].astype(F32)
+    for part in parts[1:]:
+        total = total + part.astype(F32)
+    return total.astype(BF16)
+
+
+def gather_near(own):
+    return [own] + [tab_swap(own, 2 * z) for z in range(1, 4)]
+
+
+def tie(first, second):
+    return lax.optimization_barrier((first, second))
+
+
+def finish_kernel(sizes, place_ref, near_ref, far_ref, *outs):
+    at = 0
+    for (rows, columns, turned), out in zip(sizes, outs):
+        parts = columns // 512
+        for y, ref in ((0, near_ref), (1, far_ref)):
+            for z in range(4):
+                tab = place_ref[1] ^ (y + 2 * z)
+                for part in range(parts):
+                    block = ref[z, at + part * rows : at + (part + 1) * rows, :].astype(F32)
+                    span = pl.ds(pl.multiple_of(tab * rows, GROUP), rows)
+                    out[span, part * 512 : (part + 1) * 512] = block
+        at += rows * parts
+
+
+def finish(place, near, far, sizes, waits=()):
+    return call(
+        functools.partial(finish_kernel, sizes),
+        (place, near, far,),
+        waits,
+        in_specs=[smem_spec(), vmem_spec(), vmem_spec()],
+        out_specs=[vmem_spec()] * len(sizes),
+        out_shape=[shape_of((rows * 8, columns), F32) for rows, columns, _ in sizes],
+        cost_estimate=cost_of(2),
+        name="finish",
+    )
+
+
+def join_pieces_kernel(group, starts, me_ref, *rest):
+    ins, out_ref = rest[:-1], rest[-1]
+    for (piece, start), ref in zip(starts, ins):
+        out_ref[pl.ds((me_ref[0] ^ piece) * group + start, ref.shape[0])] = ref[...]
+
+
+def join_pieces(me, blocks, group, waits=()):
+    _, rows, width = blocks[0][2].shape
+    starts = tuple(block[:2] for block in blocks)
+    return call(
+        functools.partial(join_pieces_kernel, group, starts),
+        (me, *(block[2] for block in blocks)),
+        waits,
+        in_specs=[smem_spec()] + [vmem_spec()] * len(blocks),
+        out_specs=vmem_spec(),
+        out_shape=shape_of((4 * group, rows, width)),
+        cost_estimate=cost_of(2),
+        name="join_pieces",
+    )
+
+
+def by_feature(
+    table_cells,
+    cotangent,
+    row_counts,
+    context_counts,
+    feat_gain,
+    feat_shift,
+    feat_query,
+    feat_key,
+    feat_value,
+    feat_out,
+    feat_bias,
+    row_gain,
+    row_shift,
+    row_query,
+    row_key,
+    row_value,
+    row_out,
+    row_bias,
+    mlp_gain,
+    mlp_shift,
+    up_weight,
+    up_bias,
+    down_weight,
+    down_bias,
+):
+    count = lax.axis_size("row")
+    feats = table_cells.shape[2]
+    group = feats // count
+    me = lax.axis_index("row").astype(jnp.int32)
+    own = me.reshape(1)
+    place = jnp.stack([me, lax.axis_index("tab").astype(jnp.int32)])
+    info = jnp.stack([me, row_counts[0], context_counts[0]])
+
+    def flat(vector):
+        return vector.reshape(1, -1)
+
+    cells = table_cells[0].transpose(1, 0, 2)
+    upstream = cotangent[0].transpose(1, 0, 2)
+    feat_weights = (flat(feat_gain), flat(feat_shift), feat_query, feat_key, feat_value, feat_out)
+    row_weight = (row_query, row_key, row_value)
+    mlp_weights = (
+        row_out,
+        flat(row_bias),
+        flat(mlp_gain),
+        flat(mlp_shift),
+        up_weight,
+        flat(up_bias),
+        down_weight,
+        flat(down_bias),
+    )
+    cot_own, cot_near, *cot_far = split(own, upstream, group)
+    cot_near = row_swap(cot_near, 1)
+    cot_first = [row_swap(cot_far[0], 2), row_swap(cot_far[1], 3)]
+    forward = feat_forward(own, cells, (*feat_weights, flat(feat_bias)), group)
+    after_out, kept_a = list(forward[:feats]), forward[feats:]
+    leaving = [after_out[k * group] for k in range(1, count)]
+    leaving, (cot_near, cot_first) = tie(leaving, (cot_near, cot_first))
+    after_out[group :: group] = leaving
+    afters, own_layers, kept_b, backs, mlp_sums, old_layers, late = [], [], [], [], None, [], []
+    for j in range(group):
+        afters.append([row_swap(after_out[k * group + j], k) for k in range(count)])
+        cot = cot_first if j == 0 else [row_swap(cot_far[2 * j], 2), row_swap(cot_far[2 * j + 1], 3)]
+        found = row_and_mlp(
+            info,
+            place,
+            afters[j],
+            [cot_own, cot_near, *cot],
+            (j, j, 0, 0),
+            (flat(row_gain), flat(row_shift), *row_weight),
+            mlp_weights,
+            j == group - 1,
+            mlp_sums,
+            old_layers,
+        )
+        kept_b.append(found[:5])
+        layer = found[5 : 5 + count]
+        own_layers.append(layer[0])
+        old_layers = layer[1:] if j == 0 else []
+        if j > 0:
+            early, late = late, [row_swap(layer[k], k) for k in range(1, count)]
+        backs.append(found[5 + count : 8 + count])
+        mlp_sums = found[8 + count :]
+    mlp_keep, send = mlp_sums
+    send, early = tie(send, early)
+    mlp_came = row_swap(send, 1)
+    mlp_line = tab_swap(add(mlp_keep[8:], mlp_came[8:]), 1)
+    grads, d_rows, vecs = [], [], []
+    for j in range(group):
+        query, key, value, _, extra = kept_b[j]
+        if j == 0:
+            waits = [backs[-1][2]]
+        elif j == 1:
+            waits = [vecs[-1], *late]
+        else:
+            parts = [
+                add(*(ref[2 * z : 2 * z + 2] for ref in (mlp_keep, mlp_came, mlp_line))) for z in range(4)
+            ]
+            waits = [vecs[-1], *grads[0][2:], parts[0]]
+        found = row_backward(
+            info, (query, key, value, extra), backs[j], afters[j], (flat(row_gain), *row_weight), waits
+        )
+        d_rows += found[count : count + 3]
+        vecs.append(found[count + 3])
+        grads.append([row_swap(found[k], k) for k in range(count)])
+    parts[1:] = [tab_swap(parts[z], 2 * z) for z in range(1, 4)]
+    row_keep, send = row_weights(place, [kept[3] for kept in kept_b], d_rows, vecs, grads[1][2:])
+    away = add(*(part[1] for part in parts))
+    (away, send), grads[2][1:] = tie((away, send), grads[2][1:])
+    row_came = row_swap(send, 1)
+    mlp_own = add(*(part[0] for part in parts), row_swap(away, 2))
+    mlp_near = gather_near(mlp_own[:-GROUP])
+    row_away = add(row_keep[8:], row_came[8:])
+    row_line = row_swap(row_away, 2)
+    grad_back = [grads[j][k] for k in range(count) for j in range(group)]
+
+    keep, send, *d_all = feat_backward(place, cells, kept_a, grad_back, feat_weights, group, waits=(mlp_own, row_away))
+    send, (row_line, mlp_near) = tie(send, (row_line, mlp_near))
+    came = row_swap(send, 1)
+    mlp_near = jnp.stack(mlp_near)
+    mlp_far = tab_swap(mlp_near, 1)
+    row_turned = tab_swap(add(row_keep[4:8], row_came[4:8], row_line[4:8]), 1)
+    away = add(keep[8:], came[8:])
+    cells_grad, mark = cells_backward(
+        own, cells, d_all, (flat(feat_gain), feat_query, feat_key, feat_value), grad_back, group, waits=(away,)
+    )
+    line, mark = tie(row_swap(away, 2), mark)
+    away = add(keep[4:8], came[4:8], line[4:8])
+    away, (row_turned, mlp_far) = tie(away, (row_turned, mlp_far))
+    turned = tab_swap(away, 1)
+    parts = [add(*(ref[z] for ref in (row_keep, row_came, row_line, row_turned))) for z in range(4)]
+    row_own = add(parts[0], *(tab_swap(parts[z], 2 * z) for z in range(1, 4)))
+    row_near = jnp.stack(gather_near(row_own[:-GROUP]))
+    parts = [add(*(ref[z] for ref in (keep, came, line, turned))) for z in range(4)]
+    row_far = tab_swap(row_near, 1)
+    feat_own = add(parts[0], *(tab_swap(parts[z], 2 * z) for z in range(1, 4)))
+    feat_near = jnp.stack(gather_near(feat_own[:-GROUP]))
+    feat_far = tab_swap(feat_near, 1)
+    mlp_vec, row_vec, feat_vec = mlp_own[-GROUP:], row_own[-GROUP:], feat_own[-GROUP:]
+    blocks = [(0, j, part) for j, part in enumerate(own_layers)]
+    blocks += [(k, 0, part) for k, part in enumerate(early, 1)]
+    blocks += [(k, group - 1, part) for k, part in enumerate(late, 1)]
+    layer_out = join_pieces(own, blocks, group, (feat_own,))
+
+    up_sum, down_sum, row_out_sum = finish(
+        place,
+        mlp_near,
+        mlp_far,
+        ((GROUP, 2048, False), (4 * GROUP, 512, True), (GROUP, 512, False)),
+        (feat_own,),
+    )
+    small = ((GROUP, 512, False),)
+    sum_rq, sum_rk, sum_rv = finish(place, row_near, row_far, small * 3, (feat_own,))
+    sum_fq, sum_fk, sum_fv, sum_fo = finish(place, feat_near, feat_far, small * 4, (mark,))
+
+    mlp_vec, row_vec, feat_vec = (part.astype(F32) for part in (mlp_vec, row_vec, feat_vec))
+    rows = sum_fq.shape[0]
+
+    def quarter(vector):
+        return lax.dynamic_slice_in_dim(vector, me * rows, rows, 0)
+
+    return (
+        layer_out.transpose(1, 0, 2)[None],
+        cells_grad.transpose(1, 0, 2)[None],
+        quarter(feat_vec[0]),
+        quarter(feat_vec[1]),
+        sum_fq,
+        sum_fk,
+        sum_fv,
+        sum_fo,
+        quarter(row_vec[2]),
+        quarter(row_vec[0]),
+        quarter(row_vec[1]),
+        sum_rq,
+        sum_rk,
+        sum_rv,
+        row_out_sum,
+        quarter(mlp_vec[7]),
+        quarter(mlp_vec[5]),
+        quarter(mlp_vec[6]),
+        up_sum,
+        lax.dynamic_index_in_dim(mlp_vec[:4], me, 0, keepdims=False),
+        down_sum.T,
+        quarter(mlp_vec[4]),
+    )
+
+
 def solution(mesh):
     in_specs = (
         P("tab", "row", None, None),
@@ -453,4 +1543,7 @@
         P("row", None),
         P("row"),
     )
-    return jax.shard_map(shards, mesh=mesh, in_specs=in_specs, out_specs=out_specs, check_vma=False)
+
+    near = (mesh.shape["tab"], mesh.shape["row"]) == (8, 4)
+    body = by_feature if near else shards
+    return jax.shard_map(body, mesh=mesh, in_specs=in_specs, out_specs=out_specs, check_vma=False)

time: 893 us -> 364 us (0.41)
  matrix products: 492 us -> 0 us
  Pallas kernels: 0 us -> 239 us
  waiting for transfers between devices: 148 us -> 29.5 us
  local copies, waits for them, and re-layouts: 90.7 us -> 8.82 us
  other arithmetic: 90.5 us -> 21.5 us
  starting transfers between devices: 1.59 us -> 58.4 us
  blocking collectives: 44.6 us -> 0 us
  between operations: 17.9 us -> 2.65 us
    dot_general x43 -> x0, matrix products: 492 us -> none  [the longest x10 88 us: project_back(): jnp.einsum('rfe,de->rfd', upstream, weight, preferred_element_type=jnp.fl...]
    pallas_call x0 -> x15, Pallas kernels: none -> 239 us  [call(): pl.pallas_call(body, in_specs=specs, compiler_params=params_of(), **rest)]
    all_gather x4 -> x0, waiting for transfers between devices: 91.3 us -> none  [the longest x1 70 us: shards(): lax.all_gather(key_b, 'row', axis=0, tiled=True)]
    ppermute x0 -> x61, starting transfers between devices: none -> 58.4 us  [the longest x24 31.9 us: tab_swap(): lax.ppermute(values, 'tab', [(index, index ^ step) for index in range(8)])]
    psum x1 -> x0, waiting for transfers between devices: 53 us -> none  [shards(): lax.psum(part_fq.astype(jnp.bfloat16), 'tab').astype(jnp.float32)]
    reshape x7 -> x0, local copies, waits for them, and re-layouts: 44.8 us -> none  [split_heads(): values.reshape(values.shape[0], values.shape[1], HEADS, values.shape[2] /...]
    reduce_sum x7 -> x0, other arithmetic: 40.5 us -> none  [the longest x1 21.4 us: shards(): jnp.sum(jnp.exp(scores_b - highest), -1, keepdims=True)]
    convert_element_type x4 -> x0, local copies, waits for them, and re-layouts: 30.5 us -> none  [the longest x1 7.76 us: shards(): mixed_a = join_heads(jnp.einsum('rhfg,rghd->rfhd', probs_a_low, value_a,...]
  transfers between devices with their start and end apart: 15 -> 61, of which waited for: 4 -> 11; matrix products, arithmetic and copies ran while one was open for 63% -> 7% of each run, Pallas kernels for 0% -> 65%
where the time goes in v2:
time: 364 us; the launch traced here: 360 us
  Pallas kernels  239 us (66%)
  starting transfers between devices  58.4 us (16%)
  waiting for transfers between devices  29.5 us (8%)
  other arithmetic  21.5 us (6%)
  local copies, waits for them, and re-layouts  8.82 us (2%)
    pallas_call x15, Pallas kernels, call(): pl.pallas_call(body, in_specs=specs, compiler_params=params_of(), **rest)  239 us
    ppermute x24, starting transfers between devices, tab_swap(): lax.ppermute(values, 'tab', [(index, index ^ step) for index in range(8)])  31.9 us
    ppermute x37, starting transfers between devices, row_swap(): lax.ppermute(values, 'row', [(index, index ^ step) for index in range(4)])  26.4 us
    ppermute x37, waiting for transfers between devices, row_swap(): lax.ppermute(values, 'row', [(index, index ^ step) for index in range(4)])  20.8 us
    convert_element_type x9, other arithmetic, add(): return total.astype(BF16)  14.9 us
    ppermute x24, waiting for transfers between devices, tab_swap(): lax.ppermute(values, 'tab', [(index, index ^ step) for index in range(8)])  8.69 us
  transfers between devices with their start and end apart: 61, of which 11 were waited for; matrix products, arithmetic and copies ran while one was open for 7% of the time, Pallas kernels for 65%

profile of v2, /device:TPU:0, one launch (start us, length us, event | category | flops | bytes accessed | tf_op | source)
XLA Modules:
  0.0 360.1 jit_solution(10857126254016586191)
XLA Ops:
  0.7 3.5 split.1
  4.7 2.6 collective-permute-start.1
  7.4 17.2 %feat_forward.1 = (bf16[256,512]{1,0:T(8,128)(2,1)}, bf16[256,512]{1,0:T(8,128)(2,1)}, bf16[256,512]{1,0:T(8,128)(2,1)}, bf16[256,512]{1,0:T(8,128)(2,1)}, bf16[...) custom-call(s32[1]{0:T(128)} %bitcast.refs_0_, ...), custom_call_target="tpu_custom_call" | custom-call | flops 13500000256 | bytes 1024 | tf_op jit(solution)/shard_map/feat_forward/pallas_call | solution.py:479
  24.9 1.9 collective-permute-start.4
  27.0 1.9 collective-permute-start.7
  31.5 2.8 collective-permute-done.4.refs_4_.refs_9_
  34.4 5.0 %collective-permute-done.5.refs_5_.refs_10_ = bf16[256,512]{1,0:T(8,128)(2,1)} collective-permute-done((bf16[256,512]{1,0:T(8,128)(2,1)}, bf16[256,512]{1,0:T(8,128)(2,1)}, u32[]{:S(2)}, u32[]{:S(2)}) %collective-permute-start.5) | collective-permute-done | bytes 262176 | tf_op jit(solution)/shard_map/ppermute | solution.py:1238
  40.3 32.5 %row_and_mlp.3 = (bf16[1024,512]{1,0:T(8,128)(2,1)}, bf16[1024,512]{1,0:T(8,128)(2,1)}, bf16[1024,512]{1,0:T(8,128)(2,1)}, bf16[1024,512]{1,0:T(8,128)(2,1)}, bf...) custom-call(s32[3]{0:T(128)} %pad_add_fusion.refs_0_, ...), custom_call_target="tpu_custom_call" | custom-call | flops 25200001024 | bytes 1024 | tf_op jit(solution)/shard_map/row_and_mlp/pallas_call | solution.py:479
  76.1 1.4 collective-permute-start.15
  77.5 33.3 %row_and_mlp.4 = (bf16[1024,512]{1,0:T(8,128)(2,1)}, bf16[1024,512]{1,0:T(8,128)(2,1)}, bf16[1024,512]{1,0:T(8,128)(2,1)}, bf16[1024,512]{1,0:T(8,128)(2,1)}, bf...) custom-call(s32[3]{0:T(128)} %pad_add_fusion.refs_0_, ...), custom_call_target="tpu_custom_call" | custom-call | flops 25200001024 | bytes 1024 | tf_op jit(solution)/shard_map/row_and_mlp/pallas_call | solution.py:479
  112.8 34.8 %row_and_mlp.5 = (bf16[1024,512]{1,0:T(8,128)(2,1)}, bf16[1024,512]{1,0:T(8,128)(2,1)}, bf16[1024,512]{1,0:T(8,128)(2,1)}, bf16[1024,512]{1,0:T(8,128)(2,1)}, bf...) custom-call(s32[3]{0:T(128)} %pad_add_fusion.refs_0_, ...), custom_call_target="tpu_custom_call" | custom-call | flops 25200001024 | bytes 1024 | tf_op jit(solution)/shard_map/row_and_mlp/pallas_call | solution.py:479
  149.9 2.9 collective-permute-done.24
  152.8 1.5 copy-done
  154.3 2.7 add_convert_fusion
  157.1 1.5 collective-permute-start.25
  158.6 18.6 %row_backward.3 = (bf16[256,512]{1,0:T(8,128)(2,1)}, bf16[256,512]{1,0:T(8,128)(2,1)}, bf16[256,512]{1,0:T(8,128)(2,1)}, bf16[256,512]{1,0:T(8,128)(2,1)}, bf16[...) custom-call(s32[3]{0:T(128)} %pad_add_fusion.refs_0_, ...), custom_call_target="tpu_custom_call" | custom-call | flops 13500000256 | bytes 1024 | tf_op jit(solution)/shard_map/row_backward/pallas_call | solution.py:479
  178.6 19.0 %row_backward.4 = (bf16[256,512]{1,0:T(8,128)(2,1)}, bf16[256,512]{1,0:T(8,128)(2,1)}, bf16[256,512]{1,0:T(8,128)(2,1)}, bf16[256,512]{1,0:T(8,128)(2,1)}, bf16[...) custom-call(s32[3]{0:T(128)} %pad_add_fusion.refs_0_, ...), custom_call_target="tpu_custom_call" | custom-call | flops 13500000256 | bytes 1024 | tf_op jit(solution)/shard_map/row_backward/pallas_call | solution.py:479
  197.6 1.3 collective-permute-start.31
  199.8 3.4 add_convert_fusion.6
  203.1 1.6 collective-permute-start.28
  204.8 2.5 collective-permute-start.29
  207.5 19.0 %row_backward.5 = (bf16[256,512]{1,0:T(8,128)(2,1)}, bf16[256,512]{1,0:T(8,128)(2,1)}, bf16[256,512]{1,0:T(8,128)(2,1)}, bf16[256,512]{1,0:T(8,128)(2,1)}, bf16[...) custom-call(s32[3]{0:T(128)} %pad_add_fusion.refs_0_, ...), custom_call_target="tpu_custom_call" | custom-call | flops 13500000256 | bytes 1024 | tf_op jit(solution)/shard_map/row_backward/pallas_call | solution.py:479
  228.4 9.9 %row_weights.1 = (bf16[16,64,512]{2,1,0:T(8,128)(2,1)}, bf16[16,64,512]{2,1,0:T(8,128)(2,1)}) custom-call(s32[2]{0:T(128)} %pad_add_fusion.1.refs_1_.refs_0_, bf16[1024,512]{1,0:T(8,128)(2,1)} %get-tuple-element.249.refs_1_, bf16[1024,512]{1,0:T(8,128)(2,1)} %get-tuple-element.250.refs_2_, bf16[1024,512]{1,0:T(8,128)(2,1)} %get-tuple-element.251.refs_3_, ...), custom_call_target="tpu_custom_call" | custom-call | flops 7200000000 | bytes 1024 | tf_op jit(solution)/shard_map/row_weights/pallas_call | solution.py:479
  239.5 1.2 collective-permute-done.35.refs_24_.refs_20_
  242.2 5.2 %collective-permute-done.36 = bf16[160,512]{1,0:T(8,128)(2,1)S(1)} collective-permute-done((bf16[160,512]{1,0:T(8,128)(2,1)S(1)}, bf16[160,512]{1,0:T(8,128)(2,1)S(1)}, u32[]{:S(2)}, u32[]{:S(2)}) %collective-permute-start.36) | collective-permute-done | bytes 163872 | tf_op jit(solution)/shard_map/ppermute | solution.py:1238
  249.4 3.4 collective-permute-start.40
  253.8 2.0 add_convert_fusion.2.refs_26_
  256.4 29.3 %feat_backward.1 = (bf16[16,80,512]{2,1,0:T(8,128)(2,1)}, bf16[16,80,512]{2,1,0:T(8,128)(2,1)}, bf16[3072,512]{1,0:T(8,128)(2,1)}, bf16[3072,512]{1,0:T(8,128)(2,1)}, bf16[3072,512]{1,0:T(8,128)(2,1)}) custom-call(s32[2]{0:T(128)} %pad_add_fusion.1.refs_1_.refs_0_, bf16[12,256,512]{2,1,0:T(8,128)(2,1)} %bitcast.100, ...), custom_call_target="tpu_custom_call" | custom-call | flops 17999998976 | bytes 1024 | tf_op jit(solution)/shard_map/feat_backward/pallas_call | solution.py:479
  289.2 1.2 add_convert_fusion.8
  290.4 1.6 collective-permute-start.44
  293.3 1.4 collective-permute-start.43
  294.7 11.7 %cells_backward.1 = (bf16[12,256,512]{2,1,0:T(8,128)(2,1)}, f32[8,128]{1,0:T(8,128)}) custom-call(s32[1]{0:T(128)} %bitcast.refs_0_, bf16[12,256,512]{2,1,0:T(8,128)(2,1)} %bitcast.101, bf16[3072,512]{1,0:T(8,128)(2,1)} %get-tuple-element.277.refs_2_, bf16[3072,512]{1,0:T(8,128)(2,1)} %get-tuple-element.278.refs_3_, ...), custom_call_target="tpu_custom_call" | custom-call | flops 10800000000 | bytes 1024 | tf_op jit(solution)/shard_map/cells_backward/pallas_call | solution.py:479
  306.4 3.6 collective-permute-done.43
  311.2 1.3 fusion.13
  312.6 3.3 collective-permute-start.55
  318.5 3.6 collective-permute-done.56
  323.1 1.6 collective-permute-start.58
  324.7 2.8 collective-permute-start.59
  329.8 1.6 collective-permute-start.48
  331.4 2.8 collective-permute-start.49
  335.3 2.5 collective-permute-done.49
  339.6 2.8 collective-permute-start.51
  343.3 2.8 finish.5
  346.1 2.0 finish.4
  348.1 2.5 copy.46
  351.8 3.7 %join_pieces.1 = bf16[12,256,512]{2,1,0:T(8,128)(2,1)} custom-call(s32[1]{0:T(128)} %bitcast.refs_0_, bf16[1,256,512]{2,1,0:T(8,128)(2,1)} %get-tuple-element.176.refs_1_, bf16[1,256,512]{2,1,0:T(8,128)(2,1)} %get-tuple-element.190.refs_2_, bf16[1,256,512]{2,1,0:T(8,128)(2,1)} %get-tuple-element.201.refs_3_, bf16[2,256,512]{2,1,0:T(8,128)(2,1)} %copy-done.10, ...), custom_call_target="tpu_custom_call" | custom-call | flops 1800000000 | bytes 1024 | tf_op jit(solution)/shard_map/join_pieces/pallas_call | solution.py:479
  355.5 1.6 collective-permute-done.53.refs_2_
  357.8 2.1 finish.3
  (151 shorter events, 39.1 us)
Async XLA Ops:
  4.2 20.4 %collective-permute-start = (bf16[3,256,512]{2,1,0:T(8,128)(2,1)}, bf16[3,256,512]{2,1,0:T(8,128)(2,1)S(1)}, u32[]{:S(2)}, u32[]{:S(2)}) collective-permute-start(bf16[3,256,512]{2,1,0:T(8,128)(2,1)} %get-tuple-element.166), channel_id=1, source_target_pairs={{0,1},{1,0},{2,3},{3,2},{4,5},{5,4},{6,7},{7,6},{8,9},{9,8},{10,11... | collective-permute-start | bytes 2359304 | tf_op jit(solution)/shard_map/ppermute | solution.py:1238
  4.7 19.9 %collective-permute-start.1 = (bf16[1,256,512]{2,1,0:T(8,128)(2,1)}, bf16[1,256,512]{2,1,0:T(8,128)(2,1)}, u32[]{:S(2)}, u32[]{:S(2)}) collective-permute-start(bf16[1,256,512]{2,1,0:T(8,128)(2,1)} %get-tuple-element.167), channel_id=1, source_target_pairs={{0,2},{1,3},{2,0},{3,1},{4,6},{5,7},{6,4},{7,5},{8,10},{9,11},{10,... | collective-permute-start | bytes 786440 | tf_op jit(solution)/shard_map/ppermute | solution.py:1238
  7.3 17.3 %collective-permute-start.2 = (bf16[1,256,512]{2,1,0:T(8,128)(2,1)}, bf16[1,256,512]{2,1,0:T(8,128)(2,1)}, u32[]{:S(2)}, u32[]{:S(2)}) collective-permute-start(bf16[1,256,512]{2,1,0:T(8,128)(2,1)} %get-tuple-element.168), channel_id=1, source_target_pairs={{0,3},{1,2},{2,1},{3,0},{4,7},{5,6},{6,5},{7,4},{8,11},{9,10},{10,... | collective-permute-start | bytes 786440 | tf_op jit(solution)/shard_map/ppermute | solution.py:1238
  24.9 9.4 %collective-permute-start.4 = (bf16[256,512]{1,0:T(8,128)(2,1)}, bf16[256,512]{1,0:T(8,128)(2,1)}, u32[]{:S(2)}, u32[]{:S(2)}) collective-permute-start(bf16[256,512]{1,0:T(8,128)(2,1)} %get-tuple-element.170), channel_id=1, source_target_pairs={{0,2},{1,3},{2,0},{3,1},{4,6},{5,7},{6,4},{7,5},{8,10},{9,11},{10,... | collective-permute-start | bytes 786440 | tf_op jit(solution)/shard_map/ppermute | solution.py:1238
  26.8 12.6 %collective-permute-start.5 = (bf16[256,512]{1,0:T(8,128)(2,1)}, bf16[256,512]{1,0:T(8,128)(2,1)}, u32[]{:S(2)}, u32[]{:S(2)}) collective-permute-start(bf16[256,512]{1,0:T(8,128)(2,1)} %get-tuple-element.171), channel_id=1, source_target_pairs={{0,3},{1,2},{2,1},{3,0},{4,7},{5,6},{6,5},{7,4},{8,11},{9,10},{10,... | collective-permute-start | bytes 786440 | tf_op jit(solution)/shard_map/ppermute | solution.py:1238
  26.8 46.0 %collective-permute-start.6 = (bf16[256,512]{1,0:T(8,128)(2,1)}, bf16[256,512]{1,0:T(8,128)(2,1)}, u32[]{:S(2)}, u32[]{:S(2)}) collective-permute-start(bf16[256,512]{1,0:T(8,128)(2,1)} %get-tuple-element.178), channel_id=1, source_target_pairs={{0,1},{1,0},{2,3},{3,2},{4,5},{5,4},{6,7},{7,6},{8,9},{9,8},{10,11... | collective-permute-start | bytes 786440 | tf_op jit(solution)/shard_map/ppermute | solution.py:1238
  27.0 47.0 %collective-permute-start.7 = (bf16[256,512]{1,0:T(8,128)(2,1)}, bf16[256,512]{1,0:T(8,128)(2,1)}, u32[]{:S(2)}, u32[]{:S(2)}) collective-permute-start(bf16[256,512]{1,0:T(8,128)(2,1)} %get-tuple-element.179), channel_id=1, source_target_pairs={{0,2},{1,3},{2,0},{3,1},{4,6},{5,7},{6,4},{7,5},{8,10},{9,11},{10,... | collective-permute-start | bytes 786440 | tf_op jit(solution)/shard_map/ppermute | solution.py:1238
  31.5 42.8 %collective-permute-start.8 = (bf16[256,512]{1,0:T(8,128)(2,1)}, bf16[256,512]{1,0:T(8,128)(2,1)}, u32[]{:S(2)}, u32[]{:S(2)}) collective-permute-start(bf16[256,512]{1,0:T(8,128)(2,1)} %get-tuple-element.180), channel_id=1, source_target_pairs={{0,3},{1,2},{2,1},{3,0},{4,7},{5,6},{6,5},{7,4},{8,11},{9,10},{10,... | collective-permute-start | bytes 786440 | tf_op jit(solution)/shard_map/ppermute | solution.py:1238
  34.3 41.2 %collective-permute-start.10 = (bf16[1,256,512]{2,1,0:T(8,128)(2,1)}, bf16[1,256,512]{2,1,0:T(8,128)(2,1)}, u32[]{:S(2)}, u32[]{:S(2)}) collective-permute-start(bf16[1,256,512]{2,1,0:T(8,128)(2,1)} %get-tuple-element.182), channel_id=1, source_target_pairs={{0,3},{1,2},{2,1},{3,0},{4,7},{5,6},{6,5},{7,4},{8,11},{9,10},{10,... | collective-permute-start | bytes 786440 | tf_op jit(solution)/shard_map/ppermute | solution.py:1238
  39.4 36.7 %collective-permute-start.9 = (bf16[1,256,512]{2,1,0:T(8,128)(2,1)}, bf16[1,256,512]{2,1,0:T(8,128)(2,1)}, u32[]{:S(2)}, u32[]{:S(2)}) collective-permute-start(bf16[1,256,512]{2,1,0:T(8,128)(2,1)} %get-tuple-element.181), channel_id=1, source_target_pairs={{0,2},{1,3},{2,0},{3,1},{4,6},{5,7},{6,4},{7,5},{8,10},{9,11},{10,... | collective-permute-start | bytes 786440 | tf_op jit(solution)/shard_map/ppermute | solution.py:1238
  72.8 38.0 %collective-permute-start.11 = (bf16[256,512]{1,0:T(8,128)(2,1)}, bf16[256,512]{1,0:T(8,128)(2,1)S(1)}, u32[]{:S(2)}, u32[]{:S(2)}) collective-permute-start(bf16[256,512]{1,0:T(8,128)(2,1)} %get-tuple-element.192), channel_id=1, source_target_pairs={{0,1},{1,0},{2,3},{3,2},{4,5},{5,4},{6,7},{7,6},{8,9},{9,8},{10,11... | collective-permute-start | bytes 786440 | tf_op jit(solution)/shard_map/ppermute | solution.py:1238
  74.0 37.0 %collective-permute-start.12 = (bf16[256,512]{1,0:T(8,128)(2,1)}, bf16[256,512]{1,0:T(8,128)(2,1)}, u32[]{:S(2)}, u32[]{:S(2)}) collective-permute-start(bf16[256,512]{1,0:T(8,128)(2,1)} %get-tuple-element.193), channel_id=1, source_target_pairs={{0,2},{1,3},{2,0},{3,1},{4,6},{5,7},{6,4},{7,5},{8,10},{9,11},{10,... | collective-permute-start | bytes 786440 | tf_op jit(solution)/shard_map/ppermute | solution.py:1238
  74.3 37.4 %collective-permute-start.13 = (bf16[256,512]{1,0:T(8,128)(2,1)}, bf16[256,512]{1,0:T(8,128)(2,1)}, u32[]{:S(2)}, u32[]{:S(2)}) collective-permute-start(bf16[256,512]{1,0:T(8,128)(2,1)} %get-tuple-element.194), channel_id=1, source_target_pairs={{0,3},{1,2},{2,1},{3,0},{4,7},{5,6},{6,5},{7,4},{8,11},{9,10},{10,... | collective-permute-start | bytes 786440 | tf_op jit(solution)/shard_map/ppermute | solution.py:1238
  75.5 37.4 %collective-permute-start.14 = (bf16[1,256,512]{2,1,0:T(8,128)(2,1)}, bf16[1,256,512]{2,1,0:T(8,128)(2,1)}, u32[]{:S(2)}, u32[]{:S(2)}) collective-permute-start(bf16[1,256,512]{2,1,0:T(8,128)(2,1)} %get-tuple-element.195), channel_id=1, source_target_pairs={{0,2},{1,3},{2,0},{3,1},{4,6},{5,7},{6,4},{7,5},{8,10},{9,11},{10,... | collective-permute-start | bytes 786440 | tf_op jit(solution)/shard_map/ppermute | solution.py:1238
  76.1 36.7 %collective-permute-start.15 = (bf16[1,256,512]{2,1,0:T(8,128)(2,1)}, bf16[1,256,512]{2,1,0:T(8,128)(2,1)}, u32[]{:S(2)}, u32[]{:S(2)}) collective-permute-start(bf16[1,256,512]{2,1,0:T(8,128)(2,1)} %get-tuple-element.196), channel_id=1, source_target_pairs={{0,3},{1,2},{2,1},{3,0},{4,7},{5,6},{6,5},{7,4},{8,11},{9,10},{10,... | collective-permute-start | bytes 786440 | tf_op jit(solution)/shard_map/ppermute | solution.py:1238
  110.9 36.7 %collective-permute-start.16 = (bf16[2,256,512]{2,1,0:T(8,128)(2,1)}, bf16[2,256,512]{2,1,0:T(8,128)(2,1)S(1)}, u32[]{:S(2)}, u32[]{:S(2)}) collective-permute-start(bf16[2,256,512]{2,1,0:T(8,128)(2,1)} %get-tuple-element.203), channel_id=1, source_target_pairs={{0,1},{1,0},{2,3},{3,2},{4,5},{5,4},{6,7},{7,6},{8,9},{9,8},{10,11... | collective-permute-start | bytes 1572872 | tf_op jit(solution)/shard_map/ppermute | solution.py:1238
  111.0 36.6 %collective-permute-start.17 = (bf16[2,256,512]{2,1,0:T(8,128)(2,1)}, bf16[2,256,512]{2,1,0:T(8,128)(2,1)}, u32[]{:S(2)}, u32[]{:S(2)}) collective-permute-start(bf16[2,256,512]{2,1,0:T(8,128)(2,1)} %get-tuple-element.204), channel_id=1, source_target_pairs={{0,2},{1,3},{2,0},{3,1},{4,6},{5,7},{6,4},{7,5},{8,10},{9,11},{10,... | collective-permute-start | bytes 1572872 | tf_op jit(solution)/shard_map/ppermute | solution.py:1238
  111.7 36.0 %collective-permute-start.18 = (bf16[2,256,512]{2,1,0:T(8,128)(2,1)}, bf16[2,256,512]{2,1,0:T(8,128)(2,1)}, u32[]{:S(2)}, u32[]{:S(2)}) collective-permute-start(bf16[2,256,512]{2,1,0:T(8,128)(2,1)} %get-tuple-element.205), channel_id=1, source_target_pairs={{0,3},{1,2},{2,1},{3,0},{4,7},{5,6},{6,5},{7,4},{8,11},{9,10},{10,... | collective-permute-start | bytes 1572872 | tf_op jit(solution)/shard_map/ppermute | solution.py:1238
  148.1 29.8 %collective-permute-start.19 = (bf16[1,256,512]{2,1,0:T(8,128)(2,1)}, bf16[1,256,512]{2,1,0:T(8,128)(2,1)S(1)}, u32[]{:S(2)}, u32[]{:S(2)}) collective-permute-start(bf16[1,256,512]{2,1,0:T(8,128)(2,1)} %get-tuple-element.209), channel_id=1, source_target_pairs={{0,1},{1,0},{2,3},{3,2},{4,5},{5,4},{6,7},{7,6},{8,9},{9,8},{10,11... | collective-permute-start | bytes 786440 | tf_op jit(solution)/shard_map/ppermute | solution.py:1238
  148.2 30.4 %collective-permute-start.20 = (bf16[1,256,512]{2,1,0:T(8,128)(2,1)}, bf16[1,256,512]{2,1,0:T(8,128)(2,1)}, u32[]{:S(2)}, u32[]{:S(2)}) collective-permute-start(bf16[1,256,512]{2,1,0:T(8,128)(2,1)} %get-tuple-element.210), channel_id=1, source_target_pairs={{0,2},{1,3},{2,0},{3,1},{4,6},{5,7},{6,4},{7,5},{8,10},{9,11},{10,... | collective-permute-start | bytes 786440 | tf_op jit(solution)/shard_map/ppermute | solution.py:1238
  148.8 29.9 %collective-permute-start.21 = (bf16[1,256,512]{2,1,0:T(8,128)(2,1)}, bf16[1,256,512]{2,1,0:T(8,128)(2,1)}, u32[]{:S(2)}, u32[]{:S(2)}) collective-permute-start(bf16[1,256,512]{2,1,0:T(8,128)(2,1)} %get-tuple-element.211), channel_id=1, source_target_pairs={{0,3},{1,2},{2,1},{3,0},{4,7},{5,6},{6,5},{7,4},{8,11},{9,10},{10,... | collective-permute-start | bytes 786440 | tf_op jit(solution)/shard_map/ppermute | solution.py:1238
  157.1 42.7 %collective-permute-start.25 = (bf16[8,160,512]{2,1,0:T(8,128)(2,1)}, bf16[8,160,512]{2,1,0:T(8,128)(2,1)}, u32[]{:S(2)}, u32[]{:S(2)}) collective-permute-start(bf16[8,160,512]{2,1,0:T(8,128)(2,1)} %add_convert_fusion), channel_id=1, source_target_pairs={{0,4},{4,0},{8,12},{12,8},{16,20},{20,16},{24,28},{28,24},{1,5},{5... | collective-permute-start | bytes 3932168 | tf_op jit(solution)/shard_map/ppermute | solution.py:1242
  177.1 27.6 %collective-permute-start.22 = (bf16[256,512]{1,0:T(8,128)(2,1)}, bf16[256,512]{1,0:T(8,128)(2,1)}, u32[]{:S(2)}, u32[]{:S(2)}) collective-permute-start(bf16[256,512]{1,0:T(8,128)(2,1)} %get-tuple-element.242), channel_id=1, source_target_pairs={{0,2},{1,3},{2,0},{3,1},{4,6},{5,7},{6,4},{7,5},{8,10},{9,11},{10,... | collective-permute-start | bytes 786440 | tf_op jit(solution)/shard_map/ppermute | solution.py:1238
  177.8 29.4 %collective-permute-start.23 = (bf16[256,512]{1,0:T(8,128)(2,1)}, bf16[256,512]{1,0:T(8,128)(2,1)}, u32[]{:S(2)}, u32[]{:S(2)}) collective-permute-start(bf16[256,512]{1,0:T(8,128)(2,1)} %get-tuple-element.243), channel_id=1, source_target_pairs={{0,3},{1,2},{2,1},{3,0},{4,7},{5,6},{6,5},{7,4},{8,11},{9,10},{10,... | collective-permute-start | bytes 786440 | tf_op jit(solution)/shard_map/ppermute | solution.py:1238
  197.6 28.9 %collective-permute-start.31 = (bf16[256,512]{1,0:T(8,128)(2,1)}, bf16[256,512]{1,0:T(8,128)(2,1)}, u32[]{:S(2)}, u32[]{:S(2)}) collective-permute-start(bf16[256,512]{1,0:T(8,128)(2,1)} %get-tuple-element.262), channel_id=1, source_target_pairs={{0,2},{1,3},{2,0},{3,1},{4,6},{5,7},{6,4},{7,5},{8,10},{9,11},{10,... | collective-permute-start | bytes 786440 | tf_op jit(solution)/shard_map/ppermute | solution.py:1238
  198.9 27.6 %collective-permute-start.32 = (bf16[256,512]{1,0:T(8,128)(2,1)}, bf16[256,512]{1,0:T(8,128)(2,1)}, u32[]{:S(2)}, u32[]{:S(2)}) collective-permute-start(bf16[256,512]{1,0:T(8,128)(2,1)} %get-tuple-element.263), channel_id=1, source_target_pairs={{0,3},{1,2},{2,1},{3,0},{4,7},{5,6},{6,5},{7,4},{8,11},{9,10},{10,... | collective-permute-start | bytes 786440 | tf_op jit(solution)/shard_map/ppermute | solution.py:1238
  203.1 24.2 %collective-permute-start.28 = (bf16[2,160,512]{2,1,0:T(8,128)(2,1)S(1)}, bf16[2,160,512]{2,1,0:T(8,128)(2,1)}, u32[]{:S(2)}, u32[]{:S(2)}) collective-permute-start(bf16[2,160,512]{2,1,0:T(8,128)(2,1)S(1)} %get-tuple-element.324), channel_id=1, source_target_pairs={{0,8},{4,12},{8,0},{12,4},{16,24},{20,28},{24,16},{28,20},{1,9},{5... | collective-permute-start | bytes 983048 | tf_op jit(solution)/shard_map/ppermute | solution.py:1242
  204.8 33.6 %collective-permute-start.29 = (bf16[2,160,512]{2,1,0:T(8,128)(2,1)S(1)}, bf16[2,160,512]{2,1,0:T(8,128)(2,1)}, u32[]{:S(2)}, u32[]{:S(2)}) collective-permute-start(bf16[2,160,512]{2,1,0:T(8,128)(2,1)S(1)} %get-tuple-element.326), channel_id=1, source_target_pairs={{0,16},{4,20},{8,24},{12,28},{16,0},{20,4},{24,8},{28,12},{1,17},{... | collective-permute-start | bytes 983048 | tf_op jit(solution)/shard_map/ppermute | solution.py:1242
  207.3 31.0 %collective-permute-start.30 = (bf16[2,160,512]{2,1,0:T(8,128)(2,1)S(1)}, bf16[2,160,512]{2,1,0:T(8,128)(2,1)}, u32[]{:S(2)}, u32[]{:S(2)}) collective-permute-start(bf16[2,160,512]{2,1,0:T(8,128)(2,1)S(1)} %get-tuple-element.325), channel_id=1, source_target_pairs={{0,24},{4,28},{8,16},{12,20},{16,8},{20,12},{24,0},{28,4},{1,25},{... | collective-permute-start | bytes 983048 | tf_op jit(solution)/shard_map/ppermute | solution.py:1242
  226.5 13.0 %collective-permute-start.33 = (bf16[256,512]{1,0:T(8,128)(2,1)}, bf16[256,512]{1,0:T(8,128)(2,1)}, u32[]{:S(2)}, u32[]{:S(2)}) collective-permute-start(bf16[256,512]{1,0:T(8,128)(2,1)} %get-tuple-element.265), channel_id=1, source_target_pairs={{0,1},{1,0},{2,3},{3,2},{4,5},{5,4},{6,7},{7,6},{8,9},{9,8},{10,11... | collective-permute-start | bytes 786440 | tf_op jit(solution)/shard_map/ppermute | solution.py:1238
  226.6 12.9 %collective-permute-start.34 = (bf16[256,512]{1,0:T(8,128)(2,1)}, bf16[256,512]{1,0:T(8,128)(2,1)}, u32[]{:S(2)}, u32[]{:S(2)}) collective-permute-start(bf16[256,512]{1,0:T(8,128)(2,1)} %get-tuple-element.266), channel_id=1, source_target_pairs={{0,2},{1,3},{2,0},{3,1},{4,6},{5,7},{6,4},{7,5},{8,10},{9,11},{10,... | collective-permute-start | bytes 786440 | tf_op jit(solution)/shard_map/ppermute | solution.py:1238
  227.3 13.5 %collective-permute-start.35 = (bf16[256,512]{1,0:T(8,128)(2,1)}, bf16[256,512]{1,0:T(8,128)(2,1)}, u32[]{:S(2)}, u32[]{:S(2)}) collective-permute-start(bf16[256,512]{1,0:T(8,128)(2,1)} %get-tuple-element.267), channel_id=1, source_target_pairs={{0,3},{1,2},{2,1},{3,0},{4,7},{5,6},{6,5},{7,4},{8,11},{9,10},{10,... | collective-permute-start | bytes 786440 | tf_op jit(solution)/shard_map/ppermute | solution.py:1238
  240.8 12.1 %collective-permute-start.37 = (bf16[16,64,512]{2,1,0:T(8,128)(2,1)}, bf16[16,64,512]{2,1,0:T(8,128)(2,1)S(1)}, u32[]{:S(2)}, u32[]{:S(2)}) collective-permute-start(bf16[16,64,512]{2,1,0:T(8,128)(2,1)} %get-tuple-element.273), channel_id=1, source_target_pairs={{0,1},{1,0},{2,3},{3,2},{4,5},{5,4},{6,7},{7,6},{8,9},{9,8},{10,11... | collective-permute-start | bytes 3145736 | tf_op jit(solution)/shard_map/ppermute | solution.py:1238
  241.7 14.1 %collective-permute-start.26 = (bf16[256,512]{1,0:T(8,128)(2,1)}, bf16[256,512]{1,0:T(8,128)(2,1)}, u32[]{:S(2)}, u32[]{:S(2)}) collective-permute-start(bf16[256,512]{1,0:T(8,128)(2,1)} %get-tuple-element.247), channel_id=1, source_target_pairs={{0,1},{1,0},{2,3},{3,2},{4,5},{5,4},{6,7},{7,6},{8,9},{9,8},{10,11... | collective-permute-start | bytes 786440 | tf_op jit(solution)/shard_map/ppermute | solution.py:1238
  241.7 14.7 %collective-permute-start.27 = (bf16[256,512]{1,0:T(8,128)(2,1)}, bf16[256,512]{1,0:T(8,128)(2,1)}, u32[]{:S(2)}, u32[]{:S(2)}) collective-permute-start(bf16[256,512]{1,0:T(8,128)(2,1)} %get-tuple-element.248), channel_id=1, source_target_pairs={{0,1},{1,0},{2,3},{3,2},{4,5},{5,4},{6,7},{7,6},{8,9},{9,8},{10,11... | collective-permute-start | bytes 786440 | tf_op jit(solution)/shard_map/ppermute | solution.py:1238
  248.6 37.2 %collective-permute-start.39 = (bf16[144,512]{1,0:T(8,128)(2,1)S(1)}, bf16[144,512]{1,0:T(8,128)(2,1)S(1)}, u32[]{:S(2)}, u32[]{:S(2)}) collective-permute-start(bf16[144,512]{1,0:T(8,128)(2,1)S(1)} %slice.338), channel_id=1, source_target_pairs={{0,8},{4,12},{8,0},{12,4},{16,24},{20,28},{24,16},{28,20},{1,9},{5... | collective-permute-start | bytes 442376 | tf_op jit(solution)/shard_map/ppermute | solution.py:1242
  249.4 36.4 %collective-permute-start.40 = (bf16[144,512]{1,0:T(8,128)(2,1)S(1)}, bf16[144,512]{1,0:T(8,128)(2,1)S(1)}, u32[]{:S(2)}, u32[]{:S(2)}) collective-permute-start(bf16[144,512]{1,0:T(8,128)(2,1)S(1)} %slice.338), channel_id=1, source_target_pairs={{0,16},{4,20},{8,24},{12,28},{16,0},{20,4},{24,8},{28,12},{1,17},{... | collective-permute-start | bytes 442376 | tf_op jit(solution)/shard_map/ppermute | solution.py:1242
  252.8 32.9 %collective-permute-start.41 = (bf16[144,512]{1,0:T(8,128)(2,1)S(1)}, bf16[144,512]{1,0:T(8,128)(2,1)S(1)}, u32[]{:S(2)}, u32[]{:S(2)}) collective-permute-start(bf16[144,512]{1,0:T(8,128)(2,1)S(1)} %slice.338), channel_id=1, source_target_pairs={{0,24},{4,28},{8,16},{12,20},{16,8},{20,12},{24,0},{28,4},{1,25},{... | collective-permute-start | bytes 442376 | tf_op jit(solution)/shard_map/ppermute | solution.py:1242
  255.8 30.0 %collective-permute-start.38 = (bf16[8,64,512]{2,1,0:T(8,128)(2,1)}, bf16[8,64,512]{2,1,0:T(8,128)(2,1)}, u32[]{:S(2)}, u32[]{:S(2)}) collective-permute-start(bf16[8,64,512]{2,1,0:T(8,128)(2,1)} %add_convert_fusion.2.refs_26_), channel_id=1, source_target_pairs={{0,2},{1,3},{2,0},{3,1},{4,6},{5,7},{6,4},{7,5},{8,10},{9,11},{10,... | collective-permute-start | bytes 1572872 | tf_op jit(solution)/shard_map/ppermute | solution.py:1238
  288.7 22.5 %collective-permute-start.45 = (bf16[4,144,512]{2,1,0:T(8,128)(2,1)}, bf16[4,144,512]{2,1,0:T(8,128)(2,1)}, u32[]{:S(2)}, u32[]{:S(2)}) collective-permute-start(bf16[4,144,512]{2,1,0:T(8,128)(2,1)} %pad_maximum_fusion.refs_1_), channel_id=1, source_target_pairs={{0,4},{4,0},{8,12},{12,8},{16,20},{20,16},{24,28},{28,24},{1,5},{5... | collective-permute-start | bytes 1769480 | tf_op jit(solution)/shard_map/ppermute | solution.py:1242
  290.4 20.8 %collective-permute-start.44 = (bf16[4,64,512]{2,1,0:T(8,128)(2,1)S(1)}, bf16[4,64,512]{2,1,0:T(8,128)(2,1)}, u32[]{:S(2)}, u32[]{:S(2)}) collective-permute-start(bf16[4,64,512]{2,1,0:T(8,128)(2,1)S(1)} %add_convert_fusion.8), channel_id=1, source_target_pairs={{0,4},{4,0},{8,12},{12,8},{16,20},{20,16},{24,28},{28,24},{1,5},{5... | collective-permute-start | bytes 786440 | tf_op jit(solution)/shard_map/ppermute | solution.py:1242
  293.3 16.7 %collective-permute-start.43 = (bf16[8,80,512]{2,1,0:T(8,128)(2,1)}, bf16[8,80,512]{2,1,0:T(8,128)(2,1)S(1)}, u32[]{:S(2)}, u32[]{:S(2)}) collective-permute-start(bf16[8,80,512]{2,1,0:T(8,128)(2,1)} %add_convert_fusion.1.refs_21_), channel_id=1, source_target_pairs={{0,2},{1,3},{2,0},{3,1},{4,6},{5,7},{6,4},{7,5},{8,10},{9,11},{10,... | collective-permute-start | bytes 1966088 | tf_op jit(solution)/shard_map/ppermute | solution.py:1238
  317.5 11.1 %collective-permute-start.46 = (bf16[4,80,512]{2,1,0:T(8,128)(2,1)S(1)}, bf16[4,80,512]{2,1,0:T(8,128)(2,1)S(1)}, u32[]{:S(2)}, u32[]{:S(2)}) collective-permute-start(bf16[4,80,512]{2,1,0:T(8,128)(2,1)S(1)} %add_convert_fusion.3), channel_id=1, source_target_pairs={{0,4},{4,0},{8,12},{12,8},{16,20},{20,16},{24,28},{28,24},{1,5},{5... | collective-permute-start | bytes 983048 | tf_op jit(solution)/shard_map/ppermute | solution.py:1242
  323.1 11.1 %collective-permute-start.58 = (bf16[48,512]{1,0:T(8,128)(2,1)S(1)}, bf16[48,512]{1,0:T(8,128)(2,1)S(1)}, u32[]{:S(2)}, u32[]{:S(2)}) collective-permute-start(bf16[48,512]{1,0:T(8,128)(2,1)S(1)} %get-tuple-element.337), channel_id=1, source_target_pairs={{0,16},{4,20},{8,24},{12,28},{16,0},{20,4},{24,8},{28,12},{1,17},{... | collective-permute-start | bytes 147464 | tf_op jit(solution)/shard_map/ppermute | solution.py:1242
  324.7 9.5 %collective-permute-start.59 = (bf16[48,512]{1,0:T(8,128)(2,1)S(1)}, bf16[48,512]{1,0:T(8,128)(2,1)S(1)}, u32[]{:S(2)}, u32[]{:S(2)}) collective-permute-start(bf16[48,512]{1,0:T(8,128)(2,1)S(1)} %get-tuple-element.337), channel_id=1, source_target_pairs={{0,24},{4,28},{8,16},{12,20},{16,8},{20,12},{24,0},{28,4},{1,25},{... | collective-permute-start | bytes 147464 | tf_op jit(solution)/shard_map/ppermute | solution.py:1242
  334.3 11.9 %collective-permute-start.60 = (bf16[4,48,512]{2,1,0:T(8,128)(2,1)S(1)}, bf16[4,48,512]{2,1,0:T(8,128)(2,1)}, u32[]{:S(2)}, u32[]{:S(2)}) collective-permute-start(bf16[4,48,512]{2,1,0:T(8,128)(2,1)S(1)} %pad_maximum_fusion.2.refs_1_), channel_id=1, source_target_pairs={{0,4},{4,0},{8,12},{12,8},{16,20},{20,16},{24,28},{28,24},{1,5},{5... | collective-permute-start | bytes 589832 | tf_op jit(solution)/shard_map/ppermute | solution.py:1242
  338.9 11.8 %collective-permute-start.50 = (bf16[64,512]{1,0:T(8,128)(2,1)S(1)}, bf16[64,512]{1,0:T(8,128)(2,1)S(1)}, u32[]{:S(2)}, u32[]{:S(2)}) collective-permute-start(bf16[64,512]{1,0:T(8,128)(2,1)S(1)} %get-tuple-element.335), channel_id=1, source_target_pairs={{0,8},{4,12},{8,0},{12,4},{16,24},{20,28},{24,16},{28,20},{1,9},{5... | collective-permute-start | bytes 196616 | tf_op jit(solution)/shard_map/ppermute | solution.py:1242
  339.6 11.1 %collective-permute-start.51 = (bf16[64,512]{1,0:T(8,128)(2,1)S(1)}, bf16[64,512]{1,0:T(8,128)(2,1)S(1)}, u32[]{:S(2)}, u32[]{:S(2)}) collective-permute-start(bf16[64,512]{1,0:T(8,128)(2,1)S(1)} %get-tuple-element.335), channel_id=1, source_target_pairs={{0,16},{4,20},{8,24},{12,28},{16,0},{20,4},{24,8},{28,12},{1,17},{... | collective-permute-start | bytes 196616 | tf_op jit(solution)/shard_map/ppermute | solution.py:1242
  (27 other events, 179.6 us)

commit v3 on v2

--- a/solution.py
+++ b/solution.py
@@ -522,10 +522,10 @@
     return jnp.concatenate([left, right], 1)
 
 
-def split_kernel(group, me_ref, whole_ref, *rest):
+def split_kernel(group, plan, me_ref, whole_ref, *rest):
     outs, sems = rest[:-1], rest[-1]
     copies = []
-    for index, (piece, first, size) in enumerate(split_plan(group)):
+    for index, (piece, first, size) in enumerate(plan):
         source = whole_ref.at[pl.ds((me_ref[0] ^ piece) * group + first, size)]
         copies.append(pltpu.make_async_copy(source, outs[index], sems.at[index]))
         copies[-1].start()
@@ -533,16 +533,11 @@
         copy.wait()
 
 
-def split_plan(group):
-    return [(0, 0, group), (1, 0, group)] + [(piece, j, 1) for j in range(group) for piece in (2, 3)]
-
-
-def split(me, whole, group, waits=()):
-    plan = split_plan(group)
+def split(me, whole, group, plan, waits=()):
     _, rows, width = whole.shape
     return call(
-        functools.partial(split_kernel, group),
-        (me, whole,),
+        functools.partial(split_kernel, group, plan),
+        (me, whole),
         waits,
         in_specs=[smem_spec(), any_spec()],
         out_specs=[vmem_spec()] * len(plan),
@@ -578,11 +573,13 @@
 
 
 def feat_forward_kernel(
-    group, me_ref, cells_ref, gain, shift, w_query, w_key, w_value, w_out, bias, *rest
+    group, plan, me_ref, cells_ref, cot_ref, gain, shift, w_query, w_key, w_value, w_out, bias, *rest
 ):
     feats, rows, width = cells_ref.shape
     outs = rest[:feats]
-    q_ref, k_ref, v_ref, mixed_ref, extra_ref = rest[feats:]
+    q_ref, k_ref, v_ref, mixed_ref, extra_ref = rest[feats : feats + 5]
+    for (piece, first, count), out in zip(plan, rest[feats + 5 :]):
+        out[...] = cot_ref[pl.ds((me_ref[0] ^ piece) * group + first, count)]
     size, parts = feats * GROUP, rows // GROUP
     cells = gather_cells(group, me_ref, cells_ref)
     unit, _ = unit_of(cells.astype(F32))
@@ -625,23 +622,26 @@
             outs[index][part * GROUP : (part + 1) * GROUP, :] = after[start : start + GROUP]
 
 
-def feat_forward(me, cells, weights, group, block=64, waits=()):
+def feat_forward(me, cells, cot, weights, group, plan, block=64, waits=()):
     feats, rows, width = cells.shape
     tokens = block * feats
     vector, whole = fixed((1, width)), fixed((width, width))
     return call(
-        functools.partial(feat_forward_kernel, group),
-        (me, cells, *weights,),
+        functools.partial(feat_forward_kernel, group, plan),
+        (me, cells, cot, *weights),
         waits,
         grid=(rows // block,),
-        in_specs=[smem_spec(), pl.BlockSpec((feats, block, width), lambda i: (0, i, 0))]
+        in_specs=[smem_spec()]
+        + [pl.BlockSpec((feats, block, width), lambda i: (0, i, 0))] * 2
         + [vector, vector, whole, whole, whole, whole, vector],
         out_specs=[pl.BlockSpec((block, width), lambda i: (i, 0))] * feats
         + [pl.BlockSpec((tokens, width), lambda i: (i, 0))] * 4
-        + [pl.BlockSpec((tokens, HEAD), lambda i: (i, 0))],
+        + [pl.BlockSpec((tokens, HEAD), lambda i: (i, 0))]
+        + [pl.BlockSpec((size, block, width), lambda i: (0, i, 0)) for _, _, size in plan],
         out_shape=[shape_of((rows, width))] * feats
         + [shape_of((rows * feats, width))] * 4
-        + [shape_of((rows * feats, HEAD))],
+        + [shape_of((rows * feats, HEAD))]
+        + [shape_of((size, rows, width)) for _, _, size in plan],
         cost_estimate=cost_of(15),
         name="feat_forward",
     )
@@ -844,7 +844,7 @@
         value_all[head, span, :] = dot_nn(prob.astype(BF16), mixed_grad_ref[...]).astype(BF16)
     for span, score_grad in zip(spans, score_grads):
         key_all[head, span, :] = (dot_nn(score_grad, q_ref[...]) * SCORE).astype(BF16)
-    query_sum[...] = dot_tn(jnp.concatenate(score_grads, 0), k_ref[...])
+    query_sum[...] = dot_nn(k_ref[...].T, jnp.concatenate(score_grads, 0)).T
     query_all[head] = (query_sum[...] * SCORE).astype(BF16)
 
     @pl.when(head == HEADS - 1)
@@ -1356,18 +1356,24 @@
         down_weight,
         flat(down_bias),
     )
-    cot_own, cot_near, *cot_far = split(own, upstream, group)
+    far = split(own, upstream, group, ((2, 0, 1), (3, 0, 1)))
+    cot_first = [row_swap(far[0], 2), row_swap(far[1], 3)]
+    plan = ((0, 0, group), (1, 0, group)) + tuple((k, j, 1) for j in range(1, group) for k in (2, 3))
+    forward = feat_forward(own, cells, upstream, (*feat_weights, flat(feat_bias)), group, plan, waits=(far[0],))
+    after_out, kept_a = list(forward[:feats]), forward[feats : feats + 5]
+    cot_own, cot_near, *cot_far = forward[feats + 5 :]
+    leaving = [after_out[k * group] for k in range(1, count)]
+    (leaving, cot_near), cot_first = tie((leaving, cot_near), cot_first)
+    after_out[group :: group] = leaving
     cot_near = row_swap(cot_near, 1)
-    cot_first = [row_swap(cot_far[0], 2), row_swap(cot_far[1], 3)]
-    forward = feat_forward(own, cells, (*feat_weights, flat(feat_bias)), group)
-    after_out, kept_a = list(forward[:feats]), forward[feats:]
-    leaving = [after_out[k * group] for k in range(1, count)]
-    leaving, (cot_near, cot_first) = tie(leaving, (cot_near, cot_first))
-    after_out[group :: group] = leaving
+    first = [row_swap(after_out[k * group], k) for k in range(count)]
+    leaving = [after_out[k * group + 1] for k in range(1, count)]
+    leaving, first = tie(leaving, first)
+    after_out[group + 1 :: group] = leaving
     afters, own_layers, kept_b, backs, mlp_sums, old_layers, late = [], [], [], [], None, [], []
     for j in range(group):
-        afters.append([row_swap(after_out[k * group + j], k) for k in range(count)])
-        cot = cot_first if j == 0 else [row_swap(cot_far[2 * j], 2), row_swap(cot_far[2 * j + 1], 3)]
+        afters.append(first if j == 0 else [row_swap(after_out[k * group + j], k) for k in range(count)])
+        cot = cot_first if j == 0 else [row_swap(cot_far[2 * j - 2], 2), row_swap(cot_far[2 * j - 1], 3)]
         found = row_and_mlp(
             info,
             place,
@@ -1415,17 +1421,17 @@
     away = add(*(part[1] for part in parts))
     (away, send), grads[2][1:] = tie((away, send), grads[2][1:])
     row_came = row_swap(send, 1)
-    mlp_own = add(*(part[0] for part in parts), row_swap(away, 2))
-    mlp_near = gather_near(mlp_own[:-GROUP])
+    mlp_line = row_swap(away, 2)
     row_away = add(row_keep[8:], row_came[8:])
     row_line = row_swap(row_away, 2)
+    mlp_parts = parts
     grad_back = [grads[j][k] for k in range(count) for j in range(group)]
 
-    keep, send, *d_all = feat_backward(place, cells, kept_a, grad_back, feat_weights, group, waits=(mlp_own, row_away))
-    send, (row_line, mlp_near) = tie(send, (row_line, mlp_near))
+    keep, send, *d_all = feat_backward(place, cells, kept_a, grad_back, feat_weights, group, waits=(row_away,))
+    send, (row_line, mlp_line) = tie(send, (row_line, mlp_line))
     came = row_swap(send, 1)
-    mlp_near = jnp.stack(mlp_near)
-    mlp_far = tab_swap(mlp_near, 1)
+    mlp_own = add(*(part[0] for part in mlp_parts), mlp_line)
+    mlp_near = gather_near(mlp_own[:-GROUP])
     row_turned = tab_swap(add(row_keep[4:8], row_came[4:8], row_line[4:8]), 1)
     away = add(keep[8:], came[8:])
     cells_grad, mark = cells_backward(
@@ -1433,16 +1439,19 @@
     )
     line, mark = tie(row_swap(away, 2), mark)
     away = add(keep[4:8], came[4:8], line[4:8])
-    away, (row_turned, mlp_far) = tie(away, (row_turned, mlp_far))
+    away, (row_turned, mlp_near) = tie(away, (row_turned, mlp_near))
     turned = tab_swap(away, 1)
     parts = [add(*(ref[z] for ref in (row_keep, row_came, row_line, row_turned))) for z in range(4)]
-    row_own = add(parts[0], *(tab_swap(parts[z], 2 * z) for z in range(1, 4)))
-    row_near = jnp.stack(gather_near(row_own[:-GROUP]))
+    row_parts = [parts[0]] + [tab_swap(parts[z], 2 * z) for z in range(1, 4)]
     parts = [add(*(ref[z] for ref in (keep, came, line, turned))) for z in range(4)]
-    row_far = tab_swap(row_near, 1)
-    feat_own = add(parts[0], *(tab_swap(parts[z], 2 * z) for z in range(1, 4)))
-    feat_near = jnp.stack(gather_near(feat_own[:-GROUP]))
-    feat_far = tab_swap(feat_near, 1)
+    parts, mlp_near = tie(parts, mlp_near)
+    mlp_near = jnp.stack(mlp_near)
+    mlp_far = tab_swap(mlp_near, 1)
+    parts[1:] = [tab_swap(parts[z], 2 * z) for z in range(1, 4)]
+    parts, row_parts = tie(parts, row_parts)
+    row_own, feat_own = add(*row_parts), add(*parts)
+    near = jnp.stack(gather_near(jnp.concatenate([row_own[:-GROUP], feat_own[:-GROUP]], 0)))
+    far = tab_swap(near, 1)
     mlp_vec, row_vec, feat_vec = mlp_own[-GROUP:], row_own[-GROUP:], feat_own[-GROUP:]
     blocks = [(0, j, part) for j, part in enumerate(own_layers)]
     blocks += [(k, 0, part) for k, part in enumerate(early, 1)]
@@ -1456,9 +1465,8 @@
         ((GROUP, 2048, False), (4 * GROUP, 512, True), (GROUP, 512, False)),
         (feat_own,),
     )
-    small = ((GROUP, 512, False),)
-    sum_rq, sum_rk, sum_rv = finish(place, row_near, row_far, small * 3, (feat_own,))
-    sum_fq, sum_fk, sum_fv, sum_fo = finish(place, feat_near, feat_far, small * 4, (mark,))
+    small = ((GROUP, 512, False),) * 7
+    sum_rq, sum_rk, sum_rv, sum_fq, sum_fk, sum_fv, sum_fo = finish(place, near, far, small, (mark, row_out_sum))
 
     mlp_vec, row_vec, feat_vec = (part.astype(F32) for part in (mlp_vec, row_vec, feat_vec))
     rows = sum_fq.shape[0]

time: 364 us -> 353 us (0.970)
  waiting for transfers between devices: 29.5 us -> 23.9 us
  Pallas kernels: 239 us -> 234 us
    pallas_call x15 -> x14, Pallas kernels: 239 us -> 234 us  [call(): pl.pallas_call(body, in_specs=specs, compiler_params=params_of(), **rest)]
    ppermute x37, waiting for transfers between devices: 20.8 us -> 15.9 us  [row_swap(): lax.ppermute(values, 'row', [(index, index ^ step) for index in range(4)])]
    ppermute x24 -> x20, starting transfers between devices: 31.9 us -> 29 us  [tab_swap(): lax.ppermute(values, 'tab', [(index, index ^ step) for index in range(8)])]
    ppermute x24 -> x20, waiting for transfers between devices: 8.69 us -> 7.96 us  [tab_swap(): lax.ppermute(values, 'tab', [(index, index ^ step) for index in range(8)])]
  transfers between devices with their start and end apart: 61 -> 57, of which waited for: 11 -> 11; matrix products, arithmetic and copies ran while one was open for 7% -> 8% of each run, Pallas kernels for 65% -> 66%
where the time goes in v3:
time: 353 us; the launch traced here: 349 us
  Pallas kernels  234 us (66%)
  starting transfers between devices  56.5 us (16%)
  waiting for transfers between devices  23.9 us (7%)
  other arithmetic  21.6 us (6%)
  local copies, waits for them, and re-layouts  10.1 us (3%)
    pallas_call x14, Pallas kernels, call(): pl.pallas_call(body, in_specs=specs, compiler_params=params_of(), **rest)  234 us
    ppermute x20, starting transfers between devices, tab_swap(): lax.ppermute(values, 'tab', [(index, index ^ step) for index in range(8)])  29 us
    ppermute x37, starting transfers between devices, row_swap(): lax.ppermute(values, 'row', [(index, index ^ step) for index in range(4)])  27.5 us
    ppermute x37, waiting for transfers between devices, row_swap(): lax.ppermute(values, 'row', [(index, index ^ step) for index in range(4)])  15.9 us
    convert_element_type x9, other arithmetic, add(): return total.astype(BF16)  13.9 us
    ppermute x20, waiting for transfers between devices, tab_swap(): lax.ppermute(values, 'tab', [(index, index ^ step) for index in range(8)])  7.96 us
  transfers between devices with their start and end apart: 57, of which 11 were waited for; matrix products, arithmetic and copies ran while one was open for 8% of the time, Pallas kernels for 66%

profile of v3, /device:TPU:0, one launch (start us, length us, event | category | flops | bytes accessed | tf_op | source)
XLA Modules:
  0.0 348.7 jit_solution(12185371316270026468)
XLA Ops:
  0.7 1.8 split.1
  2.5 3.0 collective-permute-start
  5.5 17.8 %feat_forward.1 = (bf16[256,512]{1,0:T(8,128)(2,1)}, bf16[256,512]{1,0:T(8,128)(2,1)}, bf16[256,512]{1,0:T(8,128)(2,1)}, bf16[256,512]{1,0:T(8,128)(2,1)}, bf16[...) custom-call(s32[1]{0:T(128)} %bitcast.refs_0_, ...), custom_call_target="tpu_custom_call" | custom-call | flops 13500000256 | bytes 1024 | tf_op jit(solution)/shard_map/feat_forward/pallas_call | solution.py:479
  24.6 1.6 collective-permute-start.3
  26.4 1.6 collective-permute-start.10
  31.0 3.0 collective-permute-done.3.refs_4_.refs_9_
  34.0 4.9 %collective-permute-done.4.refs_5_.refs_10_ = bf16[256,512]{1,0:T(8,128)(2,1)S(1)} collective-permute-done((bf16[256,512]{1,0:T(8,128)(2,1)}, bf16[256,512]{1,0:T(8,128)(2,1)S(1)}, u32[]{:S(2)}, u32[]{:S(2)}) %collective-permute-start.4) | collective-permute-done | bytes 262176 | tf_op jit(solution)/shard_map/ppermute | solution.py:1238
  39.8 1.6 collective-permute-start.7
  42.3 32.6 %row_and_mlp.3 = (bf16[1024,512]{1,0:T(8,128)(2,1)}, bf16[1024,512]{1,0:T(8,128)(2,1)}, bf16[1024,512]{1,0:T(8,128)(2,1)}, bf16[1024,512]{1,0:T(8,128)(2,1)}, bf...) custom-call(s32[3]{0:T(128)} %pad_add_fusion.refs_0_, ...), custom_call_target="tpu_custom_call" | custom-call | flops 25200001024 | bytes 1024 | tf_op jit(solution)/shard_map/row_and_mlp/pallas_call | solution.py:479
  75.0 1.4 collective-permute-start.12
  78.6 33.3 %row_and_mlp.4 = (bf16[1024,512]{1,0:T(8,128)(2,1)}, bf16[1024,512]{1,0:T(8,128)(2,1)}, bf16[1024,512]{1,0:T(8,128)(2,1)}, bf16[1024,512]{1,0:T(8,128)(2,1)}, bf...) custom-call(s32[3]{0:T(128)} %pad_add_fusion.refs_0_, ...), custom_call_target="tpu_custom_call" | custom-call | flops 25200001024 | bytes 1024 | tf_op jit(solution)/shard_map/row_and_mlp/pallas_call | solution.py:479
  113.9 34.8 %row_and_mlp.5 = (bf16[1024,512]{1,0:T(8,128)(2,1)}, bf16[1024,512]{1,0:T(8,128)(2,1)}, bf16[1024,512]{1,0:T(8,128)(2,1)}, bf16[1024,512]{1,0:T(8,128)(2,1)}, bf...) custom-call(s32[3]{0:T(128)} %pad_add_fusion.refs_0_, ...), custom_call_target="tpu_custom_call" | custom-call | flops 25200001024 | bytes 1024 | tf_op jit(solution)/shard_map/row_and_mlp/pallas_call | solution.py:479
  151.3 2.9 collective-permute-done.24
  154.2 1.5 copy-done
  155.7 2.8 add_convert_fusion
  158.5 1.5 collective-permute-start.25
  160.0 17.6 %row_backward.3 = (bf16[256,512]{1,0:T(8,128)(2,1)}, bf16[256,512]{1,0:T(8,128)(2,1)}, bf16[256,512]{1,0:T(8,128)(2,1)}, bf16[256,512]{1,0:T(8,128)(2,1)}, bf16[...) custom-call(s32[3]{0:T(128)} %pad_add_fusion.refs_0_, ...), custom_call_target="tpu_custom_call" | custom-call | flops 13500000256 | bytes 1024 | tf_op jit(solution)/shard_map/row_backward/pallas_call | solution.py:479
  179.4 18.0 %row_backward.4 = (bf16[256,512]{1,0:T(8,128)(2,1)}, bf16[256,512]{1,0:T(8,128)(2,1)}, bf16[256,512]{1,0:T(8,128)(2,1)}, bf16[256,512]{1,0:T(8,128)(2,1)}, bf16[...) custom-call(s32[3]{0:T(128)} %pad_add_fusion.refs_0_, ...), custom_call_target="tpu_custom_call" | custom-call | flops 13500000256 | bytes 1024 | tf_op jit(solution)/shard_map/row_backward/pallas_call | solution.py:479
  199.3 3.3 add_convert_fusion.6
  202.7 1.6 collective-permute-start.28
  204.3 2.6 collective-permute-start.29
  207.0 18.1 %row_backward.5 = (bf16[256,512]{1,0:T(8,128)(2,1)}, bf16[256,512]{1,0:T(8,128)(2,1)}, bf16[256,512]{1,0:T(8,128)(2,1)}, bf16[256,512]{1,0:T(8,128)(2,1)}, bf16[...) custom-call(s32[3]{0:T(128)} %pad_add_fusion.refs_0_, ...), custom_call_target="tpu_custom_call" | custom-call | flops 13500000256 | bytes 1024 | tf_op jit(solution)/shard_map/row_backward/pallas_call | solution.py:479
  227.1 9.8 %row_weights.1 = (bf16[16,64,512]{2,1,0:T(8,128)(2,1)}, bf16[16,64,512]{2,1,0:T(8,128)(2,1)}) custom-call(s32[2]{0:T(128)} %pad_add_fusion.1.refs_1_.refs_0_, bf16[1024,512]{1,0:T(8,128)(2,1)} %get-tuple-element.279.refs_1_, bf16[1024,512]{1,0:T(8,128)(2,1)} %get-tuple-element.280.refs_2_, bf16[1024,512]{1,0:T(8,128)(2,1)} %get-tuple-element.281.refs_3_, ...), custom_call_target="tpu_custom_call" | custom-call | flops 7200000000 | bytes 1024 | tf_op jit(solution)/shard_map/row_weights/pallas_call | solution.py:479
  237.0 1.8 fusion.1
  245.6 29.4 %feat_backward.1 = (bf16[16,80,512]{2,1,0:T(8,128)(2,1)}, bf16[16,80,512]{2,1,0:T(8,128)(2,1)}, bf16[3072,512]{1,0:T(8,128)(2,1)}, bf16[3072,512]{1,0:T(8,128)(2,1)}, bf16[3072,512]{1,0:T(8,128)(2,1)}) custom-call(s32[2]{0:T(128)} %pad_add_fusion.1.refs_1_.refs_0_, bf16[12,256,512]{2,1,0:T(8,128)(2,1)} %bitcast.85, ...), custom_call_target="tpu_custom_call" | custom-call | flops 17999998976 | bytes 1024 | tf_op jit(solution)/shard_map/feat_backward/pallas_call | solution.py:479
  275.1 1.3 fusion
  277.3 3.5 collective-permute-start.43
  280.9 1.9 add_convert_fusion.8
  284.5 2.1 add_convert_fusion.1.refs_21_
  287.6 11.8 %cells_backward.1 = (bf16[12,256,512]{2,1,0:T(8,128)(2,1)}, f32[8,128]{1,0:T(8,128)}) custom-call(s32[1]{0:T(128)} %bitcast.refs_0_, bf16[12,256,512]{2,1,0:T(8,128)(2,1)} %bitcast.86, bf16[3072,512]{1,0:T(8,128)(2,1)} %get-tuple-element.307.refs_2_, bf16[3072,512]{1,0:T(8,128)(2,1)} %get-tuple-element.308.refs_3_, ...), custom_call_target="tpu_custom_call" | custom-call | flops 10800000000 | bytes 1024 | tf_op jit(solution)/shard_map/cells_backward/pallas_call | solution.py:479
  299.4 3.4 collective-permute-done.40
  304.0 1.6 collective-permute-start.45
  306.2 1.4 fusion.9
  308.2 3.5 %collective-permute-start.50 = (bf16[64,512]{1,0:T(8,128)(2,1)S(1)}, bf16[64,512]{1,0:T(8,128)(2,1)S(1)}, u32[]{:S(2)}, u32[]{:S(2)}) collective-permute-start(bf16[64,512]{1,0:T(8,128)(2,1)S(1)} %get-tuple-element.379), channel_id=1, source_target_pairs={{0,16},{4,20},{8,24},{12,28},{16,0},{20,4},{24,8},{28,12},{1,17},{... | collective-permute-start | bytes 196616 | tf_op jit(solution)/shard_map/ppermute | solution.py:1242
  312.1 1.3 fusion.5
  314.4 3.2 collective-permute-start.47
  319.0 1.7 collective-permute-start.56
  320.7 1.3 collective-permute-done.47
  322.1 1.9 collective-permute-done.48
  324.2 1.6 collective-permute-start.53
  325.8 2.7 collective-permute-start.54
  329.1 1.9 collective-permute-done.52
  331.0 2.7 collective-permute-done.53
  334.6 1.4 collective-permute-start.55
  337.0 3.7 %join_pieces.1 = bf16[12,256,512]{2,1,0:T(8,128)(2,1)} custom-call(s32[1]{0:T(128)} %bitcast.refs_0_, bf16[1,256,512]{2,1,0:T(8,128)(2,1)} %get-tuple-element.206.refs_1_, bf16[1,256,512]{2,1,0:T(8,128)(2,1)} %get-tuple-element.220.refs_2_, bf16[1,256,512]{2,1,0:T(8,128)(2,1)} %get-tuple-element.231.refs_3_, bf16[2,256,512]{2,1,0:T(8,128)(2,1)} %copy-done.8, ...), custom_call_target="tpu_custom_call" | custom-call | flops 1800000000 | bytes 1024 | tf_op jit(solution)/shard_map/join_pieces/pallas_call | solution.py:479
  340.7 2.8 finish.2
  343.5 2.5 copy.46
  346.1 2.5 finish.3
  (146 shorter events, 35.8 us)
Async XLA Ops:
  2.5 20.8 %collective-permute-start = (bf16[1,256,512]{2,1,0:T(8,128)(2,1)}, bf16[1,256,512]{2,1,0:T(8,128)(2,1)S(1)}, u32[]{:S(2)}, u32[]{:S(2)}) collective-permute-start(bf16[1,256,512]{2,1,0:T(8,128)(2,1)} %get-tuple-element.185.refs_10_), channel_id=1, source_target_pairs={{0,2},{1,3},{2,0},{3,1},{4,6},{5,7},{6,4},{7,5},{8,10},{9,11},{10,... | collective-permute-start | bytes 786440 | tf_op jit(solution)/shard_map/ppermute | solution.py:1238
  5.5 17.8 %collective-permute-start.1 = (bf16[1,256,512]{2,1,0:T(8,128)(2,1)}, bf16[1,256,512]{2,1,0:T(8,128)(2,1)S(1)}, u32[]{:S(2)}, u32[]{:S(2)}) collective-permute-start(bf16[1,256,512]{2,1,0:T(8,128)(2,1)} %get-tuple-element.194), channel_id=1, source_target_pairs={{0,3},{1,2},{2,1},{3,0},{4,7},{5,6},{6,5},{7,4},{8,11},{9,10},{10,... | collective-permute-start | bytes 786440 | tf_op jit(solution)/shard_map/ppermute | solution.py:1238
  24.1 17.3 %collective-permute-start.5 = (bf16[3,256,512]{2,1,0:T(8,128)(2,1)}, bf16[3,256,512]{2,1,0:T(8,128)(2,1)S(1)}, u32[]{:S(2)}, u32[]{:S(2)}) collective-permute-start(bf16[3,256,512]{2,1,0:T(8,128)(2,1)} %get-tuple-element.203), channel_id=1, source_target_pairs={{0,1},{1,0},{2,3},{3,2},{4,5},{5,4},{6,7},{7,6},{8,9},{9,8},{10,11... | collective-permute-start | bytes 2359304 | tf_op jit(solution)/shard_map/ppermute | solution.py:1238
  24.6 9.3 %collective-permute-start.3 = (bf16[256,512]{1,0:T(8,128)(2,1)}, bf16[256,512]{1,0:T(8,128)(2,1)S(1)}, u32[]{:S(2)}, u32[]{:S(2)}) collective-permute-start(bf16[256,512]{1,0:T(8,128)(2,1)} %get-tuple-element.196), channel_id=1, source_target_pairs={{0,2},{1,3},{2,0},{3,1},{4,6},{5,7},{6,4},{7,5},{8,10},{9,11},{10,... | collective-permute-start | bytes 786440 | tf_op jit(solution)/shard_map/ppermute | solution.py:1238
  26.3 12.6 %collective-permute-start.4 = (bf16[256,512]{1,0:T(8,128)(2,1)}, bf16[256,512]{1,0:T(8,128)(2,1)S(1)}, u32[]{:S(2)}, u32[]{:S(2)}) collective-permute-start(bf16[256,512]{1,0:T(8,128)(2,1)} %get-tuple-element.197), channel_id=1, source_target_pairs={{0,3},{1,2},{2,1},{3,0},{4,7},{5,6},{6,5},{7,4},{8,11},{9,10},{10,... | collective-permute-start | bytes 786440 | tf_op jit(solution)/shard_map/ppermute | solution.py:1238
  26.4 48.5 %collective-permute-start.10 = (bf16[1,256,512]{2,1,0:T(8,128)(2,1)}, bf16[1,256,512]{2,1,0:T(8,128)(2,1)}, u32[]{:S(2)}, u32[]{:S(2)}) collective-permute-start(bf16[1,256,512]{2,1,0:T(8,128)(2,1)} %get-tuple-element.212), channel_id=1, source_target_pairs={{0,3},{1,2},{2,1},{3,0},{4,7},{5,6},{6,5},{7,4},{8,11},{9,10},{10,... | collective-permute-start | bytes 786440 | tf_op jit(solution)/shard_map/ppermute | solution.py:1238
  30.6 44.5 %collective-permute-start.9 = (bf16[1,256,512]{2,1,0:T(8,128)(2,1)}, bf16[1,256,512]{2,1,0:T(8,128)(2,1)}, u32[]{:S(2)}, u32[]{:S(2)}) collective-permute-start(bf16[1,256,512]{2,1,0:T(8,128)(2,1)} %get-tuple-element.211), channel_id=1, source_target_pairs={{0,2},{1,3},{2,0},{3,1},{4,6},{5,7},{6,4},{7,5},{8,10},{9,11},{10,... | collective-permute-start | bytes 786440 | tf_op jit(solution)/shard_map/ppermute | solution.py:1238
  38.8 37.6 %collective-permute-start.6 = (bf16[256,512]{1,0:T(8,128)(2,1)}, bf16[256,512]{1,0:T(8,128)(2,1)}, u32[]{:S(2)}, u32[]{:S(2)}) collective-permute-start(bf16[256,512]{1,0:T(8,128)(2,1)} %get-tuple-element.208), channel_id=1, source_target_pairs={{0,1},{1,0},{2,3},{3,2},{4,5},{5,4},{6,7},{7,6},{8,9},{9,8},{10,11... | collective-permute-start | bytes 786440 | tf_op jit(solution)/shard_map/ppermute | solution.py:1238
  39.8 37.1 %collective-permute-start.7 = (bf16[256,512]{1,0:T(8,128)(2,1)}, bf16[256,512]{1,0:T(8,128)(2,1)}, u32[]{:S(2)}, u32[]{:S(2)}) collective-permute-start(bf16[256,512]{1,0:T(8,128)(2,1)} %get-tuple-element.209), channel_id=1, source_target_pairs={{0,2},{1,3},{2,0},{3,1},{4,6},{5,7},{6,4},{7,5},{8,10},{9,11},{10,... | collective-permute-start | bytes 786440 | tf_op jit(solution)/shard_map/ppermute | solution.py:1238
  41.4 36.4 %collective-permute-start.8 = (bf16[256,512]{1,0:T(8,128)(2,1)}, bf16[256,512]{1,0:T(8,128)(2,1)}, u32[]{:S(2)}, u32[]{:S(2)}) collective-permute-start(bf16[256,512]{1,0:T(8,128)(2,1)} %get-tuple-element.210), channel_id=1, source_target_pairs={{0,3},{1,2},{2,1},{3,0},{4,7},{5,6},{6,5},{7,4},{8,11},{9,10},{10,... | collective-permute-start | bytes 786440 | tf_op jit(solution)/shard_map/ppermute | solution.py:1238
  74.9 37.0 %collective-permute-start.11 = (bf16[256,512]{1,0:T(8,128)(2,1)}, bf16[256,512]{1,0:T(8,128)(2,1)S(1)}, u32[]{:S(2)}, u32[]{:S(2)}) collective-permute-start(bf16[256,512]{1,0:T(8,128)(2,1)} %get-tuple-element.222), channel_id=1, source_target_pairs={{0,1},{1,0},{2,3},{3,2},{4,5},{5,4},{6,7},{7,6},{8,9},{9,8},{10,11... | collective-permute-start | bytes 786440 | tf_op jit(solution)/shard_map/ppermute | solution.py:1238
  75.0 37.4 %collective-permute-start.12 = (bf16[256,512]{1,0:T(8,128)(2,1)}, bf16[256,512]{1,0:T(8,128)(2,1)}, u32[]{:S(2)}, u32[]{:S(2)}) collective-permute-start(bf16[256,512]{1,0:T(8,128)(2,1)} %get-tuple-element.223), channel_id=1, source_target_pairs={{0,2},{1,3},{2,0},{3,1},{4,6},{5,7},{6,4},{7,5},{8,10},{9,11},{10,... | collective-permute-start | bytes 786440 | tf_op jit(solution)/shard_map/ppermute | solution.py:1238
  76.4 37.0 %collective-permute-start.13 = (bf16[256,512]{1,0:T(8,128)(2,1)}, bf16[256,512]{1,0:T(8,128)(2,1)}, u32[]{:S(2)}, u32[]{:S(2)}) collective-permute-start(bf16[256,512]{1,0:T(8,128)(2,1)} %get-tuple-element.224), channel_id=1, source_target_pairs={{0,3},{1,2},{2,1},{3,0},{4,7},{5,6},{6,5},{7,4},{8,11},{9,10},{10,... | collective-permute-start | bytes 786440 | tf_op jit(solution)/shard_map/ppermute | solution.py:1238
  76.9 37.0 %collective-permute-start.14 = (bf16[1,256,512]{2,1,0:T(8,128)(2,1)}, bf16[1,256,512]{2,1,0:T(8,128)(2,1)}, u32[]{:S(2)}, u32[]{:S(2)}) collective-permute-start(bf16[1,256,512]{2,1,0:T(8,128)(2,1)} %get-tuple-element.225), channel_id=1, source_target_pairs={{0,2},{1,3},{2,0},{3,1},{4,6},{5,7},{6,4},{7,5},{8,10},{9,11},{10,... | collective-permute-start | bytes 786440 | tf_op jit(solution)/shard_map/ppermute | solution.py:1238
  77.9 36.0 %collective-permute-start.15 = (bf16[1,256,512]{2,1,0:T(8,128)(2,1)}, bf16[1,256,512]{2,1,0:T(8,128)(2,1)}, u32[]{:S(2)}, u32[]{:S(2)}) collective-permute-start(bf16[1,256,512]{2,1,0:T(8,128)(2,1)} %get-tuple-element.226), channel_id=1, source_target_pairs={{0,3},{1,2},{2,1},{3,0},{4,7},{5,6},{6,5},{7,4},{8,11},{9,10},{10,... | collective-permute-start | bytes 786440 | tf_op jit(solution)/shard_map/ppermute | solution.py:1238
  111.9 36.7 %collective-permute-start.16 = (bf16[2,256,512]{2,1,0:T(8,128)(2,1)}, bf16[2,256,512]{2,1,0:T(8,128)(2,1)S(1)}, u32[]{:S(2)}, u32[]{:S(2)}) collective-permute-start(bf16[2,256,512]{2,1,0:T(8,128)(2,1)} %get-tuple-element.233), channel_id=1, source_target_pairs={{0,1},{1,0},{2,3},{3,2},{4,5},{5,4},{6,7},{7,6},{8,9},{9,8},{10,11... | collective-permute-start | bytes 1572872 | tf_op jit(solution)/shard_map/ppermute | solution.py:1238
  112.4 36.2 %collective-permute-start.17 = (bf16[2,256,512]{2,1,0:T(8,128)(2,1)}, bf16[2,256,512]{2,1,0:T(8,128)(2,1)}, u32[]{:S(2)}, u32[]{:S(2)}) collective-permute-start(bf16[2,256,512]{2,1,0:T(8,128)(2,1)} %get-tuple-element.234), channel_id=1, source_target_pairs={{0,2},{1,3},{2,0},{3,1},{4,6},{5,7},{6,4},{7,5},{8,10},{9,11},{10,... | collective-permute-start | bytes 1572872 | tf_op jit(solution)/shard_map/ppermute | solution.py:1238
  113.4 35.3 %collective-permute-start.18 = (bf16[2,256,512]{2,1,0:T(8,128)(2,1)}, bf16[2,256,512]{2,1,0:T(8,128)(2,1)}, u32[]{:S(2)}, u32[]{:S(2)}) collective-permute-start(bf16[2,256,512]{2,1,0:T(8,128)(2,1)} %get-tuple-element.235), channel_id=1, source_target_pairs={{0,3},{1,2},{2,1},{3,0},{4,7},{5,6},{6,5},{7,4},{8,11},{9,10},{10,... | collective-permute-start | bytes 1572872 | tf_op jit(solution)/shard_map/ppermute | solution.py:1238
  149.5 29.3 %collective-permute-start.19 = (bf16[1,256,512]{2,1,0:T(8,128)(2,1)}, bf16[1,256,512]{2,1,0:T(8,128)(2,1)S(1)}, u32[]{:S(2)}, u32[]{:S(2)}) collective-permute-start(bf16[1,256,512]{2,1,0:T(8,128)(2,1)} %get-tuple-element.239), channel_id=1, source_target_pairs={{0,1},{1,0},{2,3},{3,2},{4,5},{5,4},{6,7},{7,6},{8,9},{9,8},{10,11... | collective-permute-start | bytes 786440 | tf_op jit(solution)/shard_map/ppermute | solution.py:1238
  149.5 29.6 %collective-permute-start.20 = (bf16[1,256,512]{2,1,0:T(8,128)(2,1)}, bf16[1,256,512]{2,1,0:T(8,128)(2,1)}, u32[]{:S(2)}, u32[]{:S(2)}) collective-permute-start(bf16[1,256,512]{2,1,0:T(8,128)(2,1)} %get-tuple-element.240), channel_id=1, source_target_pairs={{0,2},{1,3},{2,0},{3,1},{4,6},{5,7},{6,4},{7,5},{8,10},{9,11},{10,... | collective-permute-start | bytes 786440 | tf_op jit(solution)/shard_map/ppermute | solution.py:1238
  150.6 28.5 %collective-permute-start.21 = (bf16[1,256,512]{2,1,0:T(8,128)(2,1)}, bf16[1,256,512]{2,1,0:T(8,128)(2,1)}, u32[]{:S(2)}, u32[]{:S(2)}) collective-permute-start(bf16[1,256,512]{2,1,0:T(8,128)(2,1)} %get-tuple-element.241), channel_id=1, source_target_pairs={{0,3},{1,2},{2,1},{3,0},{4,7},{5,6},{6,5},{7,4},{8,11},{9,10},{10,... | collective-permute-start | bytes 786440 | tf_op jit(solution)/shard_map/ppermute | solution.py:1238
  158.5 40.9 %collective-permute-start.25 = (bf16[8,160,512]{2,1,0:T(8,128)(2,1)}, bf16[8,160,512]{2,1,0:T(8,128)(2,1)}, u32[]{:S(2)}, u32[]{:S(2)}) collective-permute-start(bf16[8,160,512]{2,1,0:T(8,128)(2,1)} %add_convert_fusion), channel_id=1, source_target_pairs={{0,4},{4,0},{8,12},{12,8},{16,20},{20,16},{24,28},{28,24},{1,5},{5... | collective-permute-start | bytes 3932168 | tf_op jit(solution)/shard_map/ppermute | solution.py:1242
  177.7 26.6 %collective-permute-start.22 = (bf16[256,512]{1,0:T(8,128)(2,1)}, bf16[256,512]{1,0:T(8,128)(2,1)}, u32[]{:S(2)}, u32[]{:S(2)}) collective-permute-start(bf16[256,512]{1,0:T(8,128)(2,1)} %get-tuple-element.272), channel_id=1, source_target_pairs={{0,2},{1,3},{2,0},{3,1},{4,6},{5,7},{6,4},{7,5},{8,10},{9,11},{10,... | collective-permute-start | bytes 786440 | tf_op jit(solution)/shard_map/ppermute | solution.py:1238
  178.7 28.1 %collective-permute-start.23 = (bf16[256,512]{1,0:T(8,128)(2,1)}, bf16[256,512]{1,0:T(8,128)(2,1)}, u32[]{:S(2)}, u32[]{:S(2)}) collective-permute-start(bf16[256,512]{1,0:T(8,128)(2,1)} %get-tuple-element.273), channel_id=1, source_target_pairs={{0,3},{1,2},{2,1},{3,0},{4,7},{5,6},{6,5},{7,4},{8,11},{9,10},{10,... | collective-permute-start | bytes 786440 | tf_op jit(solution)/shard_map/ppermute | solution.py:1238
  197.4 27.8 %collective-permute-start.31 = (bf16[256,512]{1,0:T(8,128)(2,1)}, bf16[256,512]{1,0:T(8,128)(2,1)}, u32[]{:S(2)}, u32[]{:S(2)}) collective-permute-start(bf16[256,512]{1,0:T(8,128)(2,1)} %get-tuple-element.292), channel_id=1, source_target_pairs={{0,2},{1,3},{2,0},{3,1},{4,6},{5,7},{6,4},{7,5},{8,10},{9,11},{10,... | collective-permute-start | bytes 786440 | tf_op jit(solution)/shard_map/ppermute | solution.py:1238
  198.5 26.8 %collective-permute-start.32 = (bf16[256,512]{1,0:T(8,128)(2,1)}, bf16[256,512]{1,0:T(8,128)(2,1)}, u32[]{:S(2)}, u32[]{:S(2)}) collective-permute-start(bf16[256,512]{1,0:T(8,128)(2,1)} %get-tuple-element.293), channel_id=1, source_target_pairs={{0,3},{1,2},{2,1},{3,0},{4,7},{5,6},{6,5},{7,4},{8,11},{9,10},{10,... | collective-permute-start | bytes 786440 | tf_op jit(solution)/shard_map/ppermute | solution.py:1238
  202.7 23.7 %collective-permute-start.28 = (bf16[2,160,512]{2,1,0:T(8,128)(2,1)S(1)}, bf16[2,160,512]{2,1,0:T(8,128)(2,1)}, u32[]{:S(2)}, u32[]{:S(2)}) collective-permute-start(bf16[2,160,512]{2,1,0:T(8,128)(2,1)S(1)} %get-tuple-element.370), channel_id=1, source_target_pairs={{0,8},{4,12},{8,0},{12,4},{16,24},{20,28},{24,16},{28,20},{1,9},{5... | collective-permute-start | bytes 983048 | tf_op jit(solution)/shard_map/ppermute | solution.py:1242
  204.3 32.7 %collective-permute-start.29 = (bf16[2,160,512]{2,1,0:T(8,128)(2,1)S(1)}, bf16[2,160,512]{2,1,0:T(8,128)(2,1)}, u32[]{:S(2)}, u32[]{:S(2)}) collective-permute-start(bf16[2,160,512]{2,1,0:T(8,128)(2,1)S(1)} %get-tuple-element.372), channel_id=1, source_target_pairs={{0,16},{4,20},{8,24},{12,28},{16,0},{20,4},{24,8},{28,12},{1,17},{... | collective-permute-start | bytes 983048 | tf_op jit(solution)/shard_map/ppermute | solution.py:1242
  206.9 30.1 %collective-permute-start.30 = (bf16[2,160,512]{2,1,0:T(8,128)(2,1)S(1)}, bf16[2,160,512]{2,1,0:T(8,128)(2,1)}, u32[]{:S(2)}, u32[]{:S(2)}) collective-permute-start(bf16[2,160,512]{2,1,0:T(8,128)(2,1)S(1)} %get-tuple-element.371), channel_id=1, source_target_pairs={{0,24},{4,28},{8,16},{12,20},{16,8},{20,12},{24,0},{28,4},{1,25},{... | collective-permute-start | bytes 983048 | tf_op jit(solution)/shard_map/ppermute | solution.py:1242
  225.2 13.6 %collective-permute-start.33 = (bf16[256,512]{1,0:T(8,128)(2,1)}, bf16[256,512]{1,0:T(8,128)(2,1)}, u32[]{:S(2)}, u32[]{:S(2)}) collective-permute-start(bf16[256,512]{1,0:T(8,128)(2,1)} %get-tuple-element.295), channel_id=1, source_target_pairs={{0,1},{1,0},{2,3},{3,2},{4,5},{5,4},{6,7},{7,6},{8,9},{9,8},{10,11... | collective-permute-start | bytes 786440 | tf_op jit(solution)/shard_map/ppermute | solution.py:1238
  225.3 13.6 %collective-permute-start.34 = (bf16[256,512]{1,0:T(8,128)(2,1)}, bf16[256,512]{1,0:T(8,128)(2,1)}, u32[]{:S(2)}, u32[]{:S(2)}) collective-permute-start(bf16[256,512]{1,0:T(8,128)(2,1)} %get-tuple-element.296), channel_id=1, source_target_pairs={{0,2},{1,3},{2,0},{3,1},{4,6},{5,7},{6,4},{7,5},{8,10},{9,11},{10,... | collective-permute-start | bytes 786440 | tf_op jit(solution)/shard_map/ppermute | solution.py:1238
  226.3 13.1 %collective-permute-start.35 = (bf16[256,512]{1,0:T(8,128)(2,1)}, bf16[256,512]{1,0:T(8,128)(2,1)}, u32[]{:S(2)}, u32[]{:S(2)}) collective-permute-start(bf16[256,512]{1,0:T(8,128)(2,1)} %get-tuple-element.297), channel_id=1, source_target_pairs={{0,3},{1,2},{2,1},{3,0},{4,7},{5,6},{6,5},{7,4},{8,11},{9,10},{10,... | collective-permute-start | bytes 786440 | tf_op jit(solution)/shard_map/ppermute | solution.py:1238
  240.2 34.8 %collective-permute-start.38 = (bf16[160,512]{1,0:T(8,128)(2,1)}, bf16[160,512]{1,0:T(8,128)(2,1)}, u32[]{:S(2)}, u32[]{:S(2)}) collective-permute-start(bf16[160,512]{1,0:T(8,128)(2,1)} %fusion.1), channel_id=1, source_target_pairs={{0,2},{1,3},{2,0},{3,1},{4,6},{5,7},{6,4},{7,5},{8,10},{9,11},{10,... | collective-permute-start | bytes 491528 | tf_op jit(solution)/shard_map/ppermute | solution.py:1238
  244.5 30.5 %collective-permute-start.37 = (bf16[8,64,512]{2,1,0:T(8,128)(2,1)S(1)}, bf16[8,64,512]{2,1,0:T(8,128)(2,1)}, u32[]{:S(2)}, u32[]{:S(2)}) collective-permute-start(bf16[8,64,512]{2,1,0:T(8,128)(2,1)S(1)} %add_convert_fusion.2.refs_25_), channel_id=1, source_target_pairs={{0,2},{1,3},{2,0},{3,1},{4,6},{5,7},{6,4},{7,5},{8,10},{9,11},{10,... | collective-permute-start | bytes 1572872 | tf_op jit(solution)/shard_map/ppermute | solution.py:1238
  275.0 9.5 %collective-permute-start.39 = (bf16[16,80,512]{2,1,0:T(8,128)(2,1)}, bf16[16,80,512]{2,1,0:T(8,128)(2,1)}, u32[]{:S(2)}, u32[]{:S(2)}) collective-permute-start(bf16[16,80,512]{2,1,0:T(8,128)(2,1)} %get-tuple-element.306), channel_id=1, source_target_pairs={{0,1},{1,0},{2,3},{3,2},{4,5},{5,4},{6,7},{7,6},{8,9},{9,8},{10,11... | collective-permute-start | bytes 3932168 | tf_op jit(solution)/shard_map/ppermute | solution.py:1238
  276.5 27.5 %collective-permute-start.42 = (bf16[144,512]{1,0:T(8,128)(2,1)S(1)}, bf16[144,512]{1,0:T(8,128)(2,1)S(1)}, u32[]{:S(2)}, u32[]{:S(2)}) collective-permute-start(bf16[144,512]{1,0:T(8,128)(2,1)S(1)} %slice.342), channel_id=1, source_target_pairs={{0,8},{4,12},{8,0},{12,4},{16,24},{20,28},{24,16},{28,20},{1,9},{5... | collective-permute-start | bytes 442376 | tf_op jit(solution)/shard_map/ppermute | solution.py:1242
  277.3 26.7 %collective-permute-start.43 = (bf16[144,512]{1,0:T(8,128)(2,1)S(1)}, bf16[144,512]{1,0:T(8,128)(2,1)}, u32[]{:S(2)}, u32[]{:S(2)}) collective-permute-start(bf16[144,512]{1,0:T(8,128)(2,1)S(1)} %slice.342), channel_id=1, source_target_pairs={{0,16},{4,20},{8,24},{12,28},{16,0},{20,4},{24,8},{28,12},{1,17},{... | collective-permute-start | bytes 442376 | tf_op jit(solution)/shard_map/ppermute | solution.py:1242
  280.8 23.3 %collective-permute-start.44 = (bf16[144,512]{1,0:T(8,128)(2,1)S(1)}, bf16[144,512]{1,0:T(8,128)(2,1)}, u32[]{:S(2)}, u32[]{:S(2)}) collective-permute-start(bf16[144,512]{1,0:T(8,128)(2,1)S(1)} %slice.342), channel_id=1, source_target_pairs={{0,24},{4,28},{8,16},{12,20},{16,8},{20,12},{24,0},{28,4},{1,25},{... | collective-permute-start | bytes 442376 | tf_op jit(solution)/shard_map/ppermute | solution.py:1242
  282.9 21.2 %collective-permute-start.41 = (bf16[4,64,512]{2,1,0:T(8,128)(2,1)}, bf16[4,64,512]{2,1,0:T(8,128)(2,1)}, u32[]{:S(2)}, u32[]{:S(2)}) collective-permute-start(bf16[4,64,512]{2,1,0:T(8,128)(2,1)} %add_convert_fusion.8), channel_id=1, source_target_pairs={{0,4},{4,0},{8,12},{12,8},{16,20},{20,16},{24,28},{28,24},{1,5},{5... | collective-permute-start | bytes 786440 | tf_op jit(solution)/shard_map/ppermute | solution.py:1242
  286.6 16.2 %collective-permute-start.40 = (bf16[8,80,512]{2,1,0:T(8,128)(2,1)}, bf16[8,80,512]{2,1,0:T(8,128)(2,1)S(1)}, u32[]{:S(2)}, u32[]{:S(2)}) collective-permute-start(bf16[8,80,512]{2,1,0:T(8,128)(2,1)} %add_convert_fusion.1.refs_21_), channel_id=1, source_target_pairs={{0,2},{1,3},{2,0},{3,1},{4,6},{5,7},{6,4},{7,5},{8,10},{9,11},{10,... | collective-permute-start | bytes 1966088 | tf_op jit(solution)/shard_map/ppermute | solution.py:1238
  304.0 8.1 %collective-permute-start.45 = (bf16[4,80,512]{2,1,0:T(8,128)(2,1)S(1)}, bf16[4,80,512]{2,1,0:T(8,128)(2,1)S(1)}, u32[]{:S(2)}, u32[]{:S(2)}) collective-permute-start(bf16[4,80,512]{2,1,0:T(8,128)(2,1)S(1)} %add_convert_fusion.3), channel_id=1, source_target_pairs={{0,4},{4,0},{8,12},{12,8},{16,20},{20,16},{24,28},{28,24},{1,5},{5... | collective-permute-start | bytes 983048 | tf_op jit(solution)/shard_map/ppermute | solution.py:1242
  307.6 10.1 %collective-permute-start.49 = (bf16[64,512]{1,0:T(8,128)(2,1)S(1)}, bf16[64,512]{1,0:T(8,128)(2,1)S(1)}, u32[]{:S(2)}, u32[]{:S(2)}) collective-permute-start(bf16[64,512]{1,0:T(8,128)(2,1)S(1)} %get-tuple-element.380), channel_id=1, source_target_pairs={{0,8},{4,12},{8,0},{12,4},{16,24},{20,28},{24,16},{28,20},{1,9},{5... | collective-permute-start | bytes 196616 | tf_op jit(solution)/shard_map/ppermute | solution.py:1242
  308.2 10.8 %collective-permute-start.50 = (bf16[64,512]{1,0:T(8,128)(2,1)S(1)}, bf16[64,512]{1,0:T(8,128)(2,1)S(1)}, u32[]{:S(2)}, u32[]{:S(2)}) collective-permute-start(bf16[64,512]{1,0:T(8,128)(2,1)S(1)} %get-tuple-element.379), channel_id=1, source_target_pairs={{0,16},{4,20},{8,24},{12,28},{16,0},{20,4},{24,8},{28,12},{1,17},{... | collective-permute-start | bytes 196616 | tf_op jit(solution)/shard_map/ppermute | solution.py:1242
  311.7 9.0 %collective-permute-start.51 = (bf16[64,512]{1,0:T(8,128)(2,1)S(1)}, bf16[64,512]{1,0:T(8,128)(2,1)S(1)}, u32[]{:S(2)}, u32[]{:S(2)}) collective-permute-start(bf16[64,512]{1,0:T(8,128)(2,1)S(1)} %get-tuple-element.378), channel_id=1, source_target_pairs={{0,24},{4,28},{8,16},{12,20},{16,8},{20,12},{24,0},{28,4},{1,25},{... | collective-permute-start | bytes 196616 | tf_op jit(solution)/shard_map/ppermute | solution.py:1242
  319.0 21.7 %collective-permute-start.56 = (bf16[4,144,512]{2,1,0:T(8,128)(2,1)S(1)}, bf16[4,144,512]{2,1,0:T(8,128)(2,1)}, u32[]{:S(2)}, u32[]{:S(2)}) collective-permute-start(bf16[4,144,512]{2,1,0:T(8,128)(2,1)S(1)} %pad_maximum_fusion.refs_1_), channel_id=1, source_target_pairs={{0,4},{4,0},{8,12},{12,8},{16,20},{20,16},{24,28},{28,24},{1,5},{5... | collective-permute-start | bytes 1769480 | tf_op jit(solution)/shard_map/ppermute | solution.py:1242
  324.2 9.5 %collective-permute-start.53 = (bf16[112,512]{1,0:T(8,128)(2,1)S(1)}, bf16[112,512]{1,0:T(8,128)(2,1)S(1)}, u32[]{:S(2)}, u32[]{:S(2)}) collective-permute-start(bf16[112,512]{1,0:T(8,128)(2,1)S(1)} %get-tuple-element.383), channel_id=1, source_target_pairs={{0,16},{4,20},{8,24},{12,28},{16,0},{20,4},{24,8},{28,12},{1,17},{... | collective-permute-start | bytes 344072 | tf_op jit(solution)/shard_map/ppermute | solution.py:1242
  325.8 7.9 %collective-permute-start.54 = (bf16[112,512]{1,0:T(8,128)(2,1)S(1)}, bf16[112,512]{1,0:T(8,128)(2,1)S(1)}, u32[]{:S(2)}, u32[]{:S(2)}) collective-permute-start(bf16[112,512]{1,0:T(8,128)(2,1)S(1)} %get-tuple-element.383), channel_id=1, source_target_pairs={{0,24},{4,28},{8,16},{12,20},{16,8},{20,12},{24,0},{28,4},{1,25},{... | collective-permute-start | bytes 344072 | tf_op jit(solution)/shard_map/ppermute | solution.py:1242
  334.6 11.5 %collective-permute-start.55 = (bf16[4,112,512]{2,1,0:T(8,128)(2,1)}, bf16[4,112,512]{2,1,0:T(8,128)(2,1)}, u32[]{:S(2)}, u32[]{:S(2)}) collective-permute-start(bf16[4,112,512]{2,1,0:T(8,128)(2,1)} %pad_maximum_fusion.1.refs_1_), channel_id=1, source_target_pairs={{0,4},{4,0},{8,12},{12,8},{16,20},{20,16},{24,28},{28,24},{1,5},{5... | collective-permute-start | bytes 1376264 | tf_op jit(solution)/shard_map/ppermute | solution.py:1242
  (25 other events, 167.1 us)

commit v4 on v3

--- a/solution.py
+++ b/solution.py
@@ -841,11 +841,17 @@
     probs = [jnp.exp2(score * SCALE) for score in scores]
     score_grads = [(prob * inner).astype(BF16) for prob, inner in zip(probs, inners)]
     for span, prob in zip(spans, probs):
-        value_all[head, span, :] = dot_nn(prob.astype(BF16), mixed_grad_ref[...]).astype(BF16)
+        found = dot_nn(prob.astype(BF16), mixed_grad_ref[...]).astype(BF16)
+        value_all[head, span, :] = found
+        d_value[span, :] = found
     for span, score_grad in zip(spans, score_grads):
-        key_all[head, span, :] = (dot_nn(score_grad, q_ref[...]) * SCORE).astype(BF16)
+        found = (dot_nn(score_grad, q_ref[...]) * SCORE).astype(BF16)
+        key_all[head, span, :] = found
+        d_key[span, :] = found
     query_sum[...] = dot_nn(k_ref[...].T, jnp.concatenate(score_grads, 0)).T
-    query_all[head] = (query_sum[...] * SCORE).astype(BF16)
+    found = (query_sum[...] * SCORE).astype(BF16)
+    query_all[head] = found
+    d_query[...] = found
 
     @pl.when(head == HEADS - 1)
     def _():
@@ -856,13 +862,8 @@
             span = slice(piece * rows, (piece + 1) * rows)
             unit, inverse = unit_of(after[span, :].astype(F32))
             upstream = None
-            for ref, weight, out in (
-                (query_all, w_query, d_query),
-                (key_all, w_key, d_key),
-                (value_all, w_value, d_value),
-            ):
+            for ref, weight in ((query_all, w_query), (key_all, w_key), (value_all, w_value)):
                 flat = jnp.concatenate([ref[index, span, :] for index in range(HEADS)], 1)
-                out[span, :] = flat
                 part = dot_nt(flat, weight[...])
                 upstream = part if upstream is None else upstream + part
             grad_a = grad[span, :] + norm_back(upstream, unit, inverse, gain[...])
@@ -890,7 +891,7 @@
         + [any_spec()] * (count + 1)
         + [fixed((1, width))]
         + [any_spec()] * 3,
-        out_specs=[fixed((rows, width))] * count + [fixed((full, width))] * 3 + [fixed((8, width))],
+        out_specs=[fixed((rows, width))] * count + [by_head] * 3 + [fixed((8, width))],
         out_shape=[shape_of((rows, width))] * count + [shape_of((full, width))] * 3 + [shape_of((8, width), F32)],
         scratch_shapes=[
             pltpu.VMEM((full, width), BF16),
@@ -1257,26 +1258,28 @@
     return lax.optimization_barrier((first, second))
 
 
-def finish_kernel(sizes, place_ref, near_ref, far_ref, *outs):
+def finish_kernel(sizes, sources, place_ref, *rest):
+    count = 1 + max(array for array, _ in sources)
+    refs, outs = rest[:count], rest[count:]
     at = 0
     for (rows, columns, turned), out in zip(sizes, outs):
         parts = columns // 512
-        for y, ref in ((0, near_ref), (1, far_ref)):
-            for z in range(4):
-                tab = place_ref[1] ^ (y + 2 * z)
-                for part in range(parts):
-                    block = ref[z, at + part * rows : at + (part + 1) * rows, :].astype(F32)
-                    span = pl.ds(pl.multiple_of(tab * rows, GROUP), rows)
-                    out[span, part * 512 : (part + 1) * 512] = block
+        for index, (array, place) in enumerate(sources):
+            tab = place_ref[1] ^ (index // 4 + 2 * (index % 4))
+            for part in range(parts):
+                block = refs[array][place, at + part * rows : at + (part + 1) * rows, :].astype(F32)
+                span = pl.ds(pl.multiple_of(tab * rows, GROUP), rows)
+                out[span, part * 512 : (part + 1) * 512] = block
         at += rows * parts
 
 
-def finish(place, near, far, sizes, waits=()):
+def finish(place, arrays, sizes, waits=()):
+    sources = tuple((index, at) for index, block in enumerate(arrays) for at in range(block.shape[0]))
     return call(
-        functools.partial(finish_kernel, sizes),
-        (place, near, far,),
+        functools.partial(finish_kernel, sizes, sources),
+        (place, *arrays),
         waits,
-        in_specs=[smem_spec(), vmem_spec(), vmem_spec()],
+        in_specs=[smem_spec()] + [vmem_spec()] * len(arrays),
         out_specs=[vmem_spec()] * len(sizes),
         out_shape=[shape_of((rows * 8, columns), F32) for rows, columns, _ in sizes],
         cost_estimate=cost_of(2),
@@ -1450,8 +1453,10 @@
     parts[1:] = [tab_swap(parts[z], 2 * z) for z in range(1, 4)]
     parts, row_parts = tie(parts, row_parts)
     row_own, feat_own = add(*row_parts), add(*parts)
-    near = jnp.stack(gather_near(jnp.concatenate([row_own[:-GROUP], feat_own[:-GROUP]], 0)))
-    far = tab_swap(near, 1)
+    own_piece, *others = gather_near(jnp.concatenate([row_own[:-GROUP], feat_own[:-GROUP]], 0))
+    far_own = tab_swap(own_piece, 1)
+    others = jnp.stack(others)
+    back = (own_piece[None], others, far_own[None], tab_swap(others, 1))
     mlp_vec, row_vec, feat_vec = mlp_own[-GROUP:], row_own[-GROUP:], feat_own[-GROUP:]
     blocks = [(0, j, part) for j, part in enumerate(own_layers)]
     blocks += [(k, 0, part) for k, part in enumerate(early, 1)]
@@ -1460,13 +1465,12 @@
 
     up_sum, down_sum, row_out_sum = finish(
         place,
-        mlp_near,
-        mlp_far,
+        (mlp_near, mlp_far),
         ((GROUP, 2048, False), (4 * GROUP, 512, True), (GROUP, 512, False)),
         (feat_own,),
     )
     small = ((GROUP, 512, False),) * 7
-    sum_rq, sum_rk, sum_rv, sum_fq, sum_fk, sum_fv, sum_fo = finish(place, near, far, small, (mark, row_out_sum))
+    sum_rq, sum_rk, sum_rv, sum_fq, sum_fk, sum_fv, sum_fo = finish(place, back, small, (mark, row_out_sum))
 
     mlp_vec, row_vec, feat_vec = (part.astype(F32) for part in (mlp_vec, row_vec, feat_vec))
     rows = sum_fq.shape[0]

time: 353 us -> 349 us (0.989)
    ppermute x20 -> x21, waiting for transfers between devices: 7.96 us -> 5.77 us  [tab_swap(): lax.ppermute(values, 'tab', [(index, index ^ step) for index in range(8)])]
    ppermute x20 -> x21, starting transfers between devices: 29 us -> 30.3 us  [tab_swap(): lax.ppermute(values, 'tab', [(index, index ^ step) for index in range(8)])]
  transfers between devices with their start and end apart: 57 -> 58, of which waited for: 11 -> 10; matrix products, arithmetic and copies ran while one was open for 8% -> 8% of each run, Pallas kernels for 66% -> 66%
where the time goes in v4:
time: 349 us; the launch traced here: 345 us
  Pallas kernels  231 us (66%)
  starting transfers between devices  57.7 us (17%)
  waiting for transfers between devices  21.7 us (6%)
  other arithmetic  21.5 us (6%)
  local copies, waits for them, and re-layouts  10.1 us (3%)
    pallas_call x14, Pallas kernels, call(): pl.pallas_call(body, in_specs=specs, compiler_params=params_of(), **rest)  231 us
    ppermute x21, starting transfers between devices, tab_swap(): lax.ppermute(values, 'tab', [(index, index ^ step) for index in range(8)])  30.3 us
    ppermute x37, starting transfers between devices, row_swap(): lax.ppermute(values, 'row', [(index, index ^ step) for index in range(4)])  27.4 us
    ppermute x37, waiting for transfers between devices, row_swap(): lax.ppermute(values, 'row', [(index, index ^ step) for index in range(4)])  15.9 us
    convert_element_type x9, other arithmetic, add(): return total.astype(BF16)  13.9 us
  transfers between devices with their start and end apart: 58, of which 10 were waited for; matrix products, arithmetic and copies ran while one was open for 8% of the time, Pallas kernels for 66%

profile of v4, /device:TPU:0, one launch (start us, length us, event | category | flops | bytes accessed | tf_op | source)
XLA Modules:
  0.0 344.7 jit_solution(16611941532259484454)
XLA Ops:
  0.7 1.8 split.1
  2.5 3.0 collective-permute-start
  5.5 17.8 %feat_forward.1 = (bf16[256,512]{1,0:T(8,128)(2,1)}, bf16[256,512]{1,0:T(8,128)(2,1)}, bf16[256,512]{1,0:T(8,128)(2,1)}, bf16[256,512]{1,0:T(8,128)(2,1)}, bf16[...) custom-call(s32[1]{0:T(128)} %bitcast.refs_0_, ...), custom_call_target="tpu_custom_call" | custom-call | flops 13500000256 | bytes 1024 | tf_op jit(solution)/shard_map/feat_forward/pallas_call | solution.py:479
  24.7 1.6 collective-permute-start.3
  26.4 1.6 collective-permute-start.10
  31.0 3.0 collective-permute-done.3.refs_4_.refs_9_
  34.0 4.9 %collective-permute-done.4.refs_5_.refs_10_ = bf16[256,512]{1,0:T(8,128)(2,1)S(1)} collective-permute-done((bf16[256,512]{1,0:T(8,128)(2,1)}, bf16[256,512]{1,0:T(8,128)(2,1)S(1)}, u32[]{:S(2)}, u32[]{:S(2)}) %collective-permute-start.4) | collective-permute-done | bytes 262176 | tf_op jit(solution)/shard_map/ppermute | solution.py:1239
  39.8 1.6 collective-permute-start.7
  42.4 32.6 %row_and_mlp.3 = (bf16[1024,512]{1,0:T(8,128)(2,1)}, bf16[1024,512]{1,0:T(8,128)(2,1)}, bf16[1024,512]{1,0:T(8,128)(2,1)}, bf16[1024,512]{1,0:T(8,128)(2,1)}, bf...) custom-call(s32[3]{0:T(128)} %pad_add_fusion.refs_0_, ...), custom_call_target="tpu_custom_call" | custom-call | flops 25200001024 | bytes 1024 | tf_op jit(solution)/shard_map/row_and_mlp/pallas_call | solution.py:479
  75.1 1.4 collective-permute-start.12
  78.7 33.3 %row_and_mlp.4 = (bf16[1024,512]{1,0:T(8,128)(2,1)}, bf16[1024,512]{1,0:T(8,128)(2,1)}, bf16[1024,512]{1,0:T(8,128)(2,1)}, bf16[1024,512]{1,0:T(8,128)(2,1)}, bf...) custom-call(s32[3]{0:T(128)} %pad_add_fusion.refs_0_, ...), custom_call_target="tpu_custom_call" | custom-call | flops 25200001024 | bytes 1024 | tf_op jit(solution)/shard_map/row_and_mlp/pallas_call | solution.py:479
  113.9 34.8 %row_and_mlp.5 = (bf16[1024,512]{1,0:T(8,128)(2,1)}, bf16[1024,512]{1,0:T(8,128)(2,1)}, bf16[1024,512]{1,0:T(8,128)(2,1)}, bf16[1024,512]{1,0:T(8,128)(2,1)}, bf...) custom-call(s32[3]{0:T(128)} %pad_add_fusion.refs_0_, ...), custom_call_target="tpu_custom_call" | custom-call | flops 25200001024 | bytes 1024 | tf_op jit(solution)/shard_map/row_and_mlp/pallas_call | solution.py:479
  151.4 2.9 collective-permute-done.24
  154.3 1.5 copy-done
  155.7 2.8 add_convert_fusion
  158.5 1.5 collective-permute-start.25
  160.0 16.7 %row_backward.3 = (bf16[256,512]{1,0:T(8,128)(2,1)}, bf16[256,512]{1,0:T(8,128)(2,1)}, bf16[256,512]{1,0:T(8,128)(2,1)}, bf16[256,512]{1,0:T(8,128)(2,1)}, bf16[...) custom-call(s32[3]{0:T(128)} %pad_add_fusion.refs_0_, ...), custom_call_target="tpu_custom_call" | custom-call | flops 13500000256 | bytes 1024 | tf_op jit(solution)/shard_map/row_backward/pallas_call | solution.py:479
  178.5 16.8 %row_backward.4 = (bf16[256,512]{1,0:T(8,128)(2,1)}, bf16[256,512]{1,0:T(8,128)(2,1)}, bf16[256,512]{1,0:T(8,128)(2,1)}, bf16[256,512]{1,0:T(8,128)(2,1)}, bf16[...) custom-call(s32[3]{0:T(128)} %pad_add_fusion.refs_0_, ...), custom_call_target="tpu_custom_call" | custom-call | flops 13500000256 | bytes 1024 | tf_op jit(solution)/shard_map/row_backward/pallas_call | solution.py:479
  197.3 3.3 add_convert_fusion.6
  200.6 1.6 collective-permute-start.28
  202.2 2.6 collective-permute-start.29
  205.0 17.0 %row_backward.5 = (bf16[256,512]{1,0:T(8,128)(2,1)}, bf16[256,512]{1,0:T(8,128)(2,1)}, bf16[256,512]{1,0:T(8,128)(2,1)}, bf16[256,512]{1,0:T(8,128)(2,1)}, bf16[...) custom-call(s32[3]{0:T(128)} %pad_add_fusion.refs_0_, ...), custom_call_target="tpu_custom_call" | custom-call | flops 13500000256 | bytes 1024 | tf_op jit(solution)/shard_map/row_backward/pallas_call | solution.py:479
  224.0 9.8 %row_weights.1 = (bf16[16,64,512]{2,1,0:T(8,128)(2,1)}, bf16[16,64,512]{2,1,0:T(8,128)(2,1)}) custom-call(s32[2]{0:T(128)} %pad_add_fusion.1.refs_1_.refs_0_, bf16[1024,512]{1,0:T(8,128)(2,1)} %get-tuple-element.279.refs_1_, bf16[1024,512]{1,0:T(8,128)(2,1)} %get-tuple-element.280.refs_2_, bf16[1024,512]{1,0:T(8,128)(2,1)} %get-tuple-element.281.refs_3_, ...), custom_call_target="tpu_custom_call" | custom-call | flops 7200000000 | bytes 1024 | tf_op jit(solution)/shard_map/row_weights/pallas_call | solution.py:479
  233.9 1.8 fusion.1
  242.4 29.5 %feat_backward.1 = (bf16[16,80,512]{2,1,0:T(8,128)(2,1)}, bf16[16,80,512]{2,1,0:T(8,128)(2,1)}, bf16[3072,512]{1,0:T(8,128)(2,1)}, bf16[3072,512]{1,0:T(8,128)(2,1)}, bf16[3072,512]{1,0:T(8,128)(2,1)}) custom-call(s32[2]{0:T(128)} %pad_add_fusion.1.refs_1_.refs_0_, bf16[12,256,512]{2,1,0:T(8,128)(2,1)} %bitcast.86, ...), custom_call_target="tpu_custom_call" | custom-call | flops 17999998976 | bytes 1024 | tf_op jit(solution)/shard_map/feat_backward/pallas_call | solution.py:479
  272.0 1.3 fusion
  274.2 3.5 %collective-permute-start.43 = (bf16[144,512]{1,0:T(8,128)(2,1)S(1)}, bf16[144,512]{1,0:T(8,128)(2,1)}, u32[]{:S(2)}, u32[]{:S(2)}) collective-permute-start(bf16[144,512]{1,0:T(8,128)(2,1)S(1)} %slice.342), channel_id=1, source_target_pairs={{0,16},{4,20},{8,24},{12,28},{16,0},{20,4},{24,8},{28,12},{1,17},{... | collective-permute-start | bytes 442376 | tf_op jit(solution)/shard_map/ppermute | solution.py:1243
  277.8 1.9 add_convert_fusion.8
  281.4 2.1 add_convert_fusion.1.refs_21_
  284.5 11.7 %cells_backward.1 = (bf16[12,256,512]{2,1,0:T(8,128)(2,1)}, f32[8,128]{1,0:T(8,128)}) custom-call(s32[1]{0:T(128)} %bitcast.refs_0_, bf16[12,256,512]{2,1,0:T(8,128)(2,1)} %bitcast.87, bf16[3072,512]{1,0:T(8,128)(2,1)} %get-tuple-element.307.refs_2_, bf16[3072,512]{1,0:T(8,128)(2,1)} %get-tuple-element.308.refs_3_, ...), custom_call_target="tpu_custom_call" | custom-call | flops 10800000000 | bytes 1024 | tf_op jit(solution)/shard_map/cells_backward/pallas_call | solution.py:479
  296.3 3.4 collective-permute-done.40
  299.7 1.2 add_convert_fusion.3
  300.9 1.6 collective-permute-start.45
  303.1 1.4 fusion.9
  305.1 3.5 %collective-permute-start.50 = (bf16[64,512]{1,0:T(8,128)(2,1)S(1)}, bf16[64,512]{1,0:T(8,128)(2,1)S(1)}, u32[]{:S(2)}, u32[]{:S(2)}) collective-permute-start(bf16[64,512]{1,0:T(8,128)(2,1)S(1)} %get-tuple-element.379), channel_id=1, source_target_pairs={{0,16},{4,20},{8,24},{12,28},{16,0},{20,4},{24,8},{28,12},{1,17},{... | collective-permute-start | bytes 196616 | tf_op jit(solution)/shard_map/ppermute | solution.py:1243
  309.1 1.3 fusion.5
  311.3 3.2 collective-permute-start.47
  315.9 1.7 collective-permute-start.57
  317.6 1.3 collective-permute-done.47
  318.9 1.8 collective-permute-done.48
  321.6 1.7 collective-permute-start.53
  323.3 2.7 collective-permute-start.54
  326.0 1.8 collective-permute-start.55
  328.9 2.4 collective-permute-done.53
  332.9 3.7 %join_pieces.1 = bf16[12,256,512]{2,1,0:T(8,128)(2,1)} custom-call(s32[1]{0:T(128)} %bitcast.refs_0_, bf16[1,256,512]{2,1,0:T(8,128)(2,1)} %get-tuple-element.206.refs_1_, bf16[1,256,512]{2,1,0:T(8,128)(2,1)} %get-tuple-element.220.refs_2_, bf16[1,256,512]{2,1,0:T(8,128)(2,1)} %get-tuple-element.231.refs_3_, bf16[2,256,512]{2,1,0:T(8,128)(2,1)} %copy-done.9, ...), custom_call_target="tpu_custom_call" | custom-call | flops 1800000000 | bytes 1024 | tf_op jit(solution)/shard_map/join_pieces/pallas_call | solution.py:479
  336.6 2.8 finish.2
  339.4 2.5 copy.46
  341.9 2.5 finish.3
  (150 shorter events, 35.4 us)
Async XLA Ops:
  2.5 20.8 %collective-permute-start = (bf16[1,256,512]{2,1,0:T(8,128)(2,1)}, bf16[1,256,512]{2,1,0:T(8,128)(2,1)S(1)}, u32[]{:S(2)}, u32[]{:S(2)}) collective-permute-start(bf16[1,256,512]{2,1,0:T(8,128)(2,1)} %get-tuple-element.185.refs_10_), channel_id=1, source_target_pairs={{0,2},{1,3},{2,0},{3,1},{4,6},{5,7},{6,4},{7,5},{8,10},{9,11},{10,... | collective-permute-start | bytes 786440 | tf_op jit(solution)/shard_map/ppermute | solution.py:1239
  5.5 17.8 %collective-permute-start.1 = (bf16[1,256,512]{2,1,0:T(8,128)(2,1)}, bf16[1,256,512]{2,1,0:T(8,128)(2,1)S(1)}, u32[]{:S(2)}, u32[]{:S(2)}) collective-permute-start(bf16[1,256,512]{2,1,0:T(8,128)(2,1)} %get-tuple-element.194), channel_id=1, source_target_pairs={{0,3},{1,2},{2,1},{3,0},{4,7},{5,6},{6,5},{7,4},{8,11},{9,10},{10,... | collective-permute-start | bytes 786440 | tf_op jit(solution)/shard_map/ppermute | solution.py:1239
  24.1 17.3 %collective-permute-start.5 = (bf16[3,256,512]{2,1,0:T(8,128)(2,1)}, bf16[3,256,512]{2,1,0:T(8,128)(2,1)S(1)}, u32[]{:S(2)}, u32[]{:S(2)}) collective-permute-start(bf16[3,256,512]{2,1,0:T(8,128)(2,1)} %get-tuple-element.203), channel_id=1, source_target_pairs={{0,1},{1,0},{2,3},{3,2},{4,5},{5,4},{6,7},{7,6},{8,9},{9,8},{10,11... | collective-permute-start | bytes 2359304 | tf_op jit(solution)/shard_map/ppermute | solution.py:1239
  24.7 9.3 %collective-permute-start.3 = (bf16[256,512]{1,0:T(8,128)(2,1)}, bf16[256,512]{1,0:T(8,128)(2,1)S(1)}, u32[]{:S(2)}, u32[]{:S(2)}) collective-permute-start(bf16[256,512]{1,0:T(8,128)(2,1)} %get-tuple-element.196), channel_id=1, source_target_pairs={{0,2},{1,3},{2,0},{3,1},{4,6},{5,7},{6,4},{7,5},{8,10},{9,11},{10,... | collective-permute-start | bytes 786440 | tf_op jit(solution)/shard_map/ppermute | solution.py:1239
  26.3 12.6 %collective-permute-start.4 = (bf16[256,512]{1,0:T(8,128)(2,1)}, bf16[256,512]{1,0:T(8,128)(2,1)S(1)}, u32[]{:S(2)}, u32[]{:S(2)}) collective-permute-start(bf16[256,512]{1,0:T(8,128)(2,1)} %get-tuple-element.197), channel_id=1, source_target_pairs={{0,3},{1,2},{2,1},{3,0},{4,7},{5,6},{6,5},{7,4},{8,11},{9,10},{10,... | collective-permute-start | bytes 786440 | tf_op jit(solution)/shard_map/ppermute | solution.py:1239
  26.4 48.5 %collective-permute-start.10 = (bf16[1,256,512]{2,1,0:T(8,128)(2,1)}, bf16[1,256,512]{2,1,0:T(8,128)(2,1)}, u32[]{:S(2)}, u32[]{:S(2)}) collective-permute-start(bf16[1,256,512]{2,1,0:T(8,128)(2,1)} %get-tuple-element.212), channel_id=1, source_target_pairs={{0,3},{1,2},{2,1},{3,0},{4,7},{5,6},{6,5},{7,4},{8,11},{9,10},{10,... | collective-permute-start | bytes 786440 | tf_op jit(solution)/shard_map/ppermute | solution.py:1239
  30.6 44.5 %collective-permute-start.9 = (bf16[1,256,512]{2,1,0:T(8,128)(2,1)}, bf16[1,256,512]{2,1,0:T(8,128)(2,1)}, u32[]{:S(2)}, u32[]{:S(2)}) collective-permute-start(bf16[1,256,512]{2,1,0:T(8,128)(2,1)} %get-tuple-element.211), channel_id=1, source_target_pairs={{0,2},{1,3},{2,0},{3,1},{4,6},{5,7},{6,4},{7,5},{8,10},{9,11},{10,... | collective-permute-start | bytes 786440 | tf_op jit(solution)/shard_map/ppermute | solution.py:1239
  38.9 37.6 %collective-permute-start.6 = (bf16[256,512]{1,0:T(8,128)(2,1)}, bf16[256,512]{1,0:T(8,128)(2,1)}, u32[]{:S(2)}, u32[]{:S(2)}) collective-permute-start(bf16[256,512]{1,0:T(8,128)(2,1)} %get-tuple-element.208), channel_id=1, source_target_pairs={{0,1},{1,0},{2,3},{3,2},{4,5},{5,4},{6,7},{7,6},{8,9},{9,8},{10,11... | collective-permute-start | bytes 786440 | tf_op jit(solution)/shard_map/ppermute | solution.py:1239
  39.8 37.1 %collective-permute-start.7 = (bf16[256,512]{1,0:T(8,128)(2,1)}, bf16[256,512]{1,0:T(8,128)(2,1)}, u32[]{:S(2)}, u32[]{:S(2)}) collective-permute-start(bf16[256,512]{1,0:T(8,128)(2,1)} %get-tuple-element.209), channel_id=1, source_target_pairs={{0,2},{1,3},{2,0},{3,1},{4,6},{5,7},{6,4},{7,5},{8,10},{9,11},{10,... | collective-permute-start | bytes 786440 | tf_op jit(solution)/shard_map/ppermute | solution.py:1239
  41.5 36.4 %collective-permute-start.8 = (bf16[256,512]{1,0:T(8,128)(2,1)}, bf16[256,512]{1,0:T(8,128)(2,1)}, u32[]{:S(2)}, u32[]{:S(2)}) collective-permute-start(bf16[256,512]{1,0:T(8,128)(2,1)} %get-tuple-element.210), channel_id=1, source_target_pairs={{0,3},{1,2},{2,1},{3,0},{4,7},{5,6},{6,5},{7,4},{8,11},{9,10},{10,... | collective-permute-start | bytes 786440 | tf_op jit(solution)/shard_map/ppermute | solution.py:1239
  75.0 36.9 %collective-permute-start.11 = (bf16[256,512]{1,0:T(8,128)(2,1)}, bf16[256,512]{1,0:T(8,128)(2,1)S(1)}, u32[]{:S(2)}, u32[]{:S(2)}) collective-permute-start(bf16[256,512]{1,0:T(8,128)(2,1)} %get-tuple-element.222), channel_id=1, source_target_pairs={{0,1},{1,0},{2,3},{3,2},{4,5},{5,4},{6,7},{7,6},{8,9},{9,8},{10,11... | collective-permute-start | bytes 786440 | tf_op jit(solution)/shard_map/ppermute | solution.py:1239
  75.1 37.4 %collective-permute-start.12 = (bf16[256,512]{1,0:T(8,128)(2,1)}, bf16[256,512]{1,0:T(8,128)(2,1)}, u32[]{:S(2)}, u32[]{:S(2)}) collective-permute-start(bf16[256,512]{1,0:T(8,128)(2,1)} %get-tuple-element.223), channel_id=1, source_target_pairs={{0,2},{1,3},{2,0},{3,1},{4,6},{5,7},{6,4},{7,5},{8,10},{9,11},{10,... | collective-permute-start | bytes 786440 | tf_op jit(solution)/shard_map/ppermute | solution.py:1239
  76.5 37.0 %collective-permute-start.13 = (bf16[256,512]{1,0:T(8,128)(2,1)}, bf16[256,512]{1,0:T(8,128)(2,1)}, u32[]{:S(2)}, u32[]{:S(2)}) collective-permute-start(bf16[256,512]{1,0:T(8,128)(2,1)} %get-tuple-element.224), channel_id=1, source_target_pairs={{0,3},{1,2},{2,1},{3,0},{4,7},{5,6},{6,5},{7,4},{8,11},{9,10},{10,... | collective-permute-start | bytes 786440 | tf_op jit(solution)/shard_map/ppermute | solution.py:1239
  76.9 37.0 %collective-permute-start.14 = (bf16[1,256,512]{2,1,0:T(8,128)(2,1)}, bf16[1,256,512]{2,1,0:T(8,128)(2,1)}, u32[]{:S(2)}, u32[]{:S(2)}) collective-permute-start(bf16[1,256,512]{2,1,0:T(8,128)(2,1)} %get-tuple-element.225), channel_id=1, source_target_pairs={{0,2},{1,3},{2,0},{3,1},{4,6},{5,7},{6,4},{7,5},{8,10},{9,11},{10,... | collective-permute-start | bytes 786440 | tf_op jit(solution)/shard_map/ppermute | solution.py:1239
  77.9 36.0 %collective-permute-start.15 = (bf16[1,256,512]{2,1,0:T(8,128)(2,1)}, bf16[1,256,512]{2,1,0:T(8,128)(2,1)}, u32[]{:S(2)}, u32[]{:S(2)}) collective-permute-start(bf16[1,256,512]{2,1,0:T(8,128)(2,1)} %get-tuple-element.226), channel_id=1, source_target_pairs={{0,3},{1,2},{2,1},{3,0},{4,7},{5,6},{6,5},{7,4},{8,11},{9,10},{10,... | collective-permute-start | bytes 786440 | tf_op jit(solution)/shard_map/ppermute | solution.py:1239
  112.0 36.8 %collective-permute-start.16 = (bf16[2,256,512]{2,1,0:T(8,128)(2,1)}, bf16[2,256,512]{2,1,0:T(8,128)(2,1)S(1)}, u32[]{:S(2)}, u32[]{:S(2)}) collective-permute-start(bf16[2,256,512]{2,1,0:T(8,128)(2,1)} %get-tuple-element.233), channel_id=1, source_target_pairs={{0,1},{1,0},{2,3},{3,2},{4,5},{5,4},{6,7},{7,6},{8,9},{9,8},{10,11... | collective-permute-start | bytes 1572872 | tf_op jit(solution)/shard_map/ppermute | solution.py:1239
  112.5 36.3 %collective-permute-start.17 = (bf16[2,256,512]{2,1,0:T(8,128)(2,1)}, bf16[2,256,512]{2,1,0:T(8,128)(2,1)}, u32[]{:S(2)}, u32[]{:S(2)}) collective-permute-start(bf16[2,256,512]{2,1,0:T(8,128)(2,1)} %get-tuple-element.234), channel_id=1, source_target_pairs={{0,2},{1,3},{2,0},{3,1},{4,6},{5,7},{6,4},{7,5},{8,10},{9,11},{10,... | collective-permute-start | bytes 1572872 | tf_op jit(solution)/shard_map/ppermute | solution.py:1239
  113.4 35.3 %collective-permute-start.18 = (bf16[2,256,512]{2,1,0:T(8,128)(2,1)}, bf16[2,256,512]{2,1,0:T(8,128)(2,1)}, u32[]{:S(2)}, u32[]{:S(2)}) collective-permute-start(bf16[2,256,512]{2,1,0:T(8,128)(2,1)} %get-tuple-element.235), channel_id=1, source_target_pairs={{0,3},{1,2},{2,1},{3,0},{4,7},{5,6},{6,5},{7,4},{8,11},{9,10},{10,... | collective-permute-start | bytes 1572872 | tf_op jit(solution)/shard_map/ppermute | solution.py:1239
  149.5 28.3 %collective-permute-start.19 = (bf16[1,256,512]{2,1,0:T(8,128)(2,1)}, bf16[1,256,512]{2,1,0:T(8,128)(2,1)S(1)}, u32[]{:S(2)}, u32[]{:S(2)}) collective-permute-start(bf16[1,256,512]{2,1,0:T(8,128)(2,1)} %get-tuple-element.239), channel_id=1, source_target_pairs={{0,1},{1,0},{2,3},{3,2},{4,5},{5,4},{6,7},{7,6},{8,9},{9,8},{10,11... | collective-permute-start | bytes 786440 | tf_op jit(solution)/shard_map/ppermute | solution.py:1239
  149.6 28.6 %collective-permute-start.20 = (bf16[1,256,512]{2,1,0:T(8,128)(2,1)}, bf16[1,256,512]{2,1,0:T(8,128)(2,1)}, u32[]{:S(2)}, u32[]{:S(2)}) collective-permute-start(bf16[1,256,512]{2,1,0:T(8,128)(2,1)} %get-tuple-element.240), channel_id=1, source_target_pairs={{0,2},{1,3},{2,0},{3,1},{4,6},{5,7},{6,4},{7,5},{8,10},{9,11},{10,... | collective-permute-start | bytes 786440 | tf_op jit(solution)/shard_map/ppermute | solution.py:1239
  150.7 27.6 %collective-permute-start.21 = (bf16[1,256,512]{2,1,0:T(8,128)(2,1)}, bf16[1,256,512]{2,1,0:T(8,128)(2,1)}, u32[]{:S(2)}, u32[]{:S(2)}) collective-permute-start(bf16[1,256,512]{2,1,0:T(8,128)(2,1)} %get-tuple-element.241), channel_id=1, source_target_pairs={{0,3},{1,2},{2,1},{3,0},{4,7},{5,6},{6,5},{7,4},{8,11},{9,10},{10,... | collective-permute-start | bytes 786440 | tf_op jit(solution)/shard_map/ppermute | solution.py:1239
  158.5 38.8 %collective-permute-start.25 = (bf16[8,160,512]{2,1,0:T(8,128)(2,1)}, bf16[8,160,512]{2,1,0:T(8,128)(2,1)}, u32[]{:S(2)}, u32[]{:S(2)}) collective-permute-start(bf16[8,160,512]{2,1,0:T(8,128)(2,1)} %add_convert_fusion), channel_id=1, source_target_pairs={{0,4},{4,0},{8,12},{12,8},{16,20},{20,16},{24,28},{28,24},{1,5},{5... | collective-permute-start | bytes 3932168 | tf_op jit(solution)/shard_map/ppermute | solution.py:1243
  176.7 25.4 %collective-permute-start.22 = (bf16[256,512]{1,0:T(8,128)(2,1)}, bf16[256,512]{1,0:T(8,128)(2,1)}, u32[]{:S(2)}, u32[]{:S(2)}) collective-permute-start(bf16[256,512]{1,0:T(8,128)(2,1)} %get-tuple-element.272), channel_id=1, source_target_pairs={{0,2},{1,3},{2,0},{3,1},{4,6},{5,7},{6,4},{7,5},{8,10},{9,11},{10,... | collective-permute-start | bytes 786440 | tf_op jit(solution)/shard_map/ppermute | solution.py:1239
  177.8 27.0 %collective-permute-start.23 = (bf16[256,512]{1,0:T(8,128)(2,1)}, bf16[256,512]{1,0:T(8,128)(2,1)}, u32[]{:S(2)}, u32[]{:S(2)}) collective-permute-start(bf16[256,512]{1,0:T(8,128)(2,1)} %get-tuple-element.273), channel_id=1, source_target_pairs={{0,3},{1,2},{2,1},{3,0},{4,7},{5,6},{6,5},{7,4},{8,11},{9,10},{10,... | collective-permute-start | bytes 786440 | tf_op jit(solution)/shard_map/ppermute | solution.py:1239
  195.4 26.7 %collective-permute-start.31 = (bf16[256,512]{1,0:T(8,128)(2,1)}, bf16[256,512]{1,0:T(8,128)(2,1)}, u32[]{:S(2)}, u32[]{:S(2)}) collective-permute-start(bf16[256,512]{1,0:T(8,128)(2,1)} %get-tuple-element.292), channel_id=1, source_target_pairs={{0,2},{1,3},{2,0},{3,1},{4,6},{5,7},{6,4},{7,5},{8,10},{9,11},{10,... | collective-permute-start | bytes 786440 | tf_op jit(solution)/shard_map/ppermute | solution.py:1239
  196.5 25.7 %collective-permute-start.32 = (bf16[256,512]{1,0:T(8,128)(2,1)}, bf16[256,512]{1,0:T(8,128)(2,1)}, u32[]{:S(2)}, u32[]{:S(2)}) collective-permute-start(bf16[256,512]{1,0:T(8,128)(2,1)} %get-tuple-element.293), channel_id=1, source_target_pairs={{0,3},{1,2},{2,1},{3,0},{4,7},{5,6},{6,5},{7,4},{8,11},{9,10},{10,... | collective-permute-start | bytes 786440 | tf_op jit(solution)/shard_map/ppermute | solution.py:1239
  200.6 22.6 %collective-permute-start.28 = (bf16[2,160,512]{2,1,0:T(8,128)(2,1)S(1)}, bf16[2,160,512]{2,1,0:T(8,128)(2,1)}, u32[]{:S(2)}, u32[]{:S(2)}) collective-permute-start(bf16[2,160,512]{2,1,0:T(8,128)(2,1)S(1)} %get-tuple-element.370), channel_id=1, source_target_pairs={{0,8},{4,12},{8,0},{12,4},{16,24},{20,28},{24,16},{28,20},{1,9},{5... | collective-permute-start | bytes 983048 | tf_op jit(solution)/shard_map/ppermute | solution.py:1243
  202.2 31.7 %collective-permute-start.29 = (bf16[2,160,512]{2,1,0:T(8,128)(2,1)S(1)}, bf16[2,160,512]{2,1,0:T(8,128)(2,1)}, u32[]{:S(2)}, u32[]{:S(2)}) collective-permute-start(bf16[2,160,512]{2,1,0:T(8,128)(2,1)S(1)} %get-tuple-element.372), channel_id=1, source_target_pairs={{0,16},{4,20},{8,24},{12,28},{16,0},{20,4},{24,8},{28,12},{1,17},{... | collective-permute-start | bytes 983048 | tf_op jit(solution)/shard_map/ppermute | solution.py:1243
  204.8 29.1 %collective-permute-start.30 = (bf16[2,160,512]{2,1,0:T(8,128)(2,1)S(1)}, bf16[2,160,512]{2,1,0:T(8,128)(2,1)}, u32[]{:S(2)}, u32[]{:S(2)}) collective-permute-start(bf16[2,160,512]{2,1,0:T(8,128)(2,1)S(1)} %get-tuple-element.371), channel_id=1, source_target_pairs={{0,24},{4,28},{8,16},{12,20},{16,8},{20,12},{24,0},{28,4},{1,25},{... | collective-permute-start | bytes 983048 | tf_op jit(solution)/shard_map/ppermute | solution.py:1243
  222.1 13.6 %collective-permute-start.33 = (bf16[256,512]{1,0:T(8,128)(2,1)}, bf16[256,512]{1,0:T(8,128)(2,1)}, u32[]{:S(2)}, u32[]{:S(2)}) collective-permute-start(bf16[256,512]{1,0:T(8,128)(2,1)} %get-tuple-element.295), channel_id=1, source_target_pairs={{0,1},{1,0},{2,3},{3,2},{4,5},{5,4},{6,7},{7,6},{8,9},{9,8},{10,11... | collective-permute-start | bytes 786440 | tf_op jit(solution)/shard_map/ppermute | solution.py:1239
  222.1 13.5 %collective-permute-start.34 = (bf16[256,512]{1,0:T(8,128)(2,1)}, bf16[256,512]{1,0:T(8,128)(2,1)}, u32[]{:S(2)}, u32[]{:S(2)}) collective-permute-start(bf16[256,512]{1,0:T(8,128)(2,1)} %get-tuple-element.296), channel_id=1, source_target_pairs={{0,2},{1,3},{2,0},{3,1},{4,6},{5,7},{6,4},{7,5},{8,10},{9,11},{10,... | collective-permute-start | bytes 786440 | tf_op jit(solution)/shard_map/ppermute | solution.py:1239
  223.2 13.1 %collective-permute-start.35 = (bf16[256,512]{1,0:T(8,128)(2,1)}, bf16[256,512]{1,0:T(8,128)(2,1)}, u32[]{:S(2)}, u32[]{:S(2)}) collective-permute-start(bf16[256,512]{1,0:T(8,128)(2,1)} %get-tuple-element.297), channel_id=1, source_target_pairs={{0,3},{1,2},{2,1},{3,0},{4,7},{5,6},{6,5},{7,4},{8,11},{9,10},{10,... | collective-permute-start | bytes 786440 | tf_op jit(solution)/shard_map/ppermute | solution.py:1239
  237.1 34.8 %collective-permute-start.38 = (bf16[160,512]{1,0:T(8,128)(2,1)}, bf16[160,512]{1,0:T(8,128)(2,1)}, u32[]{:S(2)}, u32[]{:S(2)}) collective-permute-start(bf16[160,512]{1,0:T(8,128)(2,1)} %fusion.1), channel_id=1, source_target_pairs={{0,2},{1,3},{2,0},{3,1},{4,6},{5,7},{6,4},{7,5},{8,10},{9,11},{10,... | collective-permute-start | bytes 491528 | tf_op jit(solution)/shard_map/ppermute | solution.py:1239
  241.4 30.6 %collective-permute-start.37 = (bf16[8,64,512]{2,1,0:T(8,128)(2,1)S(1)}, bf16[8,64,512]{2,1,0:T(8,128)(2,1)}, u32[]{:S(2)}, u32[]{:S(2)}) collective-permute-start(bf16[8,64,512]{2,1,0:T(8,128)(2,1)S(1)} %add_convert_fusion.2.refs_25_), channel_id=1, source_target_pairs={{0,2},{1,3},{2,0},{3,1},{4,6},{5,7},{6,4},{7,5},{8,10},{9,11},{10,... | collective-permute-start | bytes 1572872 | tf_op jit(solution)/shard_map/ppermute | solution.py:1239
  271.9 9.4 %collective-permute-start.39 = (bf16[16,80,512]{2,1,0:T(8,128)(2,1)}, bf16[16,80,512]{2,1,0:T(8,128)(2,1)}, u32[]{:S(2)}, u32[]{:S(2)}) collective-permute-start(bf16[16,80,512]{2,1,0:T(8,128)(2,1)} %get-tuple-element.306), channel_id=1, source_target_pairs={{0,1},{1,0},{2,3},{3,2},{4,5},{5,4},{6,7},{7,6},{8,9},{9,8},{10,11... | collective-permute-start | bytes 3932168 | tf_op jit(solution)/shard_map/ppermute | solution.py:1239
  273.4 27.5 %collective-permute-start.42 = (bf16[144,512]{1,0:T(8,128)(2,1)S(1)}, bf16[144,512]{1,0:T(8,128)(2,1)S(1)}, u32[]{:S(2)}, u32[]{:S(2)}) collective-permute-start(bf16[144,512]{1,0:T(8,128)(2,1)S(1)} %slice.342), channel_id=1, source_target_pairs={{0,8},{4,12},{8,0},{12,4},{16,24},{20,28},{24,16},{28,20},{1,9},{5... | collective-permute-start | bytes 442376 | tf_op jit(solution)/shard_map/ppermute | solution.py:1243
  274.2 26.8 %collective-permute-start.43 = (bf16[144,512]{1,0:T(8,128)(2,1)S(1)}, bf16[144,512]{1,0:T(8,128)(2,1)}, u32[]{:S(2)}, u32[]{:S(2)}) collective-permute-start(bf16[144,512]{1,0:T(8,128)(2,1)S(1)} %slice.342), channel_id=1, source_target_pairs={{0,16},{4,20},{8,24},{12,28},{16,0},{20,4},{24,8},{28,12},{1,17},{... | collective-permute-start | bytes 442376 | tf_op jit(solution)/shard_map/ppermute | solution.py:1243
  277.7 23.3 %collective-permute-start.44 = (bf16[144,512]{1,0:T(8,128)(2,1)S(1)}, bf16[144,512]{1,0:T(8,128)(2,1)}, u32[]{:S(2)}, u32[]{:S(2)}) collective-permute-start(bf16[144,512]{1,0:T(8,128)(2,1)S(1)} %slice.342), channel_id=1, source_target_pairs={{0,24},{4,28},{8,16},{12,20},{16,8},{20,12},{24,0},{28,4},{1,25},{... | collective-permute-start | bytes 442376 | tf_op jit(solution)/shard_map/ppermute | solution.py:1243
  279.8 21.2 %collective-permute-start.41 = (bf16[4,64,512]{2,1,0:T(8,128)(2,1)}, bf16[4,64,512]{2,1,0:T(8,128)(2,1)}, u32[]{:S(2)}, u32[]{:S(2)}) collective-permute-start(bf16[4,64,512]{2,1,0:T(8,128)(2,1)} %add_convert_fusion.8), channel_id=1, source_target_pairs={{0,4},{4,0},{8,12},{12,8},{16,20},{20,16},{24,28},{28,24},{1,5},{5... | collective-permute-start | bytes 786440 | tf_op jit(solution)/shard_map/ppermute | solution.py:1243
  283.5 16.2 %collective-permute-start.40 = (bf16[8,80,512]{2,1,0:T(8,128)(2,1)}, bf16[8,80,512]{2,1,0:T(8,128)(2,1)S(1)}, u32[]{:S(2)}, u32[]{:S(2)}) collective-permute-start(bf16[8,80,512]{2,1,0:T(8,128)(2,1)} %add_convert_fusion.1.refs_21_), channel_id=1, source_target_pairs={{0,2},{1,3},{2,0},{3,1},{4,6},{5,7},{6,4},{7,5},{8,10},{9,11},{10,... | collective-permute-start | bytes 1966088 | tf_op jit(solution)/shard_map/ppermute | solution.py:1239
  300.9 8.1 %collective-permute-start.45 = (bf16[4,80,512]{2,1,0:T(8,128)(2,1)S(1)}, bf16[4,80,512]{2,1,0:T(8,128)(2,1)S(1)}, u32[]{:S(2)}, u32[]{:S(2)}) collective-permute-start(bf16[4,80,512]{2,1,0:T(8,128)(2,1)S(1)} %add_convert_fusion.3), channel_id=1, source_target_pairs={{0,4},{4,0},{8,12},{12,8},{16,20},{20,16},{24,28},{28,24},{1,5},{5... | collective-permute-start | bytes 983048 | tf_op jit(solution)/shard_map/ppermute | solution.py:1243
  304.5 10.1 %collective-permute-start.49 = (bf16[64,512]{1,0:T(8,128)(2,1)S(1)}, bf16[64,512]{1,0:T(8,128)(2,1)S(1)}, u32[]{:S(2)}, u32[]{:S(2)}) collective-permute-start(bf16[64,512]{1,0:T(8,128)(2,1)S(1)} %get-tuple-element.380), channel_id=1, source_target_pairs={{0,8},{4,12},{8,0},{12,4},{16,24},{20,28},{24,16},{28,20},{1,9},{5... | collective-permute-start | bytes 196616 | tf_op jit(solution)/shard_map/ppermute | solution.py:1243
  305.1 10.8 %collective-permute-start.50 = (bf16[64,512]{1,0:T(8,128)(2,1)S(1)}, bf16[64,512]{1,0:T(8,128)(2,1)S(1)}, u32[]{:S(2)}, u32[]{:S(2)}) collective-permute-start(bf16[64,512]{1,0:T(8,128)(2,1)S(1)} %get-tuple-element.379), channel_id=1, source_target_pairs={{0,16},{4,20},{8,24},{12,28},{16,0},{20,4},{24,8},{28,12},{1,17},{... | collective-permute-start | bytes 196616 | tf_op jit(solution)/shard_map/ppermute | solution.py:1243
  308.6 9.0 %collective-permute-start.51 = (bf16[64,512]{1,0:T(8,128)(2,1)S(1)}, bf16[64,512]{1,0:T(8,128)(2,1)S(1)}, u32[]{:S(2)}, u32[]{:S(2)}) collective-permute-start(bf16[64,512]{1,0:T(8,128)(2,1)S(1)} %get-tuple-element.378), channel_id=1, source_target_pairs={{0,24},{4,28},{8,16},{12,20},{16,8},{20,12},{24,0},{28,4},{1,25},{... | collective-permute-start | bytes 196616 | tf_op jit(solution)/shard_map/ppermute | solution.py:1243
  315.9 20.7 %collective-permute-start.57 = (bf16[4,144,512]{2,1,0:T(8,128)(2,1)S(1)}, bf16[4,144,512]{2,1,0:T(8,128)(2,1)}, u32[]{:S(2)}, u32[]{:S(2)}) collective-permute-start(bf16[4,144,512]{2,1,0:T(8,128)(2,1)S(1)} %pad_maximum_fusion.refs_1_), channel_id=1, source_target_pairs={{0,4},{4,0},{8,12},{12,8},{16,20},{20,16},{24,28},{28,24},{1,5},{5... | collective-permute-start | bytes 1769480 | tf_op jit(solution)/shard_map/ppermute | solution.py:1243
  321.6 9.7 %collective-permute-start.53 = (bf16[112,512]{1,0:T(8,128)(2,1)}, bf16[112,512]{1,0:T(8,128)(2,1)S(1)}, u32[]{:S(2)}, u32[]{:S(2)}) collective-permute-start(bf16[112,512]{1,0:T(8,128)(2,1)} %get-tuple-element.382), channel_id=1, source_target_pairs={{0,16},{4,20},{8,24},{12,28},{16,0},{20,4},{24,8},{28,12},{1,17},{... | collective-permute-start | bytes 344072 | tf_op jit(solution)/shard_map/ppermute | solution.py:1243
  326.0 15.9 %collective-permute-start.55 = (bf16[112,512]{1,0:T(8,128)(2,1)}, bf16[112,512]{1,0:T(8,128)(2,1)}, u32[]{:S(2)}, u32[]{:S(2)}) collective-permute-start(bf16[112,512]{1,0:T(8,128)(2,1)} %get-tuple-element.382), channel_id=1, source_target_pairs={{0,4},{4,0},{8,12},{12,8},{16,20},{20,16},{24,28},{28,24},{1,5},{5... | collective-permute-start | bytes 344072 | tf_op jit(solution)/shard_map/ppermute | solution.py:1243
  331.4 10.6 %collective-permute-start.56 = (bf16[3,112,512]{2,1,0:T(8,128)(2,1)S(1)}, bf16[3,112,512]{2,1,0:T(8,128)(2,1)}, u32[]{:S(2)}, u32[]{:S(2)}) collective-permute-start(bf16[3,112,512]{2,1,0:T(8,128)(2,1)S(1)} %pad_maximum_fusion.1.refs_2_), channel_id=1, source_target_pairs={{0,4},{4,0},{8,12},{12,8},{16,20},{20,16},{24,28},{28,24},{1,5},{5... | collective-permute-start | bytes 1032200 | tf_op jit(solution)/shard_map/ppermute | solution.py:1243
  (27 other events, 176.0 us)
